TPU v7x, 32 devices: a whole 2x2x4 slice. The times are simulated.
32 devices in a mesh: narrow: 4 (over x, core), wide: 8 (over z, y).
Axes of the slice: x: 2, y: 2, z: 4, core: 2. Of those that a mesh axis runs over, the one named last changes fastest.
Arguments:
- inputs: bfloat16 [4, 3136, 2048], P(None, 'wide', 'narrow'), may hold values from -12 to 12
- sides: int32 [4, 64], P(None, 'wide'), may hold values from 5 to 7, as said below
- w_first: bfloat16 [2048, 512], P('wide', 'narrow'), may hold values from -0.125 to 0.125
- w_middle: bfloat16 [3, 3, 512, 512], P(None, None, 'wide', 'narrow'), may hold values from -0.09375 to 0.09375
- w_last: bfloat16 [512, 2048], P('wide', 'narrow'), may hold values from -0.25 to 0.25
- gain_first: float32 [512], P('narrow'), may hold values from 0.25 to 1.75
- shift_first: float32 [512], P('narrow'), may hold values from -1.2 to 1.2
- gain_middle: float32 [512], P('narrow'), may hold values from 0.25 to 1.75
- shift_middle: float32 [512], P('narrow'), may hold values from -1.2 to 1.2
- gain_last: float32 [2048], P('narrow'), may hold values from 0.25 to 1.75
- shift_last: float32 [2048], P('narrow'), may hold values from -1.2 to 1.2
- cotangent: bfloat16 [4, 3136, 2048], P(None, 'wide', 'narrow'), may hold values from -6 to 6
Outputs:
- block_out: bfloat16 [4, 3136, 2048], P(None, 'wide', 'narrow')
- input_grad: float32 [4, 3136, 2048], P(None, 'wide', 'narrow')
- grad_first: float32 [2048, 512], P('wide', 'narrow')
- grad_middle: float32 [3, 3, 512, 512], P(None, None, 'wide', 'narrow')
- grad_last: float32 [512, 2048], P('wide', 'narrow')
- grad_gain_first: float32 [512], P('narrow')
- grad_shift_first: float32 [512], P('narrow')
- grad_gain_middle: float32 [512], P('narrow')
- grad_shift_middle: float32 [512], P('narrow')
- grad_gain_last: float32 [2048], P('narrow')
- grad_shift_last: float32 [2048], P('narrow')
Inputs may be any that keep to these rules, and one draw needn't show every extreme that they name: `sides`: each micro-batch of each index of wide holds at least one image of side 7 and one of side 5.
All inputs are finite; a program needn't handle non-finite values.
Results may differ from a plain program's by a relative error of at most 0.022.
Values may be sent and summed in bfloat16 or wider, within the bound.
No kernel may reach another device: no remote copies, remote signals or barrier semaphores. Data moves between devices by JAX's collectives and lax.ppermute only.
A program may use at most 192 MiB of HBM per device.

v0:
```python
import jax
import jax.numpy as jnp
from jax import lax
from jax.sharding import PartitionSpec as P

C = 2048
M = 512


def silu_slope(values):
    sigma = jax.nn.sigmoid(values)
    return sigma * (1.0 + values * (1.0 - sigma))


def contract_rows(left, right):
    return lax.dot_general(
        left, right, (((0,), (0,)), ((), ())), preferred_element_type=jnp.float32
    )


def contract_cols(left, right):
    return lax.dot_general(
        left, right, (((1,), (1,)), ((), ())), preferred_element_type=jnp.float32
    )


def mask_rows(sides_row):
    places = jnp.arange(7, dtype=jnp.int32)
    limit = sides_row[:, None, None]
    inside = (places[None, :, None] < limit) & (places[None, None, :] < limit)
    return inside.astype(jnp.float32).reshape(sides_row.shape[0] * 49, 1)


def columns_of(hidden, images):
    canvas = jnp.pad(
        hidden.reshape(images, 7, 7, hidden.shape[1]), ((0, 0), (1, 1), (1, 1), (0, 0))
    )
    pieces = [
        canvas[:, row_off : row_off + 7, col_off : col_off + 7, :]
        for row_off in range(3)
        for col_off in range(3)
    ]
    return jnp.concatenate(pieces, axis=3).reshape(images * 49, 9 * hidden.shape[1])


def fold_columns(grad_cols, images, channels):
    spread_out = grad_cols.reshape(images, 7, 7, 9, channels)
    total = jnp.zeros((images, 9, 9, channels), jnp.float32)
    for row_off in range(3):
        for col_off in range(3):
            piece = spread_out[:, :, :, 3 * row_off + col_off, :]
            total = total + jnp.pad(
                piece, ((0, 0), (row_off, 2 - row_off), (col_off, 2 - col_off), (0, 0))
            )
    return total[:, 1:8, 1:8, :].reshape(images * 49, channels)


def normalize(values, mask, gain, shift):
    totals = lax.psum(
        (jnp.sum(mask * values, axis=0), jnp.sum(mask * values * values, axis=0), jnp.sum(mask)),
        "wide",
    )
    count = totals[2]
    mean = totals[0] / count
    spread = totals[1] / count - mean * mean
    scale = lax.rsqrt(spread + 1e-05)
    normed = (values - mean) * scale
    return (gain * normed + shift, normed, scale, count)


def norm_backward(grad_out, normed, scale, count, mask, gain):
    sums = lax.psum((jnp.sum(grad_out, axis=0), jnp.sum(grad_out * normed, axis=0)), "wide")
    grad_pre = gain * scale * (grad_out - mask * (sums[0] + normed * sums[1]) / count)
    return (grad_pre.astype(jnp.bfloat16), sums[1], sums[0])


def on_device(
    inputs,
    sides,
    w_first,
    w_middle,
    w_last,
    gain_first,
    shift_first,
    gain_middle,
    shift_middle,
    gain_last,
    shift_last,
    cotangent,
):
    micro_count = inputs.shape[0]
    images = sides.shape[1]
    acc_first = jnp.zeros((C, w_first.shape[1]), jnp.float32)
    acc_middle = jnp.zeros((9 * M, w_middle.shape[3]), jnp.float32)
    acc_last = jnp.zeros((M, w_last.shape[1]), jnp.float32)
    acc_gain_one = jnp.zeros_like(gain_first)
    acc_shift_one = jnp.zeros_like(shift_first)
    acc_gain_two = jnp.zeros_like(gain_middle)
    acc_shift_two = jnp.zeros_like(shift_middle)
    acc_gain_three = jnp.zeros_like(gain_last)
    acc_shift_three = jnp.zeros_like(shift_last)
    block_rows = []
    input_rows = []
    for micro_index in range(micro_count):
        weights = (
            lax.all_gather(w_first, "wide", axis=0, tiled=True),
            lax.all_gather(w_middle, "wide", axis=2, tiled=True),
            lax.all_gather(w_last, "wide", axis=0, tiled=True),
        )
        first_full, middle_full, last_full = weights
        middle_flat = middle_full.reshape(9 * M, middle_full.shape[3])
        rows_low = inputs[micro_index]
        mask = mask_rows(sides[micro_index])
        input_full = lax.all_gather(rows_low, "narrow", axis=1, tiled=True)
        pre_first = jnp.dot(input_full, first_full, preferred_element_type=jnp.float32)
        act_first, normed_one, scale_one, count = normalize(
            pre_first, mask, gain_first, shift_first
        )
        hidden_one = (mask * jax.nn.silu(act_first)).astype(jnp.bfloat16)
        hidden_one_full = lax.all_gather(hidden_one, "narrow", axis=1, tiled=True)
        columns = columns_of(hidden_one_full, images)
        pre_middle = jnp.dot(columns, middle_flat, preferred_element_type=jnp.float32)
        act_middle, normed_two, scale_two, count_two = normalize(
            pre_middle, mask, gain_middle, shift_middle
        )
        hidden_two = (mask * jax.nn.silu(act_middle)).astype(jnp.bfloat16)
        hidden_two_full = lax.all_gather(hidden_two, "narrow", axis=1, tiled=True)
        pre_last = jnp.dot(hidden_two_full, last_full, preferred_element_type=jnp.float32)
        act_last, normed_three, scale_three, count_three = normalize(
            pre_last, mask, gain_last, shift_last
        )
        summed = act_last + rows_low.astype(jnp.float32)
        block_rows.append((mask * jax.nn.silu(summed)).astype(jnp.bfloat16))
        grad_sum = mask * cotangent[micro_index].astype(jnp.float32) * silu_slope(summed)
        grad_pre_last, part_gain, part_shift = norm_backward(
            grad_sum, normed_three, scale_three, count_three, mask, gain_last
        )
        acc_gain_three = acc_gain_three + part_gain
        acc_shift_three = acc_shift_three + part_shift
        acc_last = acc_last + contract_rows(hidden_two_full, grad_pre_last)
        grad_hidden_two = lax.psum_scatter(
            contract_cols(grad_pre_last, last_full).astype(jnp.bfloat16),
            "narrow",
            scatter_dimension=1,
            tiled=True,
        ).astype(jnp.float32)
        grad_act_middle = grad_hidden_two * mask * silu_slope(act_middle)
        grad_pre_middle, part_gain, part_shift = norm_backward(
            grad_act_middle, normed_two, scale_two, count_two, mask, gain_middle
        )
        acc_gain_two = acc_gain_two + part_gain
        acc_shift_two = acc_shift_two + part_shift
        acc_middle = acc_middle + contract_rows(columns, grad_pre_middle)
        grad_columns = contract_cols(grad_pre_middle, middle_flat)
        folded = fold_columns(grad_columns, images, M)
        grad_hidden_one = lax.psum_scatter(
            folded.astype(jnp.bfloat16), "narrow", scatter_dimension=1, tiled=True
        ).astype(jnp.float32)
        grad_act_first = grad_hidden_one * mask * silu_slope(act_first)
        grad_pre_first, part_gain, part_shift = norm_backward(
            grad_act_first, normed_one, scale_one, count, mask, gain_first
        )
        acc_gain_one = acc_gain_one + part_gain
        acc_shift_one = acc_shift_one + part_shift
        acc_first = acc_first + contract_rows(input_full, grad_pre_first)
        grad_input = lax.psum_scatter(
            contract_cols(grad_pre_first, first_full).astype(jnp.bfloat16),
            "narrow",
            scatter_dimension=1,
            tiled=True,
        ).astype(jnp.float32)
        input_rows.append(grad_input + grad_sum)
    grad_first, grad_middle, grad_last = (
        lax.psum_scatter(acc_first, "wide", scatter_dimension=0, tiled=True),
        lax.psum_scatter(
            acc_middle.reshape(3, 3, M, acc_middle.shape[1]),
            "wide",
            scatter_dimension=2,
            tiled=True,
        ),
        lax.psum_scatter(acc_last, "wide", scatter_dimension=0, tiled=True),
    )
    return (
        jnp.stack(block_rows),
        jnp.stack(input_rows),
        grad_first,
        grad_middle,
        grad_last,
        acc_gain_one,
        acc_shift_one,
        acc_gain_two,
        acc_shift_two,
        acc_gain_three,
        acc_shift_three,
    )


def solution(mesh):
    placed = (
        P(None, "wide", "narrow"),
        P(None, "wide"),
        P("wide", "narrow"),
        P(None, None, "wide", "narrow"),
        P("wide", "narrow"),
        P("narrow"),
        P("narrow"),
        P("narrow"),
        P("narrow"),
        P("narrow"),
        P("narrow"),
        P(None, "wide", "narrow"),
    )
    return jax.shard_map(
        on_device,
        mesh=mesh,
        in_specs=placed,
        out_specs=(
            P(None, "wide", "narrow"),
            P(None, "wide", "narrow"),
            P("wide", "narrow"),
            P(None, None, "wide", "narrow"),
            P("wide", "narrow"),
            P("narrow"),
            P("narrow"),
            P("narrow"),
            P("narrow"),
            P("narrow"),
            P("narrow"),
        ),
        check_vma=False,
    )
```

profile of v0, /device:TPU:0, one launch (start us, length us, event | category | flops | bytes accessed | tf_op | source)
XLA Modules:
  0.0 997.1 jit_solution(4573044085030399514)
XLA Ops:
  16.3 33.2 %all_gather.55 = bf16[2048,128]{1,0:T(8,128)(2,1)S(1)} all-gather(bf16[256,128]{1,0:T(8,128)(2,1)S(1)} %copy-done.83), channel_id=1, replica_groups=mesh['narrow'=4,'wide'=8] {'wide'}, dimensions={0}, use_global_device_ids=true | all-gather | bytes 589824 | tf_op jit(solution)/shard_map/all_gather | solution.py:106
  49.5 31.3 %all_gather.59 = bf16[512,512]{1,0:T(8,128)(2,1)S(1)} all-gather(bf16[64,512]{1,0:T(8,128)(2,1)S(1)} %copy-done.84), channel_id=1, replica_groups=mesh['narrow'=4,'wide'=8] {'wide'}, dimensions={0}, use_global_device_ids=true | all-gather | bytes 589824 | tf_op jit(solution)/shard_map/all_gather | solution.py:108
  87.4 10.5 %all-gather.12.cloned.1.call-done = bf16[1,392,2048]{2,1,0:T(8,128)(2,1)} async-done(((bf16[1,392,512]{2,1,0:T(8,128)(2,1)}), bf16[1,392,2048]{2,1,0:T(8,128)(2,1)}) %all-gather.12.cloned.1.call-update) | async-done | bytes 1605648 | tf_op jit(solution)/shard_map/all_gather | solution.py:114
  99.9 22.3 %all-reduce.45 = (f32[128]{0:T(128)S(1)}, f32[]{:T(128)}, f32[128]{0:T(128)S(1)}, f32[128]{0:T(128)S(1)}, f32[]{:T(128)}, /*index=5*/f32[128]{0:T(128)S(1)}, f32...) all-reduce(f32[128]{0:T(128)S(1)} %get-tuple-element.75, ...), channel_id=1, replica_groups=mesh['narrow'=4,'wide'=8] {'wide'}, use_global_device_ids=true, to_apply=%region_43.44 | all-reduce | flops 1028 | bytes 8224 | tf_op jit(solution)/shard_map/psum | solution.py:59
  138.6 6.6 all_gather.64
  145.3 6.8 all_gather.67
  268.0 17.1 %all-reduce.44 = (f32[128]{0:T(128)S(1)}, f32[128]{0:T(128)S(1)}, f32[128]{0:T(128)S(1)}, f32[128]{0:T(128)S(1)}, f32[128]{0:T(128)S(1)}, /*index=5*/f32[128]{0:T(128)S(1)}, f32[128]{0:T(128)S(1)}, f32[128]{0:T(128)S(1)}) all-reduce(f32[128]{0:T(128)S(1)} %get-tuple-element.73, ...), channel_id=1, replica_groups=mesh['narrow'=4,'wide'=8] {'wide'}, use_global_device_ids=true, to_apply=%region_49.50 | all-reduce | flops 1024 | bytes 8192 | tf_op jit(solution)/shard_map/psum | solution.py:59
  320.1 34.8 %all-reduce.43 = (f32[512]{0:T(512)S(1)}, f32[512]{0:T(512)S(1)}, f32[512]{0:T(512)S(1)}, f32[512]{0:T(512)S(1)}, f32[512]{0:T(512)S(1)}, /*index=5*/f32[512]{0:T(512)S(1)}, f32[512]{0:T(512)S(1)}, f32[512]{0:T(512)S(1)}) all-reduce(f32[512]{0:T(512)S(1)} %get-tuple-element.51, ...), channel_id=1, replica_groups=mesh['narrow'=4,'wide'=8] {'wide'}, use_global_device_ids=true, to_apply=%region_55.56 | all-reduce | flops 4096 | bytes 32768 | tf_op jit(solution)/shard_map/psum | solution.py:59
  364.7 33.1 %all-reduce.42 = (f32[512]{0:T(512)S(1)}, f32[512]{0:T(512)S(1)}, f32[512]{0:T(512)S(1)}, f32[512]{0:T(512)S(1)}, f32[512]{0:T(512)S(1)}, /*index=5*/f32[512]{0:T(512)S(1)}, f32[512]{0:T(512)S(1)}, f32[512]{0:T(512)S(1)}) all-reduce(f32[512]{0:T(512)S(1)} %get-tuple-element.227, ...), channel_id=1, replica_groups=mesh['narrow'=4,'wide'=8] {'wide'}, use_global_device_ids=true, to_apply=%region_104.105 | all-reduce | flops 4096 | bytes 32768 | tf_op jit(solution)/shard_map/psum | solution.py:72
  421.8 23.3 %reduce-scatter.54.cloned.1.call-done = bf16[128,392]{1,0:T(8,128)(2,1)} async-done(((bf16[512,392]{1,0:T(8,128)(2,1)}), bf16[128,392]{1,0:T(8,128)(2,1)}) %reduce-scatter.54.cloned.1.call-update) | async-done | bytes 100368
  446.1 23.8 %reduce-scatter.46.cloned.1.call-done = bf16[128,392]{1,0:T(8,128)(2,1)} async-done(((bf16[512,392]{1,0:T(8,128)(2,1)}), bf16[128,392]{1,0:T(8,128)(2,1)}) %reduce-scatter.46.cloned.1.call-update) | async-done | bytes 100368
  473.9 20.4 %reduce-scatter.50.cloned.1.call-done = bf16[128,392]{1,0:T(8,128)(2,1)} async-done(((bf16[512,392]{1,0:T(8,128)(2,1)}), bf16[128,392]{1,0:T(8,128)(2,1)}) %reduce-scatter.50.cloned.1.call-update) | async-done | bytes 100368
  498.1 22.5 %all-reduce.41 = (f32[128]{0:T(128)S(1)}, f32[128]{0:T(128)S(1)}, f32[128]{0:T(128)}, f32[128]{0:T(128)}, f32[128]{0:T(128)}, /*index=5*/f32[128]{0:T(128)}, f32[128]{0:T(128)}, f32[128]{0:T(128)}) all-reduce(f32[128]{0:T(128)} %get-tuple-element.91, f32[128]{0:T(128)} %get-tuple-element.90, ...), channel_id=1, replica_groups=mesh['narrow'=4,'wide'=8] {'wide'}, use_global_device_ids=true, to_apply=%region_109.110 | all-reduce | flops 1024 | bytes 8192 | tf_op jit(solution)/shard_map/psum | solution.py:72
  568.9 11.0 %reduce-scatter.52.cloned.1.call-done = bf16[128,392]{1,0:T(8,128)(2,1)} async-done(((bf16[512,392]{1,0:T(8,128)(2,1)}), bf16[128,392]{1,0:T(8,128)(2,1)}) %reduce-scatter.52.cloned.1.call-update) | async-done | bytes 100368
  580.9 23.6 %reduce-scatter.56.cloned.1.call-done = bf16[128,392]{1,0:T(8,128)(2,1)} async-done(((bf16[512,392]{1,0:T(8,128)(2,1)}), bf16[128,392]{1,0:T(8,128)(2,1)}) %reduce-scatter.56.cloned.1.call-update) | async-done | bytes 100368
  606.1 23.2 %reduce-scatter.60.cloned.1.call-done = bf16[128,392]{1,0:T(8,128)(2,1)} async-done(((bf16[512,392]{1,0:T(8,128)(2,1)}), bf16[128,392]{1,0:T(8,128)(2,1)}) %reduce-scatter.60.cloned.1.call-update) | async-done | bytes 100368
  633.1 22.1 %all-reduce.40 = (f32[128]{0:T(128)S(1)}, f32[128]{0:T(128)S(1)}, f32[128]{0:T(128)S(1)}, f32[128]{0:T(128)}, f32[128]{0:T(128)S(1)}, /*index=5*/f32[128]{0:T(128)}, f32[128]{0:T(128)S(1)}, f32[128]{0:T(128)S(1)}) all-reduce(f32[128]{0:T(128)} %get-tuple-element.89, ...), channel_id=1, replica_groups=mesh['narrow'=4,'wide'=8] {'wide'}, use_global_device_ids=true, to_apply=%region_114.115 | all-reduce | flops 1024 | bytes 8192 | tf_op jit(solution)/shard_map/psum | solution.py:72
  696.2 30.2 %reduce-scatter.40.cloned.1.call-done = f32[256,128]{0,1:T(8,128)} async-done(((f32[2048,128]{0,1:T(8,128)}), f32[256,128]{0,1:T(8,128)}) %reduce-scatter.40.cloned.1.call-update) | async-done | bytes 131088 | tf_op jit(solution)/shard_map/reduce_scatter | solution.py:174
  728.0 28.9 %reduce-scatter.38.cloned.1.call-done = bf16[392,512]{1,0:T(8,128)(2,1)} async-done(((bf16[392,2048]{1,0:T(8,128)(2,1)}), bf16[392,512]{1,0:T(8,128)(2,1)}) %reduce-scatter.38.cloned.1.call-update) | async-done | bytes 401424 | tf_op jit(solution)/shard_map/reduce_scatter | solution.py:166
  759.2 28.6 %reduce-scatter.36.cloned.1.call-done = bf16[392,512]{1,0:T(8,128)(2,1)} async-done(((bf16[392,2048]{1,0:T(8,128)(2,1)}), bf16[392,512]{1,0:T(8,128)(2,1)}) %reduce-scatter.36.cloned.1.call-update) | async-done | bytes 401424 | tf_op jit(solution)/shard_map/reduce_scatter | solution.py:166
  789.8 28.9 %reduce-scatter.34.cloned.1.call-done = bf16[392,512]{1,0:T(8,128)(2,1)} async-done(((bf16[392,2048]{1,0:T(8,128)(2,1)}), bf16[392,512]{1,0:T(8,128)(2,1)}) %reduce-scatter.34.cloned.1.call-update) | async-done | bytes 401424 | tf_op jit(solution)/shard_map/reduce_scatter | solution.py:166
  820.8 28.8 %reduce-scatter.32.cloned.1.call-done = bf16[392,512]{1,0:T(8,128)(2,1)} async-done(((bf16[392,2048]{1,0:T(8,128)(2,1)}), bf16[392,512]{1,0:T(8,128)(2,1)}) %reduce-scatter.32.cloned.1.call-update) | async-done | bytes 401424 | tf_op jit(solution)/shard_map/reduce_scatter | solution.py:166
  852.9 64.6 %reduce-scatter.44.cloned.1.call-done = f32[64,512]{1,0:T(8,128)} async-done(((f32[512,512]{1,0:T(8,128)}), f32[64,512]{1,0:T(8,128)}) %reduce-scatter.44.cloned.1.call-update) | async-done | bytes 131088 | tf_op jit(solution)/shard_map/reduce_scatter | solution.py:181
  917.4 72.5 %reduce-scatter.42.cloned.1.call-done = f32[3,3,64,128]{3,2,1,0:T(8,128)} async-done(((f32[3,3,512,128]{3,2,1,0:T(8,128)}), f32[3,3,64,128]{3,2,1,0:T(8,128)}) %reduce-scatter.42.cloned.1.call-update) | async-done | bytes 294928 | tf_op jit(solution)/shard_map/reduce_scatter | solution.py:175
  (586 shorter events, 332.2 us)
Async XLA Ops:
  7.2 73.5 %all-gather.16.cloned.1.call-start = ((), (), s32[]{:S(2)}) async-start(), calls=%async_computation.25 | async-start | bytes 2007040 | tf_op jit(solution)/shard_map/all_gather | solution.py:114
  9.8 73.0 %all-gather.18.cloned.1.call-start = ((), (), s32[]{:S(2)}) async-start(), calls=%async_computation.26 | async-start | bytes 2007040 | tf_op jit(solution)/shard_map/all_gather | solution.py:114
  10.6 74.4 %all-gather.14.cloned.1.call-start = ((), (), s32[]{:S(2)}) async-start(), calls=%async_computation.24 | async-start | bytes 2007040 | tf_op jit(solution)/shard_map/all_gather | solution.py:114
  11.3 86.5 %all-gather.12.cloned.1.call-start = ((), (), s32[]{:S(2)}) async-start(), calls=%async_computation.23 | async-start | bytes 2007040 | tf_op jit(solution)/shard_map/all_gather | solution.py:114
  11.9 198.8 %all-gather.10.cloned.1.call-start = ((), (), s32[]{:S(2)}) async-start(), calls=%async_computation.15 | async-start | bytes 1327104 | tf_op jit(solution)/shard_map/all_gather | solution.py:107
  12.5 408.3 %reduce-scatter.58.cloned.1.call-start = ((), (), s32[]{:S(2)}) async-start(), calls=%async_computation.33 | async-start | bytes 655360
  402.3 42.8 %reduce-scatter.54.cloned.1.call-start = ((), (), s32[]{:S(2)}) async-start(), calls=%async_computation.31 | async-start | bytes 655360
  406.9 63.0 %reduce-scatter.46.cloned.1.call-start = ((), (), s32[]{:S(2)}) async-start(), calls=%async_computation.27 | async-start | bytes 655360
  412.2 82.1 %reduce-scatter.50.cloned.1.call-start = ((), (), s32[]{:S(2)}) async-start(), calls=%async_computation.29 | async-start | bytes 655360
  418.6 149.3 %reduce-scatter.48.cloned.1.call-start = ((), (), s32[]{:S(2)}) async-start(), calls=%async_computation.28 | async-start | bytes 655360
  537.4 42.5 %reduce-scatter.52.cloned.1.call-start = ((), (), s32[]{:S(2)}) async-start(), calls=%async_computation.30 | async-start | bytes 655360
  549.4 55.1 %reduce-scatter.56.cloned.1.call-start = ((), (), s32[]{:S(2)}) async-start(), calls=%async_computation.32 | async-start | bytes 655360
  561.2 68.2 %reduce-scatter.60.cloned.1.call-start = ((), (), s32[]{:S(2)}) async-start(), calls=%async_computation.34 | async-start | bytes 655360
  567.7 91.0 %copy-start.138 = (f32[128]{0:T(128)S(1)}, f32[128]{0:T(128)}, u32[]{:S(2)}) copy-start(f32[128]{0:T(128)} %get-tuple-element.319) | copy-start | bytes 1540
  567.8 92.5 %copy-start.137 = (f32[128]{0:T(128)S(1)}, f32[128]{0:T(128)}, u32[]{:S(2)}) copy-start(f32[128]{0:T(128)} %get-tuple-element.316) | copy-start | bytes 1540
  567.8 158.6 %reduce-scatter.40.cloned.1.call-start = ((), (), s32[]{:S(2)}) async-start(), calls=%async_computation.20 | async-start | bytes 1179648 | tf_op jit(solution)/shard_map/reduce_scatter | solution.py:174
  665.9 91.0 %reduce-scatter.38.cloned.1.call-start = ((), (), s32[]{:S(2)}) async-start(), calls=%async_computation.19 | async-start | bytes 2007040 | tf_op jit(solution)/shard_map/reduce_scatter | solution.py:166
  667.8 120.0 %reduce-scatter.36.cloned.1.call-start = ((), (), s32[]{:S(2)}) async-start(), calls=%async_computation.18 | async-start | bytes 2007040 | tf_op jit(solution)/shard_map/reduce_scatter | solution.py:166
  669.6 149.1 %reduce-scatter.34.cloned.1.call-start = ((), (), s32[]{:S(2)}) async-start(), calls=%async_computation.17 | async-start | bytes 2007040 | tf_op jit(solution)/shard_map/reduce_scatter | solution.py:166
  671.5 178.1 %reduce-scatter.32.cloned.1.call-start = ((), (), s32[]{:S(2)}) async-start(), calls=%async_computation.16 | async-start | bytes 2007040 | tf_op jit(solution)/shard_map/reduce_scatter | solution.py:166
  673.4 244.1 %reduce-scatter.44.cloned.1.call-start = ((), (), s32[]{:S(2)}) async-start(), calls=%async_computation.22 | async-start | bytes 1179648 | tf_op jit(solution)/shard_map/reduce_scatter | solution.py:181
  677.7 312.3 %reduce-scatter.42.cloned.1.call-start = ((), (), s32[]{:S(2)}) async-start(), calls=%async_computation.21 | async-start | bytes 2654208 | tf_op jit(solution)/shard_map/reduce_scatter | solution.py:175
  691.5 96.3 %copy-start.6 = (f32[392,512]{1,0:T(8,128)S(1)}, f32[392,512]{1,0:T(8,128)}, u32[]{:S(2)}) copy-start(f32[392,512]{1,0:T(8,128)} %get-tuple-element.186) | copy-start | bytes 2408452
  692.8 125.9 %copy-start.5 = (f32[392,512]{1,0:T(8,128)S(1)}, f32[392,512]{1,0:T(8,128)}, u32[]{:S(2)}) copy-start(f32[392,512]{1,0:T(8,128)} %get-tuple-element.226) | copy-start | bytes 2408452
  (161 other events, 3186.3 us)
Sparse Core Ops, SparseCore 0:
  9.9 22.5 all-gather.15
  34.1 19.8 all-gather.17
  56.1 19.8 all-gather.13
  78.0 19.8 all-gather.11
  99.9 41.1 all-gather.9
  402.4 18.3 reduce-scatter.57
  423.4 21.6 reduce-scatter.53
  448.2 21.6 reduce-scatter.45
  472.5 21.6 reduce-scatter.49
  537.5 17.9 reduce-scatter.47
  558.2 21.6 reduce-scatter.51
  582.8 21.6 reduce-scatter.55
  607.7 21.6 reduce-scatter.59
  666.1 60.2 reduce-scatter.39
  729.5 27.4 reduce-scatter.37
  759.3 28.4 reduce-scatter.35
  790.3 28.3 reduce-scatter.33
  821.2 28.4 reduce-scatter.31
  854.0 63.4 reduce-scatter.43
  921.4 68.5 reduce-scatter.41
where the time goes:
time: 1000 us; the launch traced here: 997 us
  waiting for transfers between devices  423 us (42%)
  blocking collectives  269 us (27%)
  local copies, waits for them, and re-layouts  155 us (16%)
  other arithmetic  69.3 us (7%)
  matrix products  63 us (6%)
  between operations  16.7 us (2%)
    unnamed x28, waiting for transfers between devices  130 us
    reduce_scatter x4, waiting for transfers between devices, on_device(): lax.psum_scatter(contract_cols(grad_pre_first, first_full).astype(jnp.bfl...  115 us
    psum x3, blocking collectives, norm_backward(): lax.psum((jnp.sum(grad_out, axis=0), jnp.sum(grad_out * normed, axis=0)),...  77.6 us
    psum x3, blocking collectives, normalize(): lax.psum((jnp.sum(mask * values, axis=0), jnp.sum(mask * values * values,...  74.2 us
    reduce_scatter x1, waiting for transfers between devices, on_device(): lax.psum_scatter(acc_middle.reshape(3, 3, M, acc_middle.shape[1]), 'wide'...  72.5 us
    reduce_scatter x1, waiting for transfers between devices, on_device(): lax.psum_scatter(acc_last, 'wide', scatter_dimension=0, tiled=True)  64.6 us
    concatenate x36, local copies, waits for them, and re-layouts, columns_of(): jnp.concatenate(pieces, axis=3).reshape(images * 49, 9 * hidden.shape[1])  62.1 us
    unnamed x379, local copies, waits for them, and re-layouts  57.7 us
  transfers between devices with their start and end apart: 20, of which 15 were waited for; matrix products, arithmetic and copies ran while one was open for 17% of the time, Pallas kernels for 0%

commit v1 on v0

v1 whole, which is shorter than its diff:
```python
import jax
import jax.numpy as jnp
from jax import lax
from jax.experimental import pallas as pl
from jax.experimental.pallas import tpu as pltpu
from jax.sharding import PartitionSpec as P


F32 = jnp.float32
BF = jnp.bfloat16
EPS = 1e-05
SIDE = 7
PITCH = 8
TAPS = 9
NARROW = 4
BOTH = ("wide", "narrow")
MESH = ("narrow", "wide")
VMEM_BYTES = 40 * 2**20


def dot(left, right):
    return jnp.dot(left, right, preferred_element_type=F32)


def dot_nt(left, right):
    return lax.dot_general(left, right, (((1,), (1,)), ((), ())), preferred_element_type=F32)


def dot_tn(left, right):
    return lax.dot_general(left, right, (((0,), (0,)), ((), ())), preferred_element_type=F32)


def run(kernel, scalars, operands, outs, scratch=(), flops=0):
    moved = sum(o.size * o.dtype.itemsize for o in (*operands, *outs))
    return pl.pallas_call(
        kernel,
        out_shape=outs,
        in_specs=[pl.BlockSpec(memory_space=pltpu.SMEM)] * len(scalars)
        + [pl.BlockSpec(memory_space=pltpu.VMEM)] * len(operands),
        out_specs=[pl.BlockSpec(memory_space=pltpu.VMEM)] * len(outs),
        scratch_shapes=list(scratch),
        cost_estimate=pl.CostEstimate(flops=flops, bytes_accessed=moved, transcendentals=0),
        compiler_params=pltpu.CompilerParams(vmem_limit_bytes=VMEM_BYTES),
    )(*scalars, *operands)


def arr(shape, dtype):
    return jax.ShapeDtypeStruct(shape, dtype)


def by_rows(rows, body, carry, size=16):
    full = rows // size
    carry = lax.fori_loop(
        0, full, lambda i, c: body(pl.ds(pl.multiple_of(i * size, size), size), c), carry
    )
    if rows % size:
        carry = body(pl.ds(full * size, rows % size), carry)
    return carry


def fold(values):
    total = values[0:8]
    for start in range(8, values.shape[0], 8):
        total = total + values[start : start + 8]
    return total


def zeros_acc(channels):
    return (jnp.zeros((8, channels), F32), jnp.zeros((8, channels), F32))


def column_sum(acc):
    return jnp.sum(acc, axis=0, keepdims=True)


def sigmoid(values):
    return 0.5 * jnp.tanh(0.5 * values) + 0.5


def coefficients(total, squares, inverse, gain, shift):
    mean = total * inverse
    spread = squares * inverse - mean * mean
    scale = lax.rsqrt(spread + EPS)
    slope = gain * scale
    return mean, scale, slope, shift - mean * slope


def total_of(parts, index, wide):
    acc = parts[index]
    for place in range(1, wide):
        acc = acc + parts[place * NARROW + index]
    return acc


def total_wide(parts):
    acc = parts[0]
    for place in range(1, parts.shape[0]):
        acc = acc + parts[place]
    return acc


def wide_row(block, first, count=NARROW):
    return jnp.concatenate([block[first + k : first + k + 1] for k in range(count)], axis=1)


def row_of(block, first, index):
    rows = [jnp.where(index == k, block[first + k : first + k + 1], 0.0) for k in range(NARROW)]
    return rows[0] + rows[1] + rows[2] + rows[3]


def lane_block(index):
    return pl.ds(pl.multiple_of(index * 128, 128), 128)


def send_stats(message, first, second):
    for k in range(NARROW):
        message[0, k : k + 1, :] = first[:, 128 * k : 128 * k + 128]
        message[0, NARROW + k : NARROW + k + 1, :] = second[:, 128 * k : 128 * k + 128]
    repeat_first(message)


def repeat_first(message):
    block = message[0]
    for place in range(1, message.shape[0]):
        message[place] = block


def first_product(idx, x, *refs):
    pieces, (w_first, send_far, own_far, send_near, own_near) = refs[:-5], refs[-5:]
    n, z, y = idx[0], idx[1], idx[2]
    if len(pieces) == 1:
        w_first[...] = pieces[0][...]
    else:
        rows, cols = pieces[0].shape
        for place, piece in enumerate(pieces):
            half = y ^ (place // NARROW)
            block = (z - place % NARROW) & 3
            w_first[pl.ds(pl.multiple_of(half * rows, rows), rows), lane_block(block)] = piece[...]
    for ref, m in ((send_far, 3), (own_far, 2), (send_near, 1), (own_near, 0)):
        ref[...] = dot(x[n ^ m], w_first[...]).astype(ref.dtype)


def first_join(idx, own, near, far, mask, pre, message):
    b = idx[0]

    def body(ds, acc):
        values = own[ds, :] + near[ds, :].astype(F32) + far[ds, :].astype(F32)
        pre[ds, :] = values.astype(BF)
        kept = mask[b, ds, :] * values
        return acc[0] + fold(kept), acc[1] + fold(kept * values)

    sums = by_rows(own.shape[0], body, zeros_acc(own.shape[1]))
    send_stats(message, column_sum(sums[0]), column_sum(sums[1]))


def middle_forward(idx, inverse, pre0, pre1, pre2, pre3, parts, params, mask, to_canvas, to_rows, weight,
                   hidden, pre, coef, message, active, spread, joined):
    n = idx[0]
    wide = parts.shape[0] // NARROW
    rows, places = pre0.shape[0], to_canvas.shape[0]
    img = places // (SIDE * PITCH)
    margin = img * (PITCH + 1)
    gain = jnp.concatenate([params[k, 0:1, :] for k in range(NARROW)], axis=1)
    shift = jnp.concatenate([params[k, 1:2, :] for k in range(NARROW)], axis=1)
    spread[0:margin, :] = jnp.zeros((margin, spread.shape[1]), F32)
    spread[margin + places :, :] = jnp.zeros((margin, spread.shape[1]), F32)
    line = img * PITCH
    for m, source in enumerate((pre0, pre1, pre2, pre3)):
        b = n ^ m
        block = total_of(parts, b, wide)
        mean, scale, slope, offset = coefficients(
            wide_row(block, 0), wide_row(block, NARROW), inverse[b], gain, shift
        )
        for k, row in enumerate((mean, scale, slope, offset)):
            coef[m, k : k + 1, :] = row

        def activate(ds, carry):
            act = source[ds, :].astype(F32) * slope + offset
            active[ds, :] = (mask[b, ds, :] * act * sigmoid(act)).astype(BF)
            return carry

        by_rows(rows, activate, 0)
        hidden[m] = dot(to_canvas[...], active[...]).astype(BF)
        spread[margin : margin + places, :] = dot(hidden[m], weight[...])
        for top in range(SIDE):
            acc = None
            for tap in range(TAPS):
                start = margin + top * line + ((tap // 3 - 1) * PITCH + tap % 3 - 1) * img
                part = spread[start : start + line, 128 * tap : 128 * tap + 128]
                acc = part if acc is None else acc + part
            joined[top * line : (top + 1) * line, :] = acc.astype(BF)
        pre[m] = dot(to_rows[...], joined[...]).astype(BF)

        def collect(ds, acc):
            values = pre[m, ds, :].astype(F32)
            kept = mask[b, ds, :] * values
            return acc[0] + fold(kept), acc[1] + fold(kept * values)

        sums = by_rows(rows, collect, zeros_acc(128))
        message[0, 2 * m : 2 * m + 1, :] = column_sum(sums[0])
        message[0, 2 * m + 1 : 2 * m + 2, :] = column_sum(sums[1])
    repeat_first(message)


def last_forward(idx, inverse, src0, src1, src2, src3, parts, params, mask, weight,
                 hidden, own, coef, pre, message):
    n = idx[0]
    wide = parts.shape[0] // NARROW
    rows = own.shape[0]
    sources = (src0, src1, src2, src3)
    blocks = [total_of(parts, n ^ i, wide) for i in range(NARROW)]
    for m in range(NARROW):
        b = n ^ m
        for i in range(NARROW):
            j = m ^ i
            here = lane_block(n ^ i)
            mean, scale, slope, offset = coefficients(
                blocks[i][2 * j : 2 * j + 1], blocks[i][2 * j + 1 : 2 * j + 2], inverse[b],
                params[n ^ i, 2:3, :], params[n ^ i, 3:4, :],
            )
            if m == 0:
                own[:, here] = sources[i][j]
                for k, row in enumerate((mean, scale, slope, offset)):
                    coef[k : k + 1, here] = row

            def activate(ds, carry):
                act = sources[i][j, ds, :].astype(F32) * slope + offset
                hidden[m, ds, here] = (mask[b, ds, :] * act * sigmoid(act)).astype(BF)
                return carry

            by_rows(rows, activate, 0, 32)
        pre[m] = dot(hidden[m], weight[...])

        def collect(ds, acc):
            values = pre[m, ds, :]
            kept = mask[b, ds, :] * values
            return acc[0] + fold(kept), acc[1] + fold(kept * values)

        sums = by_rows(rows, collect, zeros_acc(pre.shape[2]))
        message[0, 2 * m : 2 * m + 1, :] = column_sum(sums[0])
        message[0, 2 * m + 1 : 2 * m + 2, :] = column_sum(sums[1])
    repeat_first(message)


def block_output(idx, inverse, pre, x, cotangent, parts, gain, shift, mask, out, grad, coef, message):
    n = idx[0]
    rows, channels = pre.shape[1:]
    block = total_wide(parts)
    for m in range(NARROW):
        b = n ^ m
        mean, scale, slope, offset = coefficients(
            block[2 * m : 2 * m + 1], block[2 * m + 1 : 2 * m + 2], inverse[b], gain[...], shift[...]
        )
        for k, row in enumerate((mean, scale, slope, offset)):
            coef[m, k : k + 1, :] = row
        back = mean * scale

        def body(ds, acc):
            values = pre[m, ds, :]
            inside = mask[b, ds, :]
            summed = values * slope + offset + x[b, ds, :].astype(F32)
            gate = sigmoid(summed)
            value = summed * gate
            out[b, ds, :] = (inside * value).astype(BF)
            local = inside * cotangent[b, ds, :].astype(F32) * (gate + value * (1.0 - gate))
            grad[m, ds, :] = local
            return acc[0] + fold(local), acc[1] + fold(local * (values * scale - back))

        sums = by_rows(rows, body, zeros_acc(channels))
        message[0, 2 * m : 2 * m + 1, :] = column_sum(sums[0])
        message[0, 2 * m + 1 : 2 * m + 2, :] = column_sum(sums[1])
    repeat_first(message)


def last_backward(idx, inverse, pre, grad, parts, coef, mask, weight,
                  grad_pre, send_far, own_far, send_near, own_near, sums):
    n = idx[0]
    rows = pre.shape[1]
    block = total_wide(parts)
    for s in range(2):
        acc = block[s : s + 1]
        for m in range(1, NARROW):
            acc = acc + block[2 * m + s : 2 * m + s + 1]
        sums[s : s + 1, :] = acc
    for m, ref in ((3, send_far), (2, own_far), (1, send_near), (0, own_near)):
        b = n ^ m
        mean, scale, slope = (coef[m, k : k + 1, :] for k in range(3))
        level = block[2 * m : 2 * m + 1] * inverse[b]
        tilt = block[2 * m + 1 : 2 * m + 2] * inverse[b]
        level, tilt = level - mean * scale * tilt, scale * tilt

        def body(ds, carry):
            away = mask[b, ds, :] * (level + pre[m, ds, :] * tilt)
            grad_pre[m, ds, :] = (slope * (grad[m, ds, :] - away)).astype(BF)
            return carry

        by_rows(rows, body, 0)
        ref[...] = dot_nt(grad_pre[m], weight[...]).astype(ref.dtype)


def middle_join(idx, own, near, far, pre, coef, mask, grad, message):
    b = idx[0]
    mean, scale, slope, offset = (coef[k : k + 1, :] for k in range(4))
    back = mean * scale

    def body(ds, acc):
        values = pre[ds, :].astype(F32)
        act = values * slope + offset
        gate = sigmoid(act)
        total = own[ds, :] + near[ds, :].astype(F32) + far[ds, :].astype(F32)
        local = total * mask[b, ds, :] * (gate * (1.0 + act * (1.0 - gate)))
        grad[ds, :] = local
        return acc[0] + fold(local), acc[1] + fold(local * (values * scale - back))

    sums = by_rows(own.shape[0], body, zeros_acc(own.shape[1]))
    send_stats(message, column_sum(sums[0]), column_sum(sums[1]))


def middle_backward(idx, inverse, grad, pre, parts, coef, mask, first_pre, first_coef, to_canvas, to_rows,
                    w0, w1, w2, w3, own, near, far, grad_first, sums, message,
                    grad_pre, weight, gathered, canvas):
    n = idx[0]
    wide = parts.shape[0] // NARROW
    rows, places = grad.shape[0], to_canvas.shape[0]
    img = places // (SIDE * PITCH)
    margin = img * (PITCH + 1)
    every = total_of(parts, 0, wide)
    for b in range(1, NARROW):
        every = every + total_of(parts, b, wide)
    sums[0:1, :] = row_of(every, 0, n)
    sums[1:2, :] = row_of(every, NARROW, n)
    block = total_of(parts, n, wide)
    mean, scale, slope = (coef[k : k + 1, :] for k in range(3))
    level = wide_row(block, 0) * inverse[n]
    tilt = wide_row(block, NARROW) * inverse[n]
    level, tilt = level - mean * scale * tilt, scale * tilt

    def body(ds, carry):
        away = mask[n, ds, :] * (level + pre[ds, :].astype(F32) * tilt)
        grad_pre[ds, :] = (slope * (grad[ds, :] - away)).astype(BF)
        return carry

    by_rows(rows, body, 0)
    own[...] = grad_pre[:, lane_block(n)]
    near[...] = grad_pre[:, lane_block(n ^ 1)]
    far[0] = grad_pre[:, lane_block(n ^ 2)]
    far[1] = grad_pre[:, lane_block(n ^ 3)]
    for j, piece in enumerate((w0, w1, w2, w3)):
        for tap in range(TAPS):
            weight[tap, :, lane_block(n ^ j)] = piece[:, 128 * tap : 128 * tap + 128]
    canvas[...] = dot(to_canvas[...], grad_pre[...]).astype(BF).astype(F32)
    gathered[...] = jnp.zeros_like(gathered)
    for tap in range(TAPS):
        start = margin + ((tap // 3 - 1) * PITCH + tap % 3 - 1) * img
        gathered[start : start + places, :] += dot_nt(canvas[...].astype(BF), weight[tap])
    canvas[...] = gathered[margin : margin + places, :]
    grad_pre[...] = dot(to_rows[...], canvas[...].astype(BF)).astype(BF)
    mean, scale, slope, offset = (first_coef[0, k : k + 1, :] for k in range(4))
    back = mean * scale

    def finish(ds, acc):
        values = first_pre[ds, :].astype(F32)
        act = values * slope + offset
        gate = sigmoid(act)
        local = grad_pre[ds, :].astype(F32) * mask[n, ds, :] * (gate * (1.0 + act * (1.0 - gate)))
        grad_first[ds, :] = local.astype(BF)
        return acc[0] + fold(local), acc[1] + fold(local * (values * scale - back))

    sums2 = by_rows(rows, finish, zeros_acc(grad.shape[1]))
    send_stats(message, column_sum(sums2[0]), column_sum(sums2[1]))


def first_backward(idx, inverse, g0, g1, g2, g3, p0, p1, p2, p3, parts, coef, mask, x, grad, weight,
                   grad_input, sums, out, grad_pre, acc):
    n, z, y = idx[0], idx[1], idx[2]
    wide = parts.shape[0] // NARROW
    rows, channels = g0.shape
    every = None
    for m, (g, pre) in enumerate(((g0, p0), (g1, p1), (g2, p2), (g3, p3))):
        b = n ^ m
        block = total_of(parts, b, wide)
        every = block if every is None else every + block
        mean, scale, slope = (coef[m, k : k + 1, :] for k in range(3))
        level = wide_row(block, 0) * inverse[b]
        tilt = wide_row(block, NARROW) * inverse[b]
        level, tilt = level - mean * scale * tilt, scale * tilt

        def body(ds, carry):
            away = mask[b, ds, :] * (level + pre[ds, :].astype(F32) * tilt)
            grad_pre[m, ds, :] = (slope * (g[ds, :].astype(F32) - away)).astype(BF)
            return carry

        by_rows(rows, body, 0)
        product = dot_tn(x[b], grad_pre[m])
        if m == 0:
            acc[...] = product
        else:
            acc[...] += product
    if len(out.shape) == 2:
        out[...] = acc[...]
    else:
        half, cols = out.shape[1:]
        for place in range(out.shape[0]):
            top = pl.multiple_of((y ^ (place // NARROW)) * half, half)
            out[place] = acc[pl.ds(top, half), lane_block((z - place % NARROW) & 3)].astype(BF)
    for m in range(NARROW):
        grad_input[n ^ m] = dot_nt(grad_pre[m], weight[...]) + grad[m]
    sums[0:1, :] = row_of(every, 0, n)
    sums[1:2, :] = row_of(every, NARROW, n)


def last_weight(idx, hidden, grad_pre, *refs):
    acc = refs[-1]
    for m in range(NARROW):
        product = dot_tn(hidden[m], grad_pre[m])
        if m == 0:
            acc[...] = product
        else:
            acc[...] += product
    hand_out(idx, acc, refs[:-1])


def hand_out(idx, acc, outs):
    if len(outs) == 1:
        outs[0][...] = acc[...]
        return
    z, y = idx[1], idx[2]
    own, away = outs
    rows = acc.shape[0] // 8
    for j in range(4):
        place = pl.ds(j * rows, rows)
        for ref, dy in ((own, 0), (away, 1)):
            top = ((z ^ j) * 2 + (y ^ dy)) * rows
            ref[place, :] = acc[pl.ds(pl.multiple_of(top, rows), rows), :].astype(ref.dtype)


def middle_weight(idx, hidden, q0, q1, q2, q3, to_canvas, *refs):
    outs, (acc, shifted, canvas) = refs[:-3], refs[-3:]
    places = to_canvas.shape[0]
    img = places // (SIDE * PITCH)
    margin = img * (PITCH + 1)
    canvas[0:margin, :] = jnp.zeros((margin, 128), F32)
    canvas[margin + places :, :] = jnp.zeros((margin, 128), F32)
    for m, piece in enumerate((q0, q1, q2, q3)):
        canvas[margin : margin + places, :] = dot(to_canvas[...], piece[...])
        for tap in range(TAPS):
            start = margin - ((tap // 3 - 1) * PITCH + tap % 3 - 1) * img
            shifted[:, 128 * tap : 128 * tap + 128] = canvas[start : start + places, :].astype(BF)
        product = dot_tn(hidden[m], shifted[...])
        if m == 0:
            acc[...] = product
        else:
            acc[...] += product
    hand_out(idx, acc, outs)


def gather_weights(idx, *refs):
    pieces, (w_middle, w_last) = refs[:-2], refs[-2:]
    z, y = idx[1], idx[2]
    rows = w_last.shape[0] // 8
    for place, piece in enumerate(pieces):
        for dy in range(2):
            top = pl.multiple_of(((z ^ place) * 2 + (y ^ dy)) * rows, rows)
            here = pl.ds(top, rows)
            for tap in range(TAPS):
                w_middle[here, 128 * tap : 128 * tap + 128] = piece[dy, tap * rows : (tap + 1) * rows, :]
            for k in range(NARROW):
                w_last[here, 128 * k : 128 * k + 128] = piece[dy, (TAPS + k) * rows : (TAPS + k + 1) * rows, :]


def sum_pieces(pieces, out):
    acc = pieces[0][...].astype(F32)
    for piece in pieces[1:]:
        acc = acc + piece[...].astype(F32)
    out[...] = acc


def swap_core(values):
    return lax.ppermute(values, "narrow", [(i, i ^ 1) for i in range(NARROW)])


def swap_chip(values):
    return lax.ppermute(values, "narrow", [(i, i ^ 2) for i in range(NARROW)])


def swap_wide(values, step, wide):
    return lax.ppermute(values, "wide", [(i, i ^ step) for i in range(wide)])


def from_all(values):
    far = swap_chip(values)
    near = swap_core(values)
    return values, near, far, swap_core(far)


def reduce_narrow(send_far, own_far, send_near, own_near):
    got_far = swap_core(send_far)
    got_near = swap_core(send_near)
    joined = (own_far + got_far.astype(F32)).astype(BF)
    return own_near, got_near, swap_chip(joined)


def exchange(message, axes):
    return lax.all_to_all(message, axes, 0, 0, tiled=True)


def reduce_wide(own, away, wide):
    rows = own.shape[0] // 4
    total = own + swap_wide(away, 1, wide).astype(F32)
    parts = [
        swap_wide(total[j * rows : (j + 1) * rows].astype(BF), 2 * j, wide).astype(F32)
        for j in range(1, 4)
    ]
    return total[0:rows] + parts[0] + parts[1] + parts[2]


def transposed_steps():
    steps = []
    for dy in range(2):
        for j in range(NARROW):
            pairs = []
            for k in range(NARROW):
                for z in range(4):
                    for y in range(2):
                        pairs.append((k * 8 + 2 * z + y, z * 8 + 2 * ((k + j) % 4) + (y ^ dy)))
            steps.append(pairs)
    return steps


def on_device(inputs, sides, w_first, w_middle, w_last, gain_first, shift_first, gain_middle, shift_middle,
              gain_last, shift_last, cotangent, *, wide):
    micro, rows, low = inputs.shape
    img = sides.shape[1]
    mid = w_last.shape[0] * wide
    cols = w_first.shape[1]
    places = img * SIDE * PITCH
    direct = wide == 8
    n = lax.axis_index("narrow")
    w = lax.axis_index("wide")
    idx = jnp.stack([n, w // 2, w % 2]).astype(jnp.int32)

    spots = jnp.arange(rows, dtype=jnp.int32)
    spot_y, spot_x, spot_img = spots % 49 // 7, spots % 7, spots // 49
    limit = jnp.repeat(sides, 49, axis=1)
    mask = ((spot_y[None] < limit) & (spot_x[None] < limit)).astype(F32)[:, :, None]
    place = (spot_y * PITCH + spot_x) * img + spot_img
    to_canvas = (jnp.arange(places, dtype=jnp.int32)[:, None] == place[None, :]).astype(BF)
    to_rows = (place[:, None] == jnp.arange(places, dtype=jnp.int32)[None, :]).astype(BF)

    if direct:
        steps = transposed_steps()
        first_pieces = [lax.ppermute(w_first, MESH, pairs) for pairs in steps]
    else:
        first_all = lax.all_gather(lax.all_gather(w_first, "narrow", axis=1, tiled=True), "wide", axis=0, tiled=True)
        first_pieces = [lax.dynamic_slice_in_dim(first_all, n * low, low, 0)]

    counts = jnp.sum((sides * sides).astype(F32), axis=1)
    small = jnp.concatenate(
        [gain_first[None], shift_first[None], gain_middle[None], shift_middle[None],
         jnp.broadcast_to(jnp.pad(counts, (0, 128 - micro))[None], (4, 128))], axis=0
    )
    smalls = exchange(jnp.broadcast_to(small[None], (wide * NARROW, 8, 128)), BOTH)
    params = smalls[0:NARROW]
    inverse = 1.0 / jnp.sum(smalls[::NARROW, 4, 0:micro], axis=0)

    if direct:
        share = w_last.shape[0]
        packed = jnp.concatenate(
            [w_middle.reshape(TAPS * share, 128)] + [w_last[:, 128 * k : 128 * k + 128] for k in range(NARROW)], axis=0
        )
        pair = jnp.stack([packed, swap_wide(packed, 1, wide)])
        pieces = [pair] + [swap_wide(pair, 2 * j, wide) for j in range(1, 4)]
        middle_slice, last_slice = run(
            gather_weights, (idx,), pieces, [arr((mid, TAPS * 128), BF), arr((mid, low), BF)]
        )
    else:
        middle_slice = lax.all_gather(w_middle, "wide", axis=2, tiled=True)
        middle_slice = middle_slice.reshape(TAPS, mid, 128).transpose(1, 0, 2).reshape(mid, TAPS * 128)
        last_slice = lax.all_gather(w_last, "wide", axis=0, tiled=True)

    everyone = arr((wide * NARROW, 8, 128), F32)
    across = arr((wide, 8, low), F32)
    flat = arr((rows, mid), BF)
    flat32 = arr((rows, mid), F32)

    w_rows, send_far, own_far, send_near, own_near = run(
        first_product, (idx,), (inputs, *first_pieces),
        [arr((low, mid), BF), flat, flat32, flat, flat32], flops=2 * micro * rows * low * mid,
    )
    joined = reduce_narrow(send_far, own_far, send_near, own_near)
    pre_one, message = run(first_join, (idx,), (*joined, mask), [flat, everyone])
    pre_ones = from_all(pre_one)
    parts_one = exchange(message, BOTH)

    hidden_one, pre_two, coef_one, message = run(
        middle_forward, (idx, inverse), (*pre_ones, parts_one, params, mask, to_canvas, to_rows, middle_slice),
        [arr((micro, places, mid), BF), arr((micro, rows, 128), BF), arr((micro, 8, mid), F32), everyone],
        [pltpu.VMEM((rows, mid), BF), pltpu.VMEM((places + 2 * img * (PITCH + 1), TAPS * 128), F32), pltpu.VMEM((places, 128), BF)],
        flops=2 * micro * places * mid * TAPS * 128,
    )
    pre_twos = from_all(pre_two)
    parts_two = exchange(message, BOTH)

    hidden_two, own_two, coef_two, pre_three, message = run(
        last_forward, (idx, inverse), (*pre_twos, parts_two, params, mask, last_slice),
        [arr((micro, rows, mid), BF), flat, arr((8, mid), F32), arr((micro, rows, low), F32), across],
        flops=2 * micro * rows * low * mid,
    )
    parts_three = exchange(message, "wide")
    block_out, grad_sum, coef_three, message = run(
        block_output, (idx, inverse),
        (pre_three, inputs, cotangent, parts_three, gain_last[None], shift_last[None], mask),
        [arr(inputs.shape, BF), arr((micro, rows, low), F32), arr((micro, 8, low), F32), across],
    )
    parts_four = exchange(message, "wide")

    grad_three, send_far, own_far, send_near, own_near, sums_three = run(
        last_backward, (idx, inverse), (pre_three, grad_sum, parts_four, coef_three, mask, last_slice),
        [arr((micro, rows, low), BF), flat, flat32, flat, flat32, arr((2, low), F32)],
        flops=2 * micro * rows * low * mid,
    )
    joined = reduce_narrow(send_far, own_far, send_near, own_near)
    grad_two, message = run(middle_join, (idx,), (*joined, own_two, coef_two, mask), [flat32, everyone])
    parts_five = exchange(message, BOTH)

    middle_slices = from_all(middle_slice)
    own_q, near_q, far_q, grad_one, sums_two, message = run(
        middle_backward, (idx, inverse),
        (grad_two, own_two, parts_five, coef_two, mask, pre_one, coef_one, to_canvas, to_rows, *middle_slices),
        [arr((rows, 128), BF), arr((rows, 128), BF), arr((2, rows, 128), BF), flat, arr((2, 128), F32), everyone],
        [pltpu.VMEM((rows, mid), BF), pltpu.VMEM((TAPS, mid, mid), BF),
         pltpu.VMEM((places + 2 * img * (PITCH + 1), mid), F32), pltpu.VMEM((places, mid), F32)],
        flops=2 * places * mid * TAPS * mid,
    )
    grad_ones = from_all(grad_one)
    parts_six = exchange(message, BOTH)
    got_near = swap_core(near_q)
    got_far = swap_chip(far_q)
    got_last = swap_core(got_far[1])

    out_first = arr((8, 2 * low // NARROW, cols), BF) if direct else arr((low, mid), F32)
    input_grad, sums_one, first_sum = run(
        first_backward, (idx, inverse),
        (*grad_ones, *pre_ones, parts_six, coef_one, mask, inputs, grad_sum, w_rows),
        [arr((micro, rows, low), F32), arr((2, 128), F32), out_first],
        [pltpu.VMEM((micro, rows, mid), BF), pltpu.VMEM((low, mid), F32)],
        flops=4 * micro * rows * low * mid,
    )

    def handed(channels):
        if direct:
            return [arr((mid // 2, channels), F32), arr((mid // 2, channels), BF)]
        return [arr((mid, channels), F32)]

    last_sum = run(
        last_weight, (idx,), (hidden_two, grad_three), handed(low), [pltpu.VMEM((mid, low), F32)],
        flops=2 * micro * rows * low * mid,
    )
    middle_sum = run(
        middle_weight, (idx,), (hidden_one, own_q, got_near, got_far[0], got_last, to_canvas), handed(TAPS * 128),
        [pltpu.VMEM((mid, TAPS * 128), F32), pltpu.VMEM((places, TAPS * 128), BF),
         pltpu.VMEM((places + 2 * img * (PITCH + 1), 128), F32)],
        flops=2 * micro * places * mid * TAPS * 128,
    )
    if direct:
        grad_last = reduce_wide(*last_sum, wide)
        grad_middle = reduce_wide(*middle_sum, wide)
        arrived = [
            lax.ppermute(first_sum[k], MESH, [(dst, src) for src, dst in pairs]) for k, pairs in enumerate(steps)
        ]
        grad_first = arrived[0].astype(F32)
        for piece in arrived[1:]:
            grad_first = grad_first + piece.astype(F32)
    else:
        grad_last = lax.psum_scatter(last_sum[0], "wide", scatter_dimension=0, tiled=True)
        grad_middle = lax.psum_scatter(middle_sum[0], "wide", scatter_dimension=0, tiled=True)
        whole = lax.psum(first_sum, "wide")
        whole = lax.all_gather(whole, "narrow", axis=0, tiled=True)
        share = whole.shape[0] // wide
        grad_first = lax.dynamic_slice(whole, (w * share, n * cols), (share, cols))
    share = grad_middle.shape[0]
    grad_middle = grad_middle.reshape(share, TAPS, 128).transpose(1, 0, 2).reshape(3, 3, share, 128)
    return (
        block_out, input_grad, grad_first, grad_middle, grad_last,
        sums_one[1], sums_one[0], sums_two[1], sums_two[0], sums_three[1], sums_three[0],
    )


def solution(mesh):
    wide = mesh.shape["wide"]
    placed = (
        P(None, "wide", "narrow"),
        P(None, "wide"),
        P("wide", "narrow"),
        P(None, None, "wide", "narrow"),
        P("wide", "narrow"),
        P("narrow"),
        P("narrow"),
        P("narrow"),
        P("narrow"),
        P("narrow"),
        P("narrow"),
        P(None, "wide", "narrow"),
    )
    return jax.shard_map(
        lambda *arrays: on_device(*arrays, wide=wide),
        mesh=mesh,
        in_specs=placed,
        out_specs=(
            P(None, "wide", "narrow"),
            P(None, "wide", "narrow"),
            P("wide", "narrow"),
            P(None, None, "wide", "narrow"),
            P("wide", "narrow"),
            P("narrow"),
            P("narrow"),
            P("narrow"),
            P("narrow"),
            P("narrow"),
            P("narrow"),
        ),
        check_vma=False,
    )
```

time: 1000 us -> 346 us (0.35)
  waiting for transfers between devices: 423 us -> 89 us
  blocking collectives: 269 us -> 19.9 us
  local copies, waits for them, and re-layouts: 155 us -> 35.7 us
  Pallas kernels: 0 us -> 109 us
  starting transfers between devices: 1.2 us -> 79.6 us
  matrix products: 63 us -> 0 us
  other arithmetic: 69.3 us -> 10.1 us
  between operations: 16.7 us -> 1.1 us
    reduce_scatter x7 -> x0, waiting for transfers between devices: 283 us -> none  [the longest x4 115 us: on_device(): lax.psum_scatter(contract_cols(grad_pre_first, first_full).astype(jnp.bfl...]
    psum x6 -> x0, blocking collectives: 152 us -> none  [the longest x3 77.6 us: norm_backward(): lax.psum((jnp.sum(grad_out, axis=0), jnp.sum(grad_out * normed, axis=0)),...]
    unnamed x28 -> x0, waiting for transfers between devices: 130 us -> none
    all_gather x10 -> x0, blocking collectives: 117 us -> none  [the longest x1 33.2 us: on_device(): lax.all_gather(w_first, 'wide', axis=0, tiled=True)]
    pallas_call x0 -> x12, Pallas kernels: none -> 109 us  [run(): pl.pallas_call(kernel, out_shape=outs, in_specs=[pl.BlockSpec(memory_spac...]
    ppermute x0 -> x49, waiting for transfers between devices: none -> 77.9 us  [the longest x7 35.7 us: swap_chip(): return lax.ppermute(values, 'narrow', [(i, i ^ 2) for i in range(NARROW)])]
    dot_general x36 -> x0, matrix products: 63 us -> none  [the longest x12 20.2 us: contract_cols(): lax.dot_general(left, right, (((1,), (1,)), ((), ())), preferred_element_...]
    ppermute x0 -> x49, starting transfers between devices: none -> 61.6 us  [the longest x8 19.5 us: on_device(): first_pieces = [lax.ppermute(w_first, MESH, pairs) for pairs in steps]]
  transfers between devices with their start and end apart: 20 -> 54, of which waited for: 15 -> 18; matrix products, arithmetic and copies ran while one was open for 17% -> 5% of each run, Pallas kernels for 0% -> 25%
where the time goes in v1:
time: 346 us; the launch traced here: 345 us
  Pallas kernels  109 us (32%)
  waiting for transfers between devices  89 us (26%)
  starting transfers between devices  79.6 us (23%)
  local copies, waits for them, and re-layouts  35.7 us (10%)
  blocking collectives  19.9 us (6%)
  other arithmetic  10.1 us (3%)
    pallas_call x12, Pallas kernels, run(): pl.pallas_call(kernel, out_shape=outs, in_specs=[pl.BlockSpec(memory_spac...  109 us
    ppermute x7, waiting for transfers between devices, swap_chip(): return lax.ppermute(values, 'narrow', [(i, i ^ 2) for i in range(NARROW)])  35.7 us
    ppermute x12, waiting for transfers between devices, swap_wide(): return lax.ppermute(values, 'wide', [(i, i ^ step) for i in range(wide)])  32.6 us
    unnamed x98, local copies, waits for them, and re-layouts  28.1 us
    all_to_all x2, blocking collectives, exchange(): return lax.all_to_all(message, axes, 0, 0, tiled=True)  19.9 us
    ppermute x8, starting transfers between devices, on_device(): first_pieces = [lax.ppermute(w_first, MESH, pairs) for pairs in steps]  19.5 us
    all_to_all x5, starting transfers between devices, exchange(): return lax.all_to_all(message, axes, 0, 0, tiled=True)  18 us
    ppermute x12, starting transfers between devices, swap_wide(): return lax.ppermute(values, 'wide', [(i, i ^ step) for i in range(wide)])  17.9 us
  transfers between devices with their start and end apart: 54, of which 18 were waited for; matrix products, arithmetic and copies ran while one was open for 5% of the time, Pallas kernels for 25%

profile of v1, /device:TPU:0, one launch (start us, length us, event | category | flops | bytes accessed | tf_op | source)
XLA Modules:
  0.0 344.6 jit_solution(1399186721484361656)
XLA Ops:
  42.4 5.7 %collective-permute-done.10.far = bf16[392,512]{1,0:T(8,128)(2,1)S(1)} collective-permute-done((bf16[392,512]{1,0:T(8,128)(2,1)S(1)}, bf16[392,512]{1,0:T(8,128)(2,1)S(1)}, u32[]{:S(2)}, u32[]{:S(2)}) %collective-permute-start.10) | collective-permute-done | bytes 401440 | tf_op jit(solution)/shard_map/ppermute | solution.py:483
  58.6 3.6 %collective-permute-done.12.pre2.p2 = bf16[392,512]{1,0:T(8,128)(2,1)} collective-permute-done((bf16[392,512]{1,0:T(8,128)(2,1)S(1)}, bf16[392,512]{1,0:T(8,128)(2,1)}, u32[]{:S(2)}, u32[]{:S(2)}) %collective-permute-start.12) | collective-permute-done | bytes 401440 | tf_op jit(solution)/shard_map/ppermute | solution.py:483
  67.4 5.8 %collective-permute-done.15.refs_1_ = bf16[2,832,128]{2,1,0:T(8,128)(2,1)S(1)} collective-permute-done((bf16[2,832,128]{2,1,0:T(8,128)(2,1)S(1)}, bf16[2,832,128]{2,1,0:T(8,128)(2,1)S(1)}, u32[]{:S(2)}, u32[]{:S(2)}) %collective-permute-start.15) | collective-permute-done | bytes 426016 | tf_op jit(solution)/shard_map/ppermute | solution.py:487
  73.9 14.1 %collective-permute-done.16.refs_2_ = bf16[2,832,128]{2,1,0:T(8,128)(2,1)S(1)} collective-permute-done((bf16[2,832,128]{2,1,0:T(8,128)(2,1)S(1)}, bf16[2,832,128]{2,1,0:T(8,128)(2,1)S(1)}, u32[]{:S(2)}, u32[]{:S(2)}) %collective-permute-start.16) | collective-permute-done | bytes 426016 | tf_op jit(solution)/shard_map/ppermute | solution.py:487
  93.2 3.6 %all-to-all-done.1.parts = f32[32,8,128]{2,1,0:T(8,128)S(1)} async-done(((f32[32,8,128]{2,1,0:T(8,128)}), f32[32,8,128]{2,1,0:T(8,128)S(1)}, u32[]{:S(2)}, u32[]{:S(2)}) %all-to-all-start.1) | async-done | bytes 131104 | tf_op jit(solution)/shard_map/all_to_all | solution.py:504
  96.8 22.9 %shard_map.206 = (bf16[4,448,512]{2,1,0:T(8,128)(2,1)S(1)}, bf16[4,392,128]{2,1,0:T(8,128)(2,1)}, f32[4,8,512]{2,1,0:T(8,128)S(1)}, f32[32,8,128]{2,1,0:T(8,128)}) custom-call(s32[3]{0:T(128)S(1)} %pad_add_fusion.idx, f32[4]{0:T(128)S(1)} %broadcast_divide_fusion.inverse, bf16[392,512]{1,0:T(8,128)(2,1)S(1)} %get-tuple-element.58.pre0.first_pre.p0, ...), custom_call_target="tpu_custom_call" | custom-call | flops 2113929216 | bytes 6074496 | tf_op jit(solution)/shard_map/pallas_call | solution.py:35
  123.0 10.5 %collective-permute-done.19.src2 = bf16[4,392,128]{2,1,0:T(8,128)(2,1)S(1)} collective-permute-done((bf16[4,392,128]{2,1,0:T(8,128)(2,1)}, bf16[4,392,128]{2,1,0:T(8,128)(2,1)S(1)}, u32[]{:S(2)}, u32[]{:S(2)}) %collective-permute-start.19) | collective-permute-done | bytes 401440 | tf_op jit(solution)/shard_map/ppermute | solution.py:483
  139.7 6.4 %all-to-all-done.2.parts = f32[32,8,128]{2,1,0:T(8,128)S(1)} async-done(((f32[32,8,128]{2,1,0:T(8,128)}), f32[32,8,128]{2,1,0:T(8,128)S(1)}, u32[]{:S(2)}, u32[]{:S(2)}) %all-to-all-start.2) | async-done | bytes 131104 | tf_op jit(solution)/shard_map/all_to_all | solution.py:504
  151.9 24.6 %shard_map.207 = (bf16[4,392,512]{2,1,0:T(8,128)(2,1)S(1)}, bf16[392,512]{1,0:T(8,128)(2,1)S(1)}, f32[8,512]{1,0:T(8,128)S(1)}, f32[4,392,512]{2,1,0:T(8,128)S(1)}, f32[8,8,512]{2,1,0:T(8,128)S(1)}) custom-call(s32[3]{0:T(128)S(1)} %copy-done.33, f32[4]{0:T(128)S(1)} %copy-done.36, bf16[4,392,128]{2,1,0:T(8,128)(2,1)} %get-tuple-element.61.src0, ...), custom_call_target="tpu_custom_call" | custom-call | flops 822083584 | bytes 7649408 | tf_op jit(solution)/shard_map/pallas_call | solution.py:35
  176.5 10.0 %all_to_all.35.parts = f32[8,8,512]{2,1,0:T(8,128)S(1)} all-to-all(f32[8,8,512]{2,1,0:T(8,128)S(1)} %get-tuple-element.65), channel_id=1, replica_groups=mesh['narrow'=4,'wide'=8] {'wide'}, dimensions={0} | all-to-all | bytes 262144 | tf_op jit(solution)/shard_map/all_to_all | solution.py:504
  186.6 9.9 %shard_map.208 = (bf16[4,392,512]{2,1,0:T(8,128)(2,1)}, f32[4,392,512]{2,1,0:T(8,128)S(1)}, f32[4,8,512]{2,1,0:T(8,128)S(1)}, f32[8,8,512]{2,1,0:T(8,128)S(1)}) custom-call(s32[3]{0:T(128)S(1)} %copy-done.33, f32[4]{0:T(128)S(1)} %copy-done.36, f32[4,392,512]{2,1,0:T(8,128)S(1)} %get-tuple-element.64.pre, bf16[4,392,512]{2,1,0:T(8,128)(2,1)S(1)} %copy-done.3, ...), custom_call_target="tpu_custom_call" | custom-call | bytes 11577472 | tf_op jit(solution)/shard_map/pallas_call | solution.py:35
  196.5 9.8 %all_to_all.36.parts = f32[8,8,512]{2,1,0:T(8,128)S(1)} all-to-all(f32[8,8,512]{2,1,0:T(8,128)S(1)} %get-tuple-element.68), channel_id=1, replica_groups=mesh['narrow'=4,'wide'=8] {'wide'}, dimensions={0} | all-to-all | bytes 262144 | tf_op jit(solution)/shard_map/all_to_all | solution.py:504
  206.3 9.6 %shard_map.209 = (bf16[4,392,512]{2,1,0:T(8,128)(2,1)S(1)}, bf16[392,512]{1,0:T(8,128)(2,1)S(1)}, f32[392,512]{1,0:T(8,128)S(1)}, bf16[392,512]{1,0:T(8,128)(2,1...) custom-call(s32[3]{0:T(128)S(1)} %copy-done.34, f32[4]{0:T(128)S(1)} %copy-done.37, ...), custom_call_target="tpu_custom_call" | custom-call | flops 822083584 | bytes 11167872 | tf_op jit(solution)/shard_map/pallas_call | solution.py:35
  221.8 7.5 %collective-permute-done.23.far = bf16[392,512]{1,0:T(8,128)(2,1)S(1)} collective-permute-done((bf16[392,512]{1,0:T(8,128)(2,1)S(1)}, bf16[392,512]{1,0:T(8,128)(2,1)S(1)}, u32[]{:S(2)}, u32[]{:S(2)}) %collective-permute-start.23) | collective-permute-done | bytes 401440 | tf_op jit(solution)/shard_map/ppermute | solution.py:483
  238.9 3.6 %collective-permute-start.48 = (bf16[64,512]{1,0:T(8,128)(2,1)}, bf16[64,512]{1,0:T(8,128)(2,1)}, u32[]{:S(2)}, u32[]{:S(2)}) collective-permute-start(bf16[64,512]{1,0:T(8,128)(2,1)} %get-tuple-element.124), channel_id=1, source_target_pairs={{0,6},{1,7},{2,4},{3,5},{4,2},{5,3},{6,0},{7,1},{8,14},{9,15},{10,... | collective-permute-start | bytes 196616 | tf_op jit(solution)/shard_map/ppermute | solution.py:487
  247.6 10.6 %shard_map.211 = (bf16[392,128]{1,0:T(8,128)(2,1)S(1)}, bf16[392,128]{1,0:T(8,128)(2,1)S(1)}, bf16[2,392,128]{2,1,0:T(8,128)(2,1)}, bf16[392,512]{1,0:T(8,128)(2...) custom-call(s32[3]{0:T(128)S(1)} %copy-done.34, f32[4]{0:T(128)S(1)} %copy-done.37, f32[392,512]{1,0:T(8,128)S(1)} %copy-done.14, ...), custom_call_target="tpu_custom_call" | custom-call | flops 2113929216 | bytes 8180864 | tf_op jit(solution)/shard_map/pallas_call | solution.py:35
  263.2 5.0 %all-to-all-start.6 = ((f32[32,8,128]{2,1,0:T(8,128)}), f32[32,8,128]{2,1,0:T(8,128)S(1)}, u32[]{:S(2)}, u32[]{:S(2)}) async-start(f32[32,8,128]{2,1,0:T(8,128)} %copy-done.30), calls=%async_computation.6 | async-start | bytes 262144 | tf_op jit(solution)/shard_map/all_to_all | solution.py:504
  268.3 8.4 %collective-permute-done.39 = bf16[2,392,128]{2,1,0:T(8,128)(2,1)} collective-permute-done((bf16[2,392,128]{2,1,0:T(8,128)(2,1)}, bf16[2,392,128]{2,1,0:T(8,128)(2,1)}, u32[]{:S(2)}, u32[]{:S(2)}) %collective-permute-start.39) | collective-permute-done | bytes 200736 | tf_op jit(solution)/shard_map/ppermute | solution.py:483
  281.5 5.7 %shard_map.213 = (f32[256,1152]{1,0:T(8,128)S(1)}, bf16[256,1152]{1,0:T(8,128)(2,1)}) custom-call(s32[3]{0:T(128)S(1)} %copy-done.34, bf16[4,448,512]{2,1,0:T(8,128)(2,1)S(1)} %copy-done.44, bf16[392,128]{1,0:T(8,128)(2,1)S(1)} %copy-done.41, bf16[392,128]{1,0:T(8,128)(2,1)S(1)} %collective-permute-done.38.q1, bf16[392,128]{1,0:T(8,128)(2,1)S(1)} %get-tuple-element.127.q2, ...), custom_call_target="tpu_custom_call" | custom-call | flops 2113929216 | bytes 4357120 | tf_op jit(solution)/shard_map/pallas_call | solution.py:35
  291.5 13.4 %shard_map.212 = (f32[4,392,512]{2,1,0:T(8,128)}, f32[2,128]{1,0:T(2,128)S(1)}, bf16[8,256,128]{2,1,0:T(8,128)(2,1)S(1)}) custom-call(s32[3]{0:T(128)S(1)} %copy-done.34, f32[4]{0:T(128)S(1)} %copy-done.37, bf16[392,512]{1,0:T(8,128)(2,1)} %get-tuple-element.79.g0, bf16[392,512]{1,0:T(8,128)(2,1)} %collective-permute-done.27.g1, ...), custom_call_target="tpu_custom_call" | custom-call | flops 1644167168 | bytes 12491904 | tf_op jit(solution)/shard_map/pallas_call | solution.py:35
  316.0 5.2 %collective-permute-done.36 = bf16[256,128]{1,0:T(8,128)(2,1)S(1)} collective-permute-done((bf16[256,128]{1,0:T(8,128)(2,1)S(1)}, bf16[256,128]{1,0:T(8,128)(2,1)S(1)}, u32[]{:S(2)}, u32[]{:S(2)}) %collective-permute-start.36) | collective-permute-done | bytes 65568 | tf_op jit(solution)/shard_map/ppermute | solution.py:669
  322.8 6.8 %collective-permute-start.44 = (bf16[64,1152]{1,0:T(8,128)(2,1)S(1)}, bf16[64,1152]{1,0:T(8,128)(2,1)S(1)}, u32[]{:S(2)}, u32[]{:S(2)}) collective-permute-start(bf16[64,1152]{1,0:T(8,128)(2,1)S(1)} %get-tuple-element.113), channel_id=1, source_target_pairs={{0,6},{1,7},{2,4},{3,5},{4,2},{5,3},{6,0},{7,1},{8,14},{9,15},{10,... | collective-permute-start | bytes 442376 | tf_op jit(solution)/shard_map/ppermute | solution.py:487
  331.0 4.6 %collective-permute-done.44 = bf16[64,1152]{1,0:T(8,128)(2,1)S(1)} collective-permute-done((bf16[64,1152]{1,0:T(8,128)(2,1)S(1)}, bf16[64,1152]{1,0:T(8,128)(2,1)S(1)}, u32[]{:S(2)}, u32[]{:S(2)}) %collective-permute-start.44) | collective-permute-done | bytes 147488 | tf_op jit(solution)/shard_map/ppermute | solution.py:487
  335.6 8.0 %collective-permute-done.43 = bf16[64,1152]{1,0:T(8,128)(2,1)S(1)} collective-permute-done((bf16[64,1152]{1,0:T(8,128)(2,1)S(1)}, bf16[64,1152]{1,0:T(8,128)(2,1)S(1)}, u32[]{:S(2)}, u32[]{:S(2)}) %collective-permute-start.43) | collective-permute-done | bytes 147488 | tf_op jit(solution)/shard_map/ppermute | solution.py:487
  (230 shorter events, 128.0 us)
Async XLA Ops:
  0.6 19.7 %collective-permute-start = (bf16[256,128]{1,0:T(8,128)(2,1)}, bf16[256,128]{1,0:T(8,128)(2,1)S(1)}, u32[]{:S(2)}, u32[]{:S(2)}) collective-permute-start(bf16[256,128]{1,0:T(8,128)(2,1)} %param.14), channel_id=1, source_target_pairs={{0,0},{1,1},{2,8},{3,9},{4,16},{5,17},{6,24},{7,25},{8,2},{9,3},{1... | collective-permute-start | bytes 196616 | tf_op jit(solution)/shard_map/ppermute | solution.py:552
  2.1 20.7 %collective-permute-start.1 = (bf16[256,128]{1,0:T(8,128)(2,1)}, bf16[256,128]{1,0:T(8,128)(2,1)S(1)}, u32[]{:S(2)}, u32[]{:S(2)}) collective-permute-start(bf16[256,128]{1,0:T(8,128)(2,1)} %param.14), channel_id=1, source_target_pairs={{0,2},{1,3},{2,10},{3,11},{4,18},{5,19},{6,26},{7,27},{8,4},{9,5},... | collective-permute-start | bytes 196616 | tf_op jit(solution)/shard_map/ppermute | solution.py:552
  5.7 19.6 %collective-permute-start.2 = (bf16[256,128]{1,0:T(8,128)(2,1)}, bf16[256,128]{1,0:T(8,128)(2,1)S(1)}, u32[]{:S(2)}, u32[]{:S(2)}) collective-permute-start(bf16[256,128]{1,0:T(8,128)(2,1)} %param.14), channel_id=1, source_target_pairs={{0,4},{1,5},{2,12},{3,13},{4,20},{5,21},{6,28},{7,29},{8,6},{9,7},... | collective-permute-start | bytes 196616 | tf_op jit(solution)/shard_map/ppermute | solution.py:552
  9.0 18.3 %collective-permute-start.3 = (bf16[256,128]{1,0:T(8,128)(2,1)}, bf16[256,128]{1,0:T(8,128)(2,1)S(1)}, u32[]{:S(2)}, u32[]{:S(2)}) collective-permute-start(bf16[256,128]{1,0:T(8,128)(2,1)} %param.14), channel_id=1, source_target_pairs={{0,6},{1,7},{2,14},{3,15},{4,22},{5,23},{6,30},{7,31},{8,0},{9,1},... | collective-permute-start | bytes 196616 | tf_op jit(solution)/shard_map/ppermute | solution.py:552
  15.4 47.0 %all-to-all-start = ((f32[32,8,128]{2,1,0:T(8,128)}), f32[32,8,128]{2,1,0:T(8,128)}, u32[]{:S(2)}, u32[]{:S(2)}) async-start(f32[32,8,128]{2,1,0:T(8,128)} %broadcast_in_dim.45), calls=%async_computation | async-start | bytes 262144 | tf_op jit(solution)/shard_map/all_to_all | solution.py:504
  54.1 19.0 %collective-permute-start.15 = (bf16[2,832,128]{2,1,0:T(8,128)(2,1)S(1)}, bf16[2,832,128]{2,1,0:T(8,128)(2,1)S(1)}, u32[]{:S(2)}, u32[]{:S(2)}) collective-permute-start(bf16[2,832,128]{2,1,0:T(8,128)(2,1)S(1)} %pad_maximum_fusion.refs_0_), channel_id=1, source_target_pairs={{0,2},{1,3},{2,0},{3,1},{4,6},{5,7},{6,4},{7,5},{8,10},{9,11},{10,... | collective-permute-start | bytes 1277960 | tf_op jit(solution)/shard_map/ppermute | solution.py:487
  54.7 33.3 %collective-permute-start.16 = (bf16[2,832,128]{2,1,0:T(8,128)(2,1)S(1)}, bf16[2,832,128]{2,1,0:T(8,128)(2,1)S(1)}, u32[]{:S(2)}, u32[]{:S(2)}) collective-permute-start(bf16[2,832,128]{2,1,0:T(8,128)(2,1)S(1)} %pad_maximum_fusion.refs_0_), channel_id=1, source_target_pairs={{0,4},{1,5},{2,6},{3,7},{4,0},{5,1},{6,2},{7,3},{8,12},{9,13},{10,... | collective-permute-start | bytes 1277960 | tf_op jit(solution)/shard_map/ppermute | solution.py:487
  56.2 32.6 %collective-permute-start.17 = (bf16[2,832,128]{2,1,0:T(8,128)(2,1)S(1)}, bf16[2,832,128]{2,1,0:T(8,128)(2,1)}, u32[]{:S(2)}, u32[]{:S(2)}) collective-permute-start(bf16[2,832,128]{2,1,0:T(8,128)(2,1)S(1)} %pad_maximum_fusion.refs_0_), channel_id=1, source_target_pairs={{0,6},{1,7},{2,4},{3,5},{4,2},{5,3},{6,0},{7,1},{8,14},{9,15},{10,... | collective-permute-start | bytes 1277960 | tf_op jit(solution)/shard_map/ppermute | solution.py:487
  58.6 38.1 %collective-permute-start.11 = (bf16[392,512]{1,0:T(8,128)(2,1)S(1)}, bf16[392,512]{1,0:T(8,128)(2,1)}, u32[]{:S(2)}, u32[]{:S(2)}) collective-permute-start(bf16[392,512]{1,0:T(8,128)(2,1)S(1)} %get-tuple-element.58.pre0.first_pre.p0), channel_id=1, source_target_pairs={{0,8},{8,0},{16,24},{24,16},{1,9},{9,1},{17,25},{25,17},{2,10},{10... | collective-permute-start | bytes 1204232 | tf_op jit(solution)/shard_map/ppermute | solution.py:479
  62.2 34.5 %collective-permute-start.13 = (bf16[392,512]{1,0:T(8,128)(2,1)}, bf16[392,512]{1,0:T(8,128)(2,1)}, u32[]{:S(2)}, u32[]{:S(2)}) collective-permute-start(bf16[392,512]{1,0:T(8,128)(2,1)} %collective-permute-done.12.pre2.p2), channel_id=1, source_target_pairs={{0,8},{8,0},{16,24},{24,16},{1,9},{9,1},{17,25},{25,17},{2,10},{10... | collective-permute-start | bytes 1204232 | tf_op jit(solution)/shard_map/ppermute | solution.py:479
  62.4 34.4 %all-to-all-start.1 = ((f32[32,8,128]{2,1,0:T(8,128)}), f32[32,8,128]{2,1,0:T(8,128)S(1)}, u32[]{:S(2)}, u32[]{:S(2)}) async-start(f32[32,8,128]{2,1,0:T(8,128)} %get-tuple-element.59), calls=%async_computation.1 | async-start | bytes 262144 | tf_op jit(solution)/shard_map/all_to_all | solution.py:504
  123.0 23.0 %collective-permute-start.18 = (bf16[4,392,128]{2,1,0:T(8,128)(2,1)}, bf16[4,392,128]{2,1,0:T(8,128)(2,1)S(1)}, u32[]{:S(2)}, u32[]{:S(2)}) collective-permute-start(bf16[4,392,128]{2,1,0:T(8,128)(2,1)} %get-tuple-element.61.src0), channel_id=1, source_target_pairs={{0,8},{8,0},{16,24},{24,16},{1,9},{9,1},{17,25},{25,17},{2,10},{10... | collective-permute-start | bytes 1204232 | tf_op jit(solution)/shard_map/ppermute | solution.py:479
  137.8 78.7 %collective-permute-start.25 = (bf16[512,1152]{1,0:T(8,128)(2,1)}, bf16[512,1152]{1,0:T(8,128)(2,1)}, u32[]{:S(2)}, u32[]{:S(2)}) collective-permute-start(bf16[512,1152]{1,0:T(8,128)(2,1)} %get-tuple-element.60.weight.w0), channel_id=1, source_target_pairs={{0,16},{8,24},{16,0},{24,8},{1,17},{9,25},{17,1},{25,9},{2,18},{10... | collective-permute-start | bytes 3538952 | tf_op jit(solution)/shard_map/ppermute | solution.py:483
  216.1 27.2 %collective-permute-start.24 = (bf16[512,1152]{1,0:T(8,128)(2,1)}, bf16[512,1152]{1,0:T(8,128)(2,1)}, u32[]{:S(2)}, u32[]{:S(2)}) collective-permute-start(bf16[512,1152]{1,0:T(8,128)(2,1)} %get-tuple-element.60.weight.w0), channel_id=1, source_target_pairs={{0,8},{8,0},{16,24},{24,16},{1,9},{9,1},{17,25},{25,17},{2,10},{10... | collective-permute-start | bytes 3538952 | tf_op jit(solution)/shard_map/ppermute | solution.py:479
  216.6 26.7 %collective-permute-start.26 = (bf16[512,1152]{1,0:T(8,128)(2,1)}, bf16[512,1152]{1,0:T(8,128)(2,1)}, u32[]{:S(2)}, u32[]{:S(2)}) collective-permute-start(bf16[512,1152]{1,0:T(8,128)(2,1)} %collective-permute-done.25.w2), channel_id=1, source_target_pairs={{0,8},{8,0},{16,24},{24,16},{1,9},{9,1},{17,25},{25,17},{2,10},{10... | collective-permute-start | bytes 3538952 | tf_op jit(solution)/shard_map/ppermute | solution.py:479
  238.9 22.6 %collective-permute-start.48 = (bf16[64,512]{1,0:T(8,128)(2,1)}, bf16[64,512]{1,0:T(8,128)(2,1)}, u32[]{:S(2)}, u32[]{:S(2)}) collective-permute-start(bf16[64,512]{1,0:T(8,128)(2,1)} %get-tuple-element.124), channel_id=1, source_target_pairs={{0,6},{1,7},{2,4},{3,5},{4,2},{5,3},{6,0},{7,1},{8,14},{9,15},{10,... | collective-permute-start | bytes 196616 | tf_op jit(solution)/shard_map/ppermute | solution.py:487
  242.5 19.0 %collective-permute-start.47 = (bf16[64,512]{1,0:T(8,128)(2,1)}, bf16[64,512]{1,0:T(8,128)(2,1)}, u32[]{:S(2)}, u32[]{:S(2)}) collective-permute-start(bf16[64,512]{1,0:T(8,128)(2,1)} %get-tuple-element.125), channel_id=1, source_target_pairs={{0,4},{1,5},{2,6},{3,7},{4,0},{5,1},{6,2},{7,3},{8,12},{9,13},{10,... | collective-permute-start | bytes 196616 | tf_op jit(solution)/shard_map/ppermute | solution.py:487
  242.5 19.0 %collective-permute-start.46 = (bf16[64,512]{1,0:T(8,128)(2,1)}, bf16[64,512]{1,0:T(8,128)(2,1)}, u32[]{:S(2)}, u32[]{:S(2)}) collective-permute-start(bf16[64,512]{1,0:T(8,128)(2,1)} %get-tuple-element.123), channel_id=1, source_target_pairs={{0,2},{1,3},{2,0},{3,1},{4,6},{5,7},{6,4},{7,5},{8,10},{9,11},{10,... | collective-permute-start | bytes 196616 | tf_op jit(solution)/shard_map/ppermute | solution.py:487
  259.5 18.3 %collective-permute-start.28 = (bf16[392,512]{1,0:T(8,128)(2,1)}, bf16[392,512]{1,0:T(8,128)(2,1)}, u32[]{:S(2)}, u32[]{:S(2)}) collective-permute-start(bf16[392,512]{1,0:T(8,128)(2,1)} %get-tuple-element.79.g0), channel_id=1, source_target_pairs={{0,16},{8,24},{16,0},{24,8},{1,17},{9,25},{17,1},{25,9},{2,18},{10... | collective-permute-start | bytes 1204232 | tf_op jit(solution)/shard_map/ppermute | solution.py:483
  260.0 16.7 %collective-permute-start.39 = (bf16[2,392,128]{2,1,0:T(8,128)(2,1)}, bf16[2,392,128]{2,1,0:T(8,128)(2,1)}, u32[]{:S(2)}, u32[]{:S(2)}) collective-permute-start(bf16[2,392,128]{2,1,0:T(8,128)(2,1)} %get-tuple-element.87), channel_id=1, source_target_pairs={{0,16},{8,24},{16,0},{24,8},{1,17},{9,25},{17,1},{25,9},{2,18},{10... | collective-permute-start | bytes 602120 | tf_op jit(solution)/shard_map/ppermute | solution.py:483
  263.2 25.3 %collective-permute-start.27 = (bf16[392,512]{1,0:T(8,128)(2,1)}, bf16[392,512]{1,0:T(8,128)(2,1)}, u32[]{:S(2)}, u32[]{:S(2)}) collective-permute-start(bf16[392,512]{1,0:T(8,128)(2,1)} %get-tuple-element.79.g0), channel_id=1, source_target_pairs={{0,8},{8,0},{16,24},{24,16},{1,9},{9,1},{17,25},{25,17},{2,10},{10... | collective-permute-start | bytes 1204232 | tf_op jit(solution)/shard_map/ppermute | solution.py:479
  263.2 25.3 %all-to-all-start.6 = ((f32[32,8,128]{2,1,0:T(8,128)}), f32[32,8,128]{2,1,0:T(8,128)S(1)}, u32[]{:S(2)}, u32[]{:S(2)}) async-start(f32[32,8,128]{2,1,0:T(8,128)} %copy-done.30), calls=%async_computation.6 | async-start | bytes 262144 | tf_op jit(solution)/shard_map/all_to_all | solution.py:504
  288.3 23.9 %collective-permute-start.41 = (bf16[256,1152]{1,0:T(8,128)(2,1)}, bf16[256,1152]{1,0:T(8,128)(2,1)}, u32[]{:S(2)}, u32[]{:S(2)}) collective-permute-start(bf16[256,1152]{1,0:T(8,128)(2,1)} %get-tuple-element.89), channel_id=1, source_target_pairs={{0,1},{1,0},{2,3},{3,2},{4,5},{5,4},{6,7},{7,6},{8,9},{9,8},{10,11... | collective-permute-start | bytes 1769480 | tf_op jit(solution)/shard_map/ppermute | solution.py:487
  312.1 17.4 %collective-permute-start.33 = (bf16[256,128]{1,0:T(8,128)(2,1)S(1)}, bf16[256,128]{1,0:T(8,128)(2,1)S(1)}, u32[]{:S(2)}, u32[]{:S(2)}) collective-permute-start(bf16[256,128]{1,0:T(8,128)(2,1)S(1)} %get-tuple-element.120), channel_id=1, source_target_pairs={{6,0},{7,1},{14,2},{15,3},{22,4},{23,5},{30,6},{31,7},{0,8},{1,9},... | collective-permute-start | bytes 196616 | tf_op jit(solution)/shard_map/ppermute | solution.py:669
  (77 other events, 829.8 us)

commit v2 on v1

v2 whole, which is shorter than its diff:
```python
import jax
import jax.numpy as jnp
from jax import lax
from jax.experimental import pallas as pl
from jax.experimental.pallas import tpu as pltpu
from jax.sharding import PartitionSpec as P


F32 = jnp.float32
BF = jnp.bfloat16
EPS = 1e-05
SIDE = 7
PITCH = 8
TAPS = 9
NARROW = 4
MESH = ("narrow", "wide")
VMEM_BYTES = 20 * 2**20


def dot(left, right):
    return jnp.dot(left, right, preferred_element_type=F32)


def dot_nt(left, right):
    return lax.dot_general(left, right, (((1,), (1,)), ((), ())), preferred_element_type=F32)


def dot_tn(left, right):
    return lax.dot_general(left, right, (((0,), (0,)), ((), ())), preferred_element_type=F32)


def position():
    n, w = lax.axis_index("narrow"), lax.axis_index("wide")
    return n, w // 2, w % 2


def run(kernel, operands, outs, scratch=(), flops=0):
    moved = sum(o.size * o.dtype.itemsize for o in (*operands, *outs))
    return pl.pallas_call(
        kernel,
        out_shape=outs,
        name=kernel.__name__,
        in_specs=[pl.BlockSpec(memory_space=pltpu.VMEM)] * len(operands),
        out_specs=[pl.BlockSpec(memory_space=pltpu.VMEM)] * len(outs),
        scratch_shapes=list(scratch),
        cost_estimate=pl.CostEstimate(flops=flops, bytes_accessed=moved, transcendentals=0),
        compiler_params=pltpu.CompilerParams(vmem_limit_bytes=VMEM_BYTES),
    )(*operands)


def arr(shape, dtype):
    return jax.ShapeDtypeStruct(shape, dtype)


def by_rows(rows, body, carry):
    return body(pl.ds(0, rows), carry)


def fold(values):
    total = values[0:8]
    for start in range(8, values.shape[0], 8):
        total = total + values[start : start + 8]
    return total


def zeros_acc(channels):
    return (jnp.zeros((8, channels), F32), jnp.zeros((8, channels), F32))


def column_sum(acc):
    return jnp.sum(acc, axis=0, keepdims=True)


def sigmoid(values):
    return 0.5 * jnp.tanh(0.5 * values) + 0.5


def coefficients(total, squares, inverse, gain, shift):
    mean = total * inverse
    spread = squares * inverse - mean * mean
    scale = lax.rsqrt(spread + EPS)
    slope = gain * scale
    return mean, scale, slope, shift - mean * slope


def wide_row(block, first, count=NARROW):
    return jnp.concatenate([block[first + k : first + k + 1] for k in range(count)], axis=1)


def row_of(block, first, index):
    rows = [jnp.where(index == k, block[first + k : first + k + 1], 0.0) for k in range(NARROW)]
    return rows[0] + rows[1] + rows[2] + rows[3]


def inverse_count(params, b, channels):
    row = params[b, 4:5, :]
    return row if channels == 128 else jnp.concatenate([row] * (channels // 128), axis=1)


def lane_block(index):
    return pl.ds(pl.multiple_of(index * 128, 128), 128)


def send_stats(message, first, second):
    for k in range(NARROW):
        message[k : k + 1, :] = first[:, 128 * k : 128 * k + 128]
        message[NARROW + k : NARROW + k + 1, :] = second[:, 128 * k : 128 * k + 128]


def first_product(x, *refs):
    pieces, (w_first, send_far, own_far, send_near, own_near) = refs[:-5], refs[-5:]
    n, z, y = position()
    if len(pieces) == 1:
        w_first[...] = pieces[0][...]
    else:
        rows, cols = pieces[0].shape
        for place, piece in enumerate(pieces):
            half = y ^ (place // NARROW)
            block = (z - place % NARROW) & 3
            w_first[pl.ds(pl.multiple_of(half * rows, rows), rows), lane_block(block)] = piece[...]
    for ref, m in ((send_far, 3), (own_far, 2), (send_near, 1), (own_near, 0)):
        ref[...] = dot(x[n ^ m], w_first[...]).astype(ref.dtype)


def first_join(own, near, far, mask, small, pre, message):
    b = position()[0]

    def body(ds, acc):
        values = own[ds, :] + near[ds, :].astype(F32) + far[ds, :].astype(F32)
        pre[ds, :] = values.astype(BF)
        kept = mask[b, ds, :] * values
        return acc[0] + fold(kept), acc[1] + fold(kept * values)

    sums = by_rows(own.shape[0], body, zeros_acc(own.shape[1]))
    send_stats(message, column_sum(sums[0]), column_sum(sums[1]))
    message[8:16, :] = small[...]


def middle_forward(pre0, pre1, pre2, pre3, sum0, sum1, sum2, sum3, mask, to_canvas, to_rows, weight,
                   hidden, pre, coef, message, params, active, spread, joined):
    n = position()[0]
    blocks = (sum0[...], sum1[...], sum2[...], sum3[...])
    for m, block in enumerate(blocks):
        params[n ^ m, 0:4, :] = block[8:12]
    for b in range(NARROW):
        params[b, 4:5, :] = 1.0 / blocks[0][12 + b : 13 + b]
        params[b, 5:8, :] = jnp.zeros((3, 128), F32)
    rows, places = pre0.shape[0], to_canvas.shape[0]
    img = places // (SIDE * PITCH)
    margin = img * (PITCH + 1)
    gain = jnp.concatenate([params[k, 0:1, :] for k in range(NARROW)], axis=1)
    shift = jnp.concatenate([params[k, 1:2, :] for k in range(NARROW)], axis=1)
    spread[0:margin, :] = jnp.zeros((margin, spread.shape[1]), F32)
    spread[margin + places :, :] = jnp.zeros((margin, spread.shape[1]), F32)
    line = img * PITCH
    for m, source in enumerate((pre0, pre1, pre2, pre3)):
        b = n ^ m
        block = blocks[m]
        mean, scale, slope, offset = coefficients(
            wide_row(block, 0), wide_row(block, NARROW), inverse_count(params, b, gain.shape[1]), gain, shift
        )
        for k, row in enumerate((mean, scale, slope, offset)):
            coef[m, k : k + 1, :] = row

        def activate(ds, carry):
            act = source[ds, :].astype(F32) * slope + offset
            active[ds, :] = (mask[b, ds, :] * act * sigmoid(act)).astype(BF)
            return carry

        by_rows(rows, activate, 0)
        hidden[m] = dot(to_canvas[...], active[...]).astype(BF)
        spread[margin : margin + places, :] = dot(hidden[m], weight[...])
        for top in range(SIDE):
            acc = None
            for tap in range(TAPS):
                start = margin + top * line + ((tap // 3 - 1) * PITCH + tap % 3 - 1) * img
                part = spread[start : start + line, 128 * tap : 128 * tap + 128]
                acc = part if acc is None else acc + part
            joined[top * line : (top + 1) * line, :] = acc.astype(BF)
        pre[m] = dot(to_rows[...], joined[...]).astype(BF)

        def collect(ds, acc):
            values = pre[m, ds, :].astype(F32)
            kept = mask[b, ds, :] * values
            return acc[0] + fold(kept), acc[1] + fold(kept * values)

        sums = by_rows(rows, collect, zeros_acc(128))
        message[2 * m : 2 * m + 1, :] = column_sum(sums[0])
        message[2 * m + 1 : 2 * m + 2, :] = column_sum(sums[1])


def last_forward(src0, src1, src2, src3, sum0, sum1, sum2, sum3, params, mask, weight,
                 hidden, own, coef, pre, message):
    n = position()[0]
    rows = own.shape[0]
    sources = (src0, src1, src2, src3)
    blocks = (sum0[...], sum1[...], sum2[...], sum3[...])
    for m in range(NARROW):
        b = n ^ m
        for i in range(NARROW):
            j = m ^ i
            here = lane_block(n ^ i)
            mean, scale, slope, offset = coefficients(
                blocks[i][2 * j : 2 * j + 1], blocks[i][2 * j + 1 : 2 * j + 2], inverse_count(params, b, 128),
                params[n ^ i, 2:3, :], params[n ^ i, 3:4, :],
            )
            if m == 0:
                own[:, here] = sources[i][j]
                for k, row in enumerate((mean, scale, slope, offset)):
                    coef[k : k + 1, here] = row

            def activate(ds, carry):
                act = sources[i][j, ds, :].astype(F32) * slope + offset
                hidden[m, ds, here] = (mask[b, ds, :] * act * sigmoid(act)).astype(BF)
                return carry

            by_rows(rows, activate, 0)
        pre[m] = dot(hidden[m], weight[...])

        def collect(ds, acc):
            values = pre[m, ds, :]
            kept = mask[b, ds, :] * values
            return acc[0] + fold(kept), acc[1] + fold(kept * values)

        sums = by_rows(rows, collect, zeros_acc(pre.shape[2]))
        message[2 * m : 2 * m + 1, :] = column_sum(sums[0])
        message[2 * m + 1 : 2 * m + 2, :] = column_sum(sums[1])


def block_output(pre, x, cotangent, parts, params, gain, shift, mask, out, grad, coef, message):
    n = position()[0]
    rows, channels = pre.shape[1:]
    block = parts[...]
    for m in range(NARROW):
        b = n ^ m
        mean, scale, slope, offset = coefficients(
            block[2 * m : 2 * m + 1], block[2 * m + 1 : 2 * m + 2], inverse_count(params, b, channels), gain[...], shift[...]
        )
        for k, row in enumerate((mean, scale, slope, offset)):
            coef[m, k : k + 1, :] = row
        back = mean * scale

        def body(ds, acc):
            values = pre[m, ds, :]
            inside = mask[b, ds, :]
            summed = values * slope + offset + x[b, ds, :].astype(F32)
            gate = sigmoid(summed)
            value = summed * gate
            out[b, ds, :] = (inside * value).astype(BF)
            local = inside * cotangent[b, ds, :].astype(F32) * (gate + value * (1.0 - gate))
            grad[m, ds, :] = local
            return acc[0] + fold(local), acc[1] + fold(local * (values * scale - back))

        sums = by_rows(rows, body, zeros_acc(channels))
        message[2 * m : 2 * m + 1, :] = column_sum(sums[0])
        message[2 * m + 1 : 2 * m + 2, :] = column_sum(sums[1])


def last_backward(pre, grad, parts, params, coef, mask, weight,
                  grad_pre, send_far, own_far, send_near, own_near, level_sum, tilt_sum):
    n = position()[0]
    rows = pre.shape[1]
    block = parts[...]
    for s, ref in enumerate((level_sum, tilt_sum)):
        acc = block[s : s + 1]
        for m in range(1, NARROW):
            acc = acc + block[2 * m + s : 2 * m + s + 1]
        ref[...] = acc
    for m, ref in ((3, send_far), (2, own_far), (1, send_near), (0, own_near)):
        b = n ^ m
        mean, scale, slope = (coef[m, k : k + 1, :] for k in range(3))
        inverse = inverse_count(params, b, block.shape[1])
        level = block[2 * m : 2 * m + 1] * inverse
        tilt = block[2 * m + 1 : 2 * m + 2] * inverse
        level, tilt = level - mean * scale * tilt, scale * tilt

        def body(ds, carry):
            away = mask[b, ds, :] * (level + pre[m, ds, :] * tilt)
            grad_pre[m, ds, :] = (slope * (grad[m, ds, :] - away)).astype(BF)
            return carry

        by_rows(rows, body, 0)
        ref[...] = dot_nt(grad_pre[m], weight[...]).astype(ref.dtype)


def middle_join(own, near, far, pre, coef, mask, grad, own_q, near_q, far_q, last_q, message):
    b = position()[0]
    mean, scale, slope, offset = (coef[k : k + 1, :] for k in range(4))
    back = mean * scale

    def body(ds, acc):
        values = pre[ds, :].astype(F32)
        act = values * slope + offset
        gate = sigmoid(act)
        total = own[ds, :] + near[ds, :].astype(F32) + far[ds, :].astype(F32)
        local = total * mask[b, ds, :] * (gate * (1.0 + act * (1.0 - gate)))
        grad[ds, :] = local
        return acc[0] + fold(local), acc[1] + fold(local * (values * scale - back))

    sums = by_rows(own.shape[0], body, zeros_acc(own.shape[1]))
    send_stats(message, column_sum(sums[0]), column_sum(sums[1]))
    own_q[...] = grad[:, lane_block(b)].astype(BF)
    near_q[...] = grad[:, lane_block(b ^ 1)].astype(BF)
    far_q[...] = grad[:, lane_block(b ^ 2)].astype(BF)
    last_q[...] = grad[:, lane_block(b ^ 3)].astype(BF)


def middle_backward(grad, pre, parts, params, coef, mask, first_pre, first_coef, to_canvas, to_rows,
                    w0, w1, w2, w3, grad_first, message,
                    grad_pre, weight, gathered, canvas):
    n = position()[0]
    rows, places = grad.shape[0], to_canvas.shape[0]
    img = places // (SIDE * PITCH)
    margin = img * (PITCH + 1)
    block = parts[...]
    mean, scale, slope = (coef[k : k + 1, :] for k in range(3))
    inverse = inverse_count(params, n, grad.shape[1])
    level = wide_row(block, 0) * inverse
    tilt = wide_row(block, NARROW) * inverse
    level, tilt = level - mean * scale * tilt, scale * tilt

    def body(ds, carry):
        away = mask[n, ds, :] * (level + pre[ds, :].astype(F32) * tilt)
        grad_pre[ds, :] = (slope * (grad[ds, :] - away)).astype(BF)
        return carry

    by_rows(rows, body, 0)
    for j, piece in enumerate((w0, w1, w2, w3)):
        for tap in range(TAPS):
            weight[tap, :, lane_block(n ^ j)] = piece[:, 128 * tap : 128 * tap + 128]
    canvas[...] = dot(to_canvas[...], grad_pre[...]).astype(BF).astype(F32)
    gathered[...] = jnp.zeros_like(gathered)
    for tap in range(TAPS):
        start = margin + ((tap // 3 - 1) * PITCH + tap % 3 - 1) * img
        gathered[start : start + places, :] += dot_nt(canvas[...].astype(BF), weight[tap])
    canvas[...] = gathered[margin : margin + places, :]
    grad_pre[...] = dot(to_rows[...], canvas[...].astype(BF)).astype(BF)
    mean, scale, slope, offset = (first_coef[0, k : k + 1, :] for k in range(4))
    back = mean * scale

    def finish(ds, acc):
        values = first_pre[ds, :].astype(F32)
        act = values * slope + offset
        gate = sigmoid(act)
        local = grad_pre[ds, :].astype(F32) * mask[n, ds, :] * (gate * (1.0 + act * (1.0 - gate)))
        grad_first[ds, :] = local.astype(BF)
        return acc[0] + fold(local), acc[1] + fold(local * (values * scale - back))

    sums2 = by_rows(rows, finish, zeros_acc(grad.shape[1]))
    send_stats(message, column_sum(sums2[0]), column_sum(sums2[1]))


def first_backward(g0, g1, g2, g3, p0, p1, p2, p3, sum0, sum1, sum2, sum3, params, coef, mask, x, grad, weight,
                   grad_input, level_sum, tilt_sum, out, grad_pre, acc):
    n, z, y = position()
    rows, channels = g0.shape
    blocks = (sum0[...], sum1[...], sum2[...], sum3[...])
    every = blocks[0] + blocks[1] + blocks[2] + blocks[3]
    for m, (g, pre) in enumerate(((g0, p0), (g1, p1), (g2, p2), (g3, p3))):
        b = n ^ m
        block = blocks[m]
        mean, scale, slope = (coef[m, k : k + 1, :] for k in range(3))
        inverse = inverse_count(params, b, channels)
        level = wide_row(block, 0) * inverse
        tilt = wide_row(block, NARROW) * inverse
        level, tilt = level - mean * scale * tilt, scale * tilt

        def body(ds, carry):
            away = mask[b, ds, :] * (level + pre[ds, :].astype(F32) * tilt)
            grad_pre[m, ds, :] = (slope * (g[ds, :].astype(F32) - away)).astype(BF)
            return carry

        by_rows(rows, body, 0)
        product = dot_tn(x[b], grad_pre[m])
        if m == 0:
            acc[...] = product
        else:
            acc[...] += product
    if len(out.shape) == 2:
        out[...] = acc[...]
    else:
        half, cols = out.shape[1:]
        for place in range(out.shape[0]):
            top = pl.multiple_of((y ^ (place // NARROW)) * half, half)
            out[place] = acc[pl.ds(top, half), lane_block((z - place % NARROW) & 3)].astype(BF)
    for m in range(NARROW):
        grad_input[n ^ m] = dot_nt(grad_pre[m], weight[...]) + grad[m]
    level_sum[...] = row_of(every, 0, n)
    tilt_sum[...] = row_of(every, NARROW, n)


def last_weight(hidden, grad_pre, *refs):
    acc = refs[-1]
    for m in range(NARROW):
        product = dot_tn(hidden[m], grad_pre[m])
        if m == 0:
            acc[...] = product
        else:
            acc[...] += product
    hand_out(acc, refs[:-1])


def hand_out(acc, outs):
    if len(outs) == 1:
        outs[0][...] = acc[...]
        return
    _, z, y = position()
    own, away = outs
    rows = acc.shape[0] // 8
    for j in range(4):
        place = pl.ds(j * rows, rows)
        for ref, dy in ((own, 0), (away, 1)):
            top = ((z ^ j) * 2 + (y ^ dy)) * rows
            ref[place, :] = acc[pl.ds(pl.multiple_of(top, rows), rows), :].astype(ref.dtype)


def middle_weight(hidden, q0, q1, q2, q3, pre, sum0, sum1, sum2, sum3, norm, params, mask, to_canvas,
                  level_sum, tilt_sum, *refs):
    outs, (acc, shifted, canvas) = refs[:-3], refs[-3:]
    n = position()[0]
    places = to_canvas.shape[0]
    img = places // (SIDE * PITCH)
    margin = img * (PITCH + 1)
    canvas[0:margin, :] = jnp.zeros((margin, 128), F32)
    canvas[margin + places :, :] = jnp.zeros((margin, 128), F32)
    norms = norm[...]
    blocks = (sum0[...], sum1[...], sum2[...], sum3[...])
    every = blocks[0] + blocks[1] + blocks[2] + blocks[3]
    level_sum[...] = row_of(every, 0, n)
    tilt_sum[...] = row_of(every, NARROW, n)
    for m, piece in enumerate((q0, q1, q2, q3)):
        b = n ^ m
        inverse = inverse_count(params, b, 128)
        mean, scale, slope, _ = coefficients(
            norms[2 * m : 2 * m + 1], norms[2 * m + 1 : 2 * m + 2], inverse, params[n, 2:3, :], params[n, 3:4, :]
        )
        block = blocks[m]
        level = row_of(block, 0, n) * inverse
        tilt = row_of(block, NARROW, n) * inverse
        level, tilt = level - mean * scale * tilt, scale * tilt
        away = mask[b] * (level + pre[m].astype(F32) * tilt)
        grad_pre = (slope * (piece[...].astype(F32) - away)).astype(BF)
        canvas[margin : margin + places, :] = dot(to_canvas[...], grad_pre)
        for tap in range(TAPS):
            start = margin - ((tap // 3 - 1) * PITCH + tap % 3 - 1) * img
            shifted[:, 128 * tap : 128 * tap + 128] = canvas[start : start + places, :].astype(BF)
        product = dot_tn(hidden[m], shifted[...])
        if m == 0:
            acc[...] = product
        else:
            acc[...] += product
    hand_out(acc, outs)


def gather_middle(near, far, out):
    _, z, y = position()
    rows = out.shape[0] // 8
    for dy, stack in enumerate((near, far)):
        for j in range(4):
            here = pl.ds(pl.multiple_of(((z ^ j) * 2 + (y ^ dy)) * rows, rows), rows)
            for tap in range(TAPS):
                top = (j * TAPS + tap) * rows
                out[here, 128 * tap : 128 * tap + 128] = stack[top : top + rows, :]


def gather_last(*refs):
    pieces, out = refs[:-1], refs[-1]
    _, z, y = position()
    rows = out.shape[0] // 8
    for j, pair in enumerate(pieces):
        for dy in range(2):
            here = pl.ds(pl.multiple_of(((z ^ j) * 2 + (y ^ dy)) * rows, rows), rows)
            out[here, :] = pair[dy * rows : (dy + 1) * rows, :]


def add_tiles(*refs):
    total = refs[0][...]
    for ref in refs[1:-1]:
        total = total + ref[...]
    refs[-1][...] = total


def merge_wide(own, away, own_last, away_last, keep, keep_last, *sends):
    rows, middle = keep.shape
    keep[...] = own[0:rows, :] + away[0:rows, :].astype(F32)
    keep_last[...] = own_last[0:rows, :] + away_last[0:rows, :].astype(F32)
    for j, send in enumerate(sends):
        here = slice((j + 1) * rows, (j + 2) * rows)
        send[:, 0:middle] = (own[here, :] + away[here, :].astype(F32)).astype(BF)
        send[:, middle:] = (own_last[here, :] + away_last[here, :].astype(F32)).astype(BF)


def finish_wide(keep, keep_last, p1, p2, p3, out, out_last):
    middle = keep.shape[1]
    for tap in range(TAPS):
        here = slice(128 * tap, 128 * tap + 128)
        out[tap] = keep[:, here] + p1[:, here].astype(F32) + p2[:, here].astype(F32) + p3[:, here].astype(F32)
    out_last[...] = (
        keep_last[...] + p1[:, middle:].astype(F32) + p2[:, middle:].astype(F32) + p3[:, middle:].astype(F32)
    )


def swap_core(values):
    return lax.ppermute(values, "narrow", [(i, i ^ 1) for i in range(NARROW)])


def swap_chip(values):
    return lax.ppermute(values, "narrow", [(i, i ^ 2) for i in range(NARROW)])


def swap_wide(values, step, wide):
    return lax.ppermute(values, "wide", [(i, i ^ step) for i in range(wide)])


def after(value, *others):
    return lax.optimization_barrier((value, *others))[0]


def from_all(values, *others):
    far = swap_chip(values)
    if others:
        return values, swap_core(after(values, *others)), far, swap_core(after(far, *others))
    return values, swap_core(values), far, swap_core(far)


def add(*tiles):
    return run(add_tiles, tiles, [arr(tiles[0].shape, F32)])[0]


def sum_wide(values, wide, *beside):
    if wide == 8:
        values = add(after(values, *beside) if beside else values, swap_wide(values, 1, wide))
        if beside:
            return values, add(values, *(swap_wide(values, step, wide) for step in (2, 4, 6)))
        return add(values, *(swap_wide(values, step, wide) for step in (2, 4, 6)))
    step = 1
    while step < wide:
        values = add(values, swap_wide(values, step, wide))
        step *= 2
    return (values, values) if beside else values


def reduce_narrow(send_far, own_far, send_near, own_near, *others):
    got_far = swap_core(send_far)
    got_near = swap_core(send_near)
    joined = (own_far + got_far.astype(F32)).astype(BF)
    if others:
        joined = after(joined, *others)
    return (own_near, got_near, swap_chip(joined)), joined


def transposed_steps():
    steps = []
    for dy in range(2):
        for j in range(NARROW):
            pairs = []
            for k in range(NARROW):
                for z in range(4):
                    for y in range(2):
                        pairs.append((k * 8 + 2 * z + y, z * 8 + 2 * ((k + j) % 4) + (y ^ dy)))
            steps.append(pairs)
    return steps


def on_device(inputs, sides, w_first, w_middle, w_last, gain_first, shift_first, gain_middle, shift_middle,
              gain_last, shift_last, cotangent, *, wide):
    micro, rows, low = inputs.shape
    img = sides.shape[1]
    mid = w_last.shape[0] * wide
    cols = w_first.shape[1]
    places = img * SIDE * PITCH
    direct = wide == 8
    n = lax.axis_index("narrow")
    w = lax.axis_index("wide")

    spots = jnp.arange(rows, dtype=jnp.int32)
    spot_y, spot_x, spot_img = spots % 49 // 7, spots % 7, spots // 49
    limit = jnp.repeat(sides, 49, axis=1)
    mask = ((spot_y[None] < limit) & (spot_x[None] < limit)).astype(F32)[:, :, None]
    place = (spot_y * PITCH + spot_x) * img + spot_img
    to_canvas = (jnp.arange(places, dtype=jnp.int32)[:, None] == place[None, :]).astype(BF)
    to_rows = (place[:, None] == jnp.arange(places, dtype=jnp.int32)[None, :]).astype(BF)

    if direct:
        steps = transposed_steps()
        share = w_last.shape[0]
        first_pieces = [lax.ppermute(w_first, MESH, pairs) for pairs in steps]
    else:
        first_all = lax.all_gather(lax.all_gather(w_first, "narrow", axis=1, tiled=True), "wide", axis=0, tiled=True)
        first_pieces = [lax.dynamic_slice_in_dim(first_all, n * low, low, 0)]
        middle_slice = lax.all_gather(w_middle, "wide", axis=2, tiled=True)
        middle_slice = middle_slice.reshape(TAPS, mid, 128).transpose(1, 0, 2).reshape(mid, TAPS * 128)
        last_slice = lax.all_gather(w_last, "wide", axis=0, tiled=True)

    counts = jnp.sum((sides * sides).astype(F32), axis=1)
    small = jnp.concatenate(
        [jnp.stack([gain_first, shift_first, gain_middle, shift_middle]) * (1.0 / wide),
         jnp.broadcast_to(counts[:, None], (micro, 128))], axis=0
    )

    tile = arr((8, 128), F32)
    across = arr((8, low), F32)
    flat = arr((rows, mid), BF)
    flat32 = arr((rows, mid), F32)

    w_rows, send_far, own_far, send_near, own_near = run(
        first_product, (inputs, *first_pieces),
        [arr((low, mid), BF), flat, flat32, flat, flat32], flops=2 * micro * rows * low * mid,
    )
    joined, begun = reduce_narrow(send_far, own_far, send_near, own_near)
    if direct:
        flat_middle = after(w_middle.reshape(TAPS * share, 128), begun)
        middle_near = jnp.concatenate([flat_middle] + [swap_wide(flat_middle, 2 * j, wide) for j in range(1, 4)], axis=0)
        middle_far = swap_wide(middle_near, 1, wide)
        held = after(w_last, begun)
        last_pair = jnp.concatenate([held, swap_wide(held, 1, wide)], axis=0)
        last_pieces = [last_pair] + [swap_wide(last_pair, 2 * j, wide) for j in range(1, 4)]
        joined = (after(joined[0], middle_near, last_pair), *joined[1:])
    pre_one, message = run(first_join, (*joined, mask, small), [flat, arr((16, 128), F32)])
    total = sum_wide(message, wide)
    pre_ones = from_all(pre_one, total, *((middle_far,) if direct else ()))
    sums_one = from_all(total)
    if direct:
        middle_slice = run(gather_middle, (middle_near, middle_far), [arr((mid, TAPS * 128), BF)])[0]
        last_slice = run(gather_last, last_pieces, [arr((mid, low), BF)])[0]
        middle_slice = after(middle_slice, *last_pieces)

    hidden_one, pre_two, coef_one, message, params = run(
        middle_forward, (*pre_ones, *sums_one, mask, to_canvas, to_rows, middle_slice),
        [arr((micro, places, mid), BF), arr((micro, rows, 128), BF), arr((micro, 8, mid), F32), tile, arr((NARROW, 8, 128), F32)],
        [pltpu.VMEM((rows, mid), BF), pltpu.VMEM((places + 2 * img * (PITCH + 1), TAPS * 128), F32), pltpu.VMEM((places, 128), BF)],
        flops=2 * micro * places * mid * TAPS * 128,
    )
    total = sum_wide(message, wide)
    pre_twos = from_all(pre_two, total)
    sums_two = from_all(total)
    held = after(middle_slice, pre_twos[3], sums_two[3])
    middle_away = swap_chip(held)

    hidden_two, own_two, coef_two, pre_three, message = run(
        last_forward, (*pre_twos, *sums_two, params, mask, last_slice),
        [arr((micro, rows, mid), BF), flat, arr((8, mid), F32), arr((micro, rows, low), F32), across],
        flops=2 * micro * rows * low * mid,
    )
    parts_three = sum_wide(message, wide)
    block_out, grad_sum, coef_three, message = run(
        block_output,
        (pre_three, inputs, cotangent, parts_three, params, gain_last[None], shift_last[None], mask),
        [arr(inputs.shape, BF), arr((micro, rows, low), F32), arr((micro, 8, low), F32), across],
    )
    parts_four = sum_wide(message, wide)

    grad_three, send_far, own_far, send_near, own_near, level_three, tilt_three = run(
        last_backward, (pre_three, grad_sum, parts_four, params, coef_three, mask, last_slice),
        [arr((micro, rows, low), BF), flat, flat32, flat, flat32, arr((1, low), F32), arr((1, low), F32)],
        flops=2 * micro * rows * low * mid,
    )
    joined, _ = reduce_narrow(send_far, own_far, send_near, own_near, middle_away)

    def handed(channels):
        if direct:
            return [arr((mid // 2, channels), F32), arr((mid // 2, channels), BF)]
        return [arr((mid, channels), F32)]

    last_sum = run(
        last_weight, (hidden_two, grad_three), handed(low), [pltpu.VMEM((mid, low), F32)],
        flops=2 * micro * rows * low * mid,
    )
    slim = arr((rows, 128), BF)
    row = arr((1, 128), F32)
    if direct:
        got_last_sum = swap_wide(last_sum[1], 1, wide)
        joined = (after(joined[0], got_last_sum), *joined[1:])
    grad_two, own_q, near_q, far_q, last_q, message = run(
        middle_join, (*joined, own_two, coef_two, mask), [flat32, slim, slim, slim, slim, tile]
    )
    total_five = sum_wide(message, wide)
    got_far, got_last, got_near = swap_chip(far_q), swap_core(swap_chip(last_q)), swap_core(near_q)
    middle_slices = (middle_slice, swap_core(held), middle_away, swap_core(middle_away))
    sums_five = from_all(total_five)

    grad_one, message = run(
        middle_backward,
        (grad_two, own_two, total_five, params, coef_two, mask, pre_one, coef_one, to_canvas, to_rows, *middle_slices),
        [flat, tile],
        [pltpu.VMEM((rows, mid), BF), pltpu.VMEM((TAPS, mid, mid), BF),
         pltpu.VMEM((places + 2 * img * (PITCH + 1), mid), F32), pltpu.VMEM((places, mid), F32)],
        flops=2 * places * mid * TAPS * mid,
    )
    level_two, tilt_two, *middle_sum = run(
        middle_weight,
        (hidden_one, own_q, got_near, got_far, got_last, pre_two, *sums_five, sums_two[0], params, mask, to_canvas),
        [row, row, *handed(TAPS * 128)],
        [pltpu.VMEM((mid, TAPS * 128), F32), pltpu.VMEM((places, TAPS * 128), BF),
         pltpu.VMEM((places + 2 * img * (PITCH + 1), 128), F32)],
        flops=2 * micro * places * mid * TAPS * 128,
    )
    begun, total = sum_wide(message, wide, *middle_sum)
    grad_ones = from_all(after(grad_one, sums_five[2]), total)
    sums_six = from_all(total)
    if direct:
        got_middle = swap_wide(after(middle_sum[1], begun), 1, wide)

    out_first = arr((8, 2 * low // NARROW, cols), BF) if direct else arr((low, mid), F32)
    input_grad, level_one, tilt_one, first_sum = run(
        first_backward,
        (*grad_ones, *pre_ones, *sums_six, params, coef_one, mask, inputs, grad_sum, w_rows),
        [arr((micro, rows, low), F32), row, row, out_first],
        [pltpu.VMEM((micro, rows, mid), BF), pltpu.VMEM((low, mid), F32)],
        flops=4 * micro * rows * low * mid,
    )

    if direct:
        arrived = [
            lax.ppermute(first_sum[k], MESH, [(dst, src) for src, dst in pairs]) for k, pairs in enumerate(steps)
        ]
        channels = TAPS * 128
        keep, keep_last, *sends = run(
            merge_wide, (middle_sum[0], after(got_middle, first_sum), last_sum[0], got_last_sum),
            [arr((share, channels), F32), arr((share, low), F32)] + [arr((share, channels + low), BF)] * 3,
        )
        parts = [swap_wide(send, 2 * j + 2, wide) for j, send in enumerate(sends)]
        grad_middle, grad_last = run(
            finish_wide, (after(keep, arrived[0]), keep_last, *parts),
            [arr((TAPS, share, 128), F32), arr((share, low), F32)],
        )
        grad_middle = grad_middle.reshape(3, 3, share, 128)
        grad_first = arrived[0].astype(F32)
        for piece in arrived[1:]:
            grad_first = grad_first + piece.astype(F32)
    else:
        grad_last = lax.psum_scatter(last_sum[0], "wide", scatter_dimension=0, tiled=True)
        grad_middle = lax.psum_scatter(middle_sum[0], "wide", scatter_dimension=0, tiled=True)
        share = grad_middle.shape[0]
        grad_middle = grad_middle.reshape(share, TAPS, 128).transpose(1, 0, 2).reshape(3, 3, share, 128)
        whole = lax.psum(first_sum, "wide")
        whole = lax.all_gather(whole, "narrow", axis=0, tiled=True)
        share = whole.shape[0] // wide
        grad_first = lax.dynamic_slice(whole, (w * share, n * cols), (share, cols))
    return (
        block_out, input_grad, grad_first, grad_middle, grad_last,
        tilt_one[0], level_one[0], tilt_two[0], level_two[0], tilt_three[0], level_three[0],
    )


def solution(mesh):
    wide = mesh.shape["wide"]
    placed = (
        P(None, "wide", "narrow"),
        P(None, "wide"),
        P("wide", "narrow"),
        P(None, None, "wide", "narrow"),
        P("wide", "narrow"),
        P("narrow"),
        P("narrow"),
        P("narrow"),
        P("narrow"),
        P("narrow"),
        P("narrow"),
        P(None, "wide", "narrow"),
    )
    return jax.shard_map(
        lambda *arrays: on_device(*arrays, wide=wide),
        mesh=mesh,
        in_specs=placed,
        out_specs=(
            P(None, "wide", "narrow"),
            P(None, "wide", "narrow"),
            P("wide", "narrow"),
            P(None, None, "wide", "narrow"),
            P("wide", "narrow"),
            P("narrow"),
            P("narrow"),
            P("narrow"),
            P("narrow"),
            P("narrow"),
            P("narrow"),
        ),
        check_vma=False,
    )
```

time: 346 us -> 248 us (0.72)
  Pallas kernels: 109 us -> 31.7 us
  local copies, waits for them, and re-layouts: 35.7 us -> 3.03 us
  starting transfers between devices: 79.6 us -> 106 us
  blocking collectives: 19.9 us -> 0 us
  waiting for transfers between devices: 89 us -> 101 us
  other arithmetic: 10.1 us -> 3.5 us
    pallas_call x12 -> x27, Pallas kernels: 109 us -> 31.7 us  [run(): pl.pallas_call(kernel, out_shape=outs, name=kernel.__name__, in_specs=[pl...]
    ppermute x12 -> x37, waiting for transfers between devices: 32.6 us -> 74.6 us  [swap_wide(): return lax.ppermute(values, 'wide', [(i, i ^ step) for i in range(wide)])]
    ppermute x12 -> x37, starting transfers between devices: 17.9 us -> 50.8 us  [swap_wide(): return lax.ppermute(values, 'wide', [(i, i ^ step) for i in range(wide)])]
    unnamed x98 -> x28, local copies, waits for them, and re-layouts: 28.1 us -> 1.53 us
    all_to_all x2 -> x0, blocking collectives: 19.9 us -> none  [exchange(): return lax.all_to_all(message, axes, 0, 0, tiled=True)]
    ppermute x7 -> x12, waiting for transfers between devices: 35.7 us -> 17.7 us  [swap_chip(): return lax.ppermute(values, 'narrow', [(i, i ^ 2) for i in range(NARROW)])]
    all_to_all x5 -> x0, starting transfers between devices: 18 us -> none  [exchange(): return lax.all_to_all(message, axes, 0, 0, tiled=True)]
    all_to_all x5 -> x0, waiting for transfers between devices: 11.1 us -> none  [exchange(): return lax.all_to_all(message, axes, 0, 0, tiled=True)]
  transfers between devices with their start and end apart: 54 -> 87, of which waited for: 18 -> 36; matrix products, arithmetic and copies ran while one was open for 5% -> 2% of each run, Pallas kernels for 25% -> 10%
where the time goes in v2:
time: 248 us; the launch traced here: 246 us
  starting transfers between devices  106 us (43%)
  waiting for transfers between devices  101 us (41%)
  Pallas kernels  31.7 us (13%)
  other arithmetic  3.5 us (1%)
  local copies, waits for them, and re-layouts  3.03 us (1%)
    ppermute x37, waiting for transfers between devices, swap_wide(): return lax.ppermute(values, 'wide', [(i, i ^ step) for i in range(wide)])  74.6 us
    ppermute x37, starting transfers between devices, swap_wide(): return lax.ppermute(values, 'wide', [(i, i ^ step) for i in range(wide)])  50.8 us
    pallas_call x27, Pallas kernels, run(): pl.pallas_call(kernel, out_shape=outs, name=kernel.__name__, in_specs=[pl...  31.7 us
    ppermute x8, starting transfers between devices, on_device(): first_pieces = [lax.ppermute(w_first, MESH, pairs) for pairs in steps]  19 us
    ppermute x12, waiting for transfers between devices, swap_chip(): return lax.ppermute(values, 'narrow', [(i, i ^ 2) for i in range(NARROW)])  17.7 us
    ppermute x12, starting transfers between devices, swap_chip(): return lax.ppermute(values, 'narrow', [(i, i ^ 2) for i in range(NARROW)])  16.7 us
    ppermute x8, starting transfers between devices, on_device(): lax.ppermute(first_sum[k], MESH, [(dst, src) for src, dst in pairs])  14.6 us
    ppermute x22, waiting for transfers between devices, swap_core(): return lax.ppermute(values, 'narrow', [(i, i ^ 1) for i in range(NARROW)])  6.49 us
  transfers between devices with their start and end apart: 87, of which 36 were waited for; matrix products, arithmetic and copies ran while one was open for 2% of the time, Pallas kernels for 10%

profile of v2, /device:TPU:0, one launch (start us, length us, event | category | flops | bytes accessed | tf_op | source)
XLA Modules:
  0.0 246.0 jit_solution(1281326281420037434)
XLA Ops:
  2.3 3.5 %collective-permute-start.1 = (bf16[256,128]{1,0:T(8,128)(2,1)}, bf16[256,128]{1,0:T(8,128)(2,1)S(1)}, u32[]{:S(2)}, u32[]{:S(2)}) collective-permute-start(bf16[256,128]{1,0:T(8,128)(2,1)} %param.14), channel_id=1, source_target_pairs={{0,2},{1,3},{2,10},{3,11},{4,18},{5,19},{6,26},{7,27},{8,4},{9,5},... | collective-permute-start | bytes 196616 | tf_op jit(solution)/shard_map/ppermute | solution.py:587
  5.8 3.4 %collective-permute-start.2 = (bf16[256,128]{1,0:T(8,128)(2,1)}, bf16[256,128]{1,0:T(8,128)(2,1)S(1)}, u32[]{:S(2)}, u32[]{:S(2)}) collective-permute-start(bf16[256,128]{1,0:T(8,128)(2,1)} %param.14), channel_id=1, source_target_pairs={{0,4},{1,5},{2,12},{3,13},{4,20},{5,21},{6,28},{7,29},{8,6},{9,7},... | collective-permute-start | bytes 196616 | tf_op jit(solution)/shard_map/ppermute | solution.py:587
  16.8 3.0 %collective-permute-start.7 = (bf16[256,128]{1,0:T(8,128)(2,1)}, bf16[256,128]{1,0:T(8,128)(2,1)S(1)}, u32[]{:S(2)}, u32[]{:S(2)}) collective-permute-start(bf16[256,128]{1,0:T(8,128)(2,1)} %param.14), channel_id=1, source_target_pairs={{0,7},{1,6},{2,15},{3,14},{4,23},{5,22},{6,31},{7,30},{8,1},{9,0},... | collective-permute-start | bytes 196616 | tf_op jit(solution)/shard_map/ppermute | solution.py:587
  29.3 4.2 %collective-permute-start.10 = (bf16[576,128]{1,0:T(8,128)(2,1)S(1)}, bf16[576,128]{1,0:T(8,128)(2,1)S(1)}, u32[]{:S(2)}, u32[]{:S(2)}) collective-permute-start(bf16[576,128]{1,0:T(8,128)(2,1)S(1)} %bitcast.33), channel_id=1, source_target_pairs={{0,4},{1,5},{2,6},{3,7},{4,0},{5,1},{6,2},{7,3},{8,12},{9,13},{10,... | collective-permute-start | bytes 442376 | tf_op jit(solution)/shard_map/ppermute | solution.py:512
  37.9 6.6 %collective-permute-done.10 = bf16[576,128]{1,0:T(8,128)(2,1)S(1)} collective-permute-done((bf16[576,128]{1,0:T(8,128)(2,1)S(1)}, bf16[576,128]{1,0:T(8,128)(2,1)S(1)}, u32[]{:S(2)}, u32[]{:S(2)}) %collective-permute-start.10) | collective-permute-done | bytes 147488 | tf_op jit(solution)/shard_map/ppermute | solution.py:512
  48.8 10.8 %collective-permute-done.15.refs_1_ = f32[16,128]{1,0:T(8,128)S(1)} collective-permute-done((f32[16,128]{1,0:T(8,128)S(1)}, f32[16,128]{1,0:T(8,128)S(1)}, u32[]{:S(2)}, u32[]{:S(2)}) %collective-permute-start.15) | collective-permute-done | bytes 8224 | tf_op jit(solution)/shard_map/ppermute | solution.py:512
  59.6 3.7 %collective-permute-start.16 = (f32[16,128]{1,0:T(8,128)S(1)}, f32[16,128]{1,0:T(8,128)S(1)}, u32[]{:S(2)}, u32[]{:S(2)}) collective-permute-start(f32[16,128]{1,0:T(8,128)S(1)} %add_tiles.12.refs_0_), channel_id=1, source_target_pairs={{0,2},{1,3},{2,0},{3,1},{4,6},{5,7},{6,4},{7,5},{8,10},{9,11},{10,... | collective-permute-start | bytes 24584 | tf_op jit(solution)/shard_map/ppermute | solution.py:512
  75.4 3.5 %collective-permute-done.28.refs_3_ = bf16[128,512]{1,0:T(8,128)(2,1)S(1)} collective-permute-done((bf16[128,512]{1,0:T(8,128)(2,1)S(1)}, bf16[128,512]{1,0:T(8,128)(2,1)S(1)}, u32[]{:S(2)}, u32[]{:S(2)}) %collective-permute-start.28) | collective-permute-done | bytes 131104 | tf_op jit(solution)/shard_map/ppermute | solution.py:512
  78.9 5.6 %middle_forward.1 = (bf16[4,448,512]{2,1,0:T(8,128)(2,1)S(1)}, bf16[4,392,128]{2,1,0:T(8,128)(2,1)S(1)}, f32[4,8,512]{2,1,0:T(8,128)S(1)}, f32[8,128]{1,0:T(8,128)S(1)}, f32[4,8,128]{2,1,0:T(8,128)S(1)}) custom-call(bf16[392,512]{1,0:T(8,128)(2,1)S(1)} %get-tuple-element.91.pre0.first_pre.p0, bf16[392,512]{1,0:T(8,128)(2,1)S(1)} %collective-permute-done.20.pre1.p1, ...), custom_call_target="tpu_custom_call" | custom-call | flops 2113929216 | bytes 5849216 | tf_op jit(solution)/shard_map/middle_forward/pallas_call | solution.py:39
  86.5 3.2 %collective-permute-done.29.refs_1_ = f32[8,128]{1,0:T(8,128)S(1)} collective-permute-done((f32[8,128]{1,0:T(8,128)S(1)}, f32[8,128]{1,0:T(8,128)S(1)}, u32[]{:S(2)}, u32[]{:S(2)}) %collective-permute-start.29) | collective-permute-done | bytes 4128 | tf_op jit(solution)/shard_map/ppermute | solution.py:512
  107.8 3.5 %collective-permute-done.39.refs_1_ = f32[8,512]{1,0:T(8,128)S(1)} collective-permute-done((f32[8,512]{1,0:T(8,128)S(1)}, f32[8,512]{1,0:T(8,128)S(1)}, u32[]{:S(2)}, u32[]{:S(2)}) %collective-permute-start.39) | collective-permute-done | bytes 16416 | tf_op jit(solution)/shard_map/ppermute | solution.py:512
  118.9 3.6 %block_output.1 = (bf16[4,392,512]{2,1,0:T(8,128)(2,1)}, f32[4,392,512]{2,1,0:T(8,128)S(1)}, f32[4,8,512]{2,1,0:T(8,128)S(1)}, f32[8,512]{1,0:T(8,128)S(1)}) custom-call(f32[4,392,512]{2,1,0:T(8,128)S(1)} %get-tuple-element.99.pre, bf16[4,392,512]{2,1,0:T(8,128)(2,1)S(1)} %copy-done.1, bf16[4,392,512]{2,1,0:T(8,128)(2,1)S(1)} %copy-done.2, ...), custom_call_target="tpu_custom_call" | custom-call | bytes 11364480 | tf_op jit(solution)/shard_map/block_output/pallas_call | solution.py:39
  123.0 6.9 %collective-permute-done.50.w2 = bf16[512,1152]{1,0:T(8,128)(2,1)S(1)} collective-permute-done((bf16[512,1152]{1,0:T(8,128)(2,1)S(1)}, bf16[512,1152]{1,0:T(8,128)(2,1)S(1)}, u32[]{:S(2)}, u32[]{:S(2)}) %collective-permute-start.50) | collective-permute-done | bytes 1179680 | tf_op jit(solution)/shard_map/ppermute | solution.py:508
  130.2 3.0 %collective-permute-start.45 = (f32[8,512]{1,0:T(8,128)S(1)}, f32[8,512]{1,0:T(8,128)S(1)}, u32[]{:S(2)}, u32[]{:S(2)}) collective-permute-start(f32[8,512]{1,0:T(8,128)S(1)} %add_tiles.18.refs_0_), channel_id=1, source_target_pairs={{0,4},{1,5},{2,6},{3,7},{4,0},{5,1},{6,2},{7,3},{8,12},{9,13},{10,... | collective-permute-start | bytes 49160 | tf_op jit(solution)/shard_map/ppermute | solution.py:512
  134.9 3.8 %collective-permute-done.46.refs_3_ = f32[8,512]{1,0:T(8,128)S(1)} collective-permute-done((f32[8,512]{1,0:T(8,128)S(1)}, f32[8,512]{1,0:T(8,128)S(1)}, u32[]{:S(2)}, u32[]{:S(2)}) %collective-permute-start.46) | collective-permute-done | bytes 16416 | tf_op jit(solution)/shard_map/ppermute | solution.py:512
  145.1 7.5 %collective-permute-done.47.away_last = bf16[256,512]{1,0:T(8,128)(2,1)S(1)} collective-permute-done((bf16[256,512]{1,0:T(8,128)(2,1)S(1)}, bf16[256,512]{1,0:T(8,128)(2,1)S(1)}, u32[]{:S(2)}, u32[]{:S(2)}) %collective-permute-start.47) | collective-permute-done | bytes 262176 | tf_op jit(solution)/shard_map/ppermute | solution.py:512
  155.1 3.2 %collective-permute-done.52.refs_1_ = f32[8,128]{1,0:T(8,128)S(1)} collective-permute-done((f32[8,128]{1,0:T(8,128)S(1)}, f32[8,128]{1,0:T(8,128)S(1)}, u32[]{:S(2)}, u32[]{:S(2)}) %collective-permute-start.52) | collective-permute-done | bytes 4128 | tf_op jit(solution)/shard_map/ppermute | solution.py:512
  167.3 4.1 %middle_backward.1 = (bf16[392,512]{1,0:T(8,128)(2,1)S(1)}, f32[8,128]{1,0:T(8,128)S(1)}) custom-call(f32[392,512]{1,0:T(8,128)S(1)} %get-tuple-element.117.grad, bf16[392,512]{1,0:T(8,128)(2,1)S(1)} %get-tuple-element.115.pre, f32[8,128]{1,0:T(8,128)S(1)} %add_tiles.21.parts.sum0, f32[4,8,128]{2,1,0:T(8,128)S(1)} %get-tuple-element.98.params, ...), custom_call_target="tpu_custom_call" | custom-call | flops 2113929216 | bytes 7540864 | tf_op jit(solution)/shard_map/middle_backward/pallas_call | solution.py:39
  176.4 5.1 %collective-permute-done.60.q2 = bf16[392,128]{1,0:T(8,128)(2,1)S(1)} collective-permute-done((bf16[392,128]{1,0:T(8,128)(2,1)S(1)}, bf16[392,128]{1,0:T(8,128)(2,1)S(1)}, u32[]{:S(2)}, u32[]{:S(2)}) %collective-permute-start.60) | collective-permute-done | bytes 100384 | tf_op jit(solution)/shard_map/ppermute | solution.py:508
  181.4 5.2 %middle_weight.1 = (f32[1,128]{1,0:T(1,128)}, f32[1,128]{1,0:T(1,128)}, f32[256,1152]{1,0:T(8,128)S(1)}, bf16[256,1152]{1,0:T(8,128)(2,1)S(1)}) custom-call(bf16[4,448,512]{2,1,0:T(8,128)(2,1)S(1)} %get-tuple-element.123.hidden, bf16[392,128]{1,0:T(8,128)(2,1)S(1)} %get-tuple-element.124.q0, bf16[392,128]{1,0:T(8,128)(2,1)S(1)} %collective-permute-done.59.q1, ...), custom_call_target="tpu_custom_call" | custom-call | flops 2113929216 | bytes 4802688 | tf_op jit(solution)/shard_map/middle_weight/pallas_call | solution.py:39
  200.0 4.3 %first_backward.1 = (f32[4,392,512]{2,1,0:T(8,128)}, f32[1,128]{1,0:T(1,128)}, f32[1,128]{1,0:T(1,128)}, bf16[8,256,128]{2,1,0:T(8,128)(2,1)S(1)}) custom-call(bf16[392,512]{1,0:T(8,128)(2,1)S(1)} %get-tuple-element.131.g0, bf16[392,512]{1,0:T(8,128)(2,1)S(1)} %collective-permute-done.69.g1, bf16[392,512]{1,0:T(8,128)(2,1)S(1)} %collective-permute-done.70.g2, ...), custom_call_target="tpu_custom_call" | custom-call | flops 1644167168 | bytes 12393600 | tf_op jit(solution)/shard_map/first_backward/pallas_call | solution.py:39
  207.5 4.7 %collective-permute-start.80 = (bf16[256,128]{1,0:T(8,128)(2,1)S(1)}, bf16[256,128]{1,0:T(8,128)(2,1)S(1)}, u32[]{:S(2)}, u32[]{:S(2)}) collective-permute-start(bf16[256,128]{1,0:T(8,128)(2,1)S(1)} %get-tuple-element.156), channel_id=1, source_target_pairs={{3,0},{2,1},{11,2},{10,3},{19,4},{18,5},{27,6},{26,7},{5,8},{4,9},... | collective-permute-start | bytes 196616 | tf_op jit(solution)/shard_map/ppermute | solution.py:715
  220.9 8.5 %collective-permute-start.85 = (bf16[64,1664]{1,0:T(8,128)(2,1)S(1)}, bf16[64,1664]{1,0:T(8,128)(2,1)S(1)}, u32[]{:S(2)}, u32[]{:S(2)}) collective-permute-start(bf16[64,1664]{1,0:T(8,128)(2,1)S(1)} %get-tuple-element.143), channel_id=1, source_target_pairs={{0,4},{1,5},{2,6},{3,7},{4,0},{5,1},{6,2},{7,3},{8,12},{9,13},{10,... | collective-permute-start | bytes 638984 | tf_op jit(solution)/shard_map/ppermute | solution.py:512
  230.2 15.1 %collective-permute-done.85.p2 = bf16[64,1664]{1,0:T(8,128)(2,1)S(1)} collective-permute-done((bf16[64,1664]{1,0:T(8,128)(2,1)S(1)}, bf16[64,1664]{1,0:T(8,128)(2,1)S(1)}, u32[]{:S(2)}, u32[]{:S(2)}) %collective-permute-start.85) | collective-permute-done | bytes 213024 | tf_op jit(solution)/shard_map/ppermute | solution.py:512
  (222 shorter events, 118.9 us)
Async XLA Ops:
  0.7 12.7 %collective-permute-start = (bf16[256,128]{1,0:T(8,128)(2,1)}, bf16[256,128]{1,0:T(8,128)(2,1)S(1)}, u32[]{:S(2)}, u32[]{:S(2)}) collective-permute-start(bf16[256,128]{1,0:T(8,128)(2,1)} %param.14), channel_id=1, source_target_pairs={{0,0},{1,1},{2,8},{3,9},{4,16},{5,17},{6,24},{7,25},{8,2},{9,3},{1... | collective-permute-start | bytes 196616 | tf_op jit(solution)/shard_map/ppermute | solution.py:587
  2.3 11.5 %collective-permute-start.1 = (bf16[256,128]{1,0:T(8,128)(2,1)}, bf16[256,128]{1,0:T(8,128)(2,1)S(1)}, u32[]{:S(2)}, u32[]{:S(2)}) collective-permute-start(bf16[256,128]{1,0:T(8,128)(2,1)} %param.14), channel_id=1, source_target_pairs={{0,2},{1,3},{2,10},{3,11},{4,18},{5,19},{6,26},{7,27},{8,4},{9,5},... | collective-permute-start | bytes 196616 | tf_op jit(solution)/shard_map/ppermute | solution.py:587
  9.2 11.3 %collective-permute-start.3 = (bf16[256,128]{1,0:T(8,128)(2,1)}, bf16[256,128]{1,0:T(8,128)(2,1)S(1)}, u32[]{:S(2)}, u32[]{:S(2)}) collective-permute-start(bf16[256,128]{1,0:T(8,128)(2,1)} %param.14), channel_id=1, source_target_pairs={{0,6},{1,7},{2,14},{3,15},{4,22},{5,23},{6,30},{7,31},{8,0},{9,1},... | collective-permute-start | bytes 196616 | tf_op jit(solution)/shard_map/ppermute | solution.py:587
  29.2 15.9 %collective-permute-start.13 = (bf16[392,512]{1,0:T(8,128)(2,1)S(1)}, bf16[392,512]{1,0:T(8,128)(2,1)S(1)}, u32[]{:S(2)}, u32[]{:S(2)}) collective-permute-start(bf16[392,512]{1,0:T(8,128)(2,1)S(1)} %get-tuple-element.88), channel_id=1, source_target_pairs={{0,8},{8,0},{16,24},{24,16},{1,9},{9,1},{17,25},{25,17},{2,10},{10... | collective-permute-start | bytes 1204232 | tf_op jit(solution)/shard_map/ppermute | solution.py:504
  29.3 15.2 %collective-permute-start.10 = (bf16[576,128]{1,0:T(8,128)(2,1)S(1)}, bf16[576,128]{1,0:T(8,128)(2,1)S(1)}, u32[]{:S(2)}, u32[]{:S(2)}) collective-permute-start(bf16[576,128]{1,0:T(8,128)(2,1)S(1)} %bitcast.33), channel_id=1, source_target_pairs={{0,4},{1,5},{2,6},{3,7},{4,0},{5,1},{6,2},{7,3},{8,12},{9,13},{10,... | collective-permute-start | bytes 442376 | tf_op jit(solution)/shard_map/ppermute | solution.py:512
  33.5 11.0 %collective-permute-start.11 = (bf16[576,128]{1,0:T(8,128)(2,1)S(1)}, bf16[576,128]{1,0:T(8,128)(2,1)S(1)}, u32[]{:S(2)}, u32[]{:S(2)}) collective-permute-start(bf16[576,128]{1,0:T(8,128)(2,1)S(1)} %bitcast.35), channel_id=1, source_target_pairs={{0,6},{1,7},{2,4},{3,5},{4,2},{5,3},{6,0},{7,1},{8,14},{9,15},{10,... | collective-permute-start | bytes 442376 | tf_op jit(solution)/shard_map/ppermute | solution.py:512
  33.7 11.5 %collective-permute-start.14 = (bf16[392,512]{1,0:T(8,128)(2,1)S(1)}, bf16[392,512]{1,0:T(8,128)(2,1)S(1)}, u32[]{:S(2)}, u32[]{:S(2)}) collective-permute-start(bf16[392,512]{1,0:T(8,128)(2,1)S(1)} %add_convert_fusion.1), channel_id=1, source_target_pairs={{0,16},{8,24},{16,0},{24,8},{1,17},{9,25},{17,1},{25,9},{2,18},{10... | collective-permute-start | bytes 1204232 | tf_op jit(solution)/shard_map/ppermute | solution.py:508
  44.6 25.7 %collective-permute-start.19 = (bf16[2304,128]{1,0:T(8,128)(2,1)S(1)}, bf16[2304,128]{1,0:T(8,128)(2,1)S(1)}, u32[]{:S(2)}, u32[]{:S(2)}) collective-permute-start(bf16[2304,128]{1,0:T(8,128)(2,1)S(1)} %constant_dynamic-update-slice_fusion.near), channel_id=1, source_target_pairs={{0,1},{1,0},{2,3},{3,2},{4,5},{5,4},{6,7},{7,6},{8,9},{9,8},{10,11... | collective-permute-start | bytes 1769480 | tf_op jit(solution)/shard_map/ppermute | solution.py:512
  45.4 24.9 %collective-permute-start.21 = (bf16[392,512]{1,0:T(8,128)(2,1)S(1)}, bf16[392,512]{1,0:T(8,128)(2,1)S(1)}, u32[]{:S(2)}, u32[]{:S(2)}) collective-permute-start(bf16[392,512]{1,0:T(8,128)(2,1)S(1)} %get-tuple-element.91.pre0.first_pre.p0), channel_id=1, source_target_pairs={{0,16},{8,24},{16,0},{24,8},{1,17},{9,25},{17,1},{25,9},{2,18},{10... | collective-permute-start | bytes 1204232 | tf_op jit(solution)/shard_map/ppermute | solution.py:508
  47.5 12.1 %collective-permute-start.15 = (f32[16,128]{1,0:T(8,128)S(1)}, f32[16,128]{1,0:T(8,128)S(1)}, u32[]{:S(2)}, u32[]{:S(2)}) collective-permute-start(f32[16,128]{1,0:T(8,128)S(1)} %get-tuple-element.90.refs_0_), channel_id=1, source_target_pairs={{0,1},{1,0},{2,3},{3,2},{4,5},{5,4},{6,7},{7,6},{8,9},{9,8},{10,11... | collective-permute-start | bytes 24584 | tf_op jit(solution)/shard_map/ppermute | solution.py:512
  84.6 12.4 %collective-permute-start.34 = (bf16[4,392,128]{2,1,0:T(8,128)(2,1)S(1)}, bf16[4,392,128]{2,1,0:T(8,128)(2,1)S(1)}, u32[]{:S(2)}, u32[]{:S(2)}) collective-permute-start(bf16[4,392,128]{2,1,0:T(8,128)(2,1)S(1)} %get-tuple-element.96.src0.pre), channel_id=1, source_target_pairs={{0,16},{8,24},{16,0},{24,8},{1,17},{9,25},{17,1},{25,9},{2,18},{10... | collective-permute-start | bytes 1204232 | tf_op jit(solution)/shard_map/ppermute | solution.py:508
  101.9 28.0 %collective-permute-start.50 = (bf16[512,1152]{1,0:T(8,128)(2,1)S(1)}, bf16[512,1152]{1,0:T(8,128)(2,1)S(1)}, u32[]{:S(2)}, u32[]{:S(2)}) collective-permute-start(bf16[512,1152]{1,0:T(8,128)(2,1)S(1)} %gather_middle.1.weight.w0), channel_id=1, source_target_pairs={{0,16},{8,24},{16,0},{24,8},{1,17},{9,25},{17,1},{25,9},{2,18},{10... | collective-permute-start | bytes 3538952 | tf_op jit(solution)/shard_map/ppermute | solution.py:508
  123.0 44.2 %collective-permute-start.56 = (bf16[512,1152]{1,0:T(8,128)(2,1)S(1)}, bf16[512,1152]{1,0:T(8,128)(2,1)S(1)}, u32[]{:S(2)}, u32[]{:S(2)}) collective-permute-start(bf16[512,1152]{1,0:T(8,128)(2,1)S(1)} %gather_middle.1.weight.w0), channel_id=1, source_target_pairs={{0,8},{8,0},{16,24},{24,16},{1,9},{9,1},{17,25},{25,17},{2,10},{10... | collective-permute-start | bytes 3538952 | tf_op jit(solution)/shard_map/ppermute | solution.py:504
  130.0 37.3 %collective-permute-start.57 = (bf16[512,1152]{1,0:T(8,128)(2,1)S(1)}, bf16[512,1152]{1,0:T(8,128)(2,1)S(1)}, u32[]{:S(2)}, u32[]{:S(2)}) collective-permute-start(bf16[512,1152]{1,0:T(8,128)(2,1)S(1)} %collective-permute-done.50.w2), channel_id=1, source_target_pairs={{0,8},{8,0},{16,24},{24,16},{1,9},{9,1},{17,25},{25,17},{2,10},{10... | collective-permute-start | bytes 3538952 | tf_op jit(solution)/shard_map/ppermute | solution.py:504
  140.7 11.9 %collective-permute-start.48 = (bf16[392,512]{1,0:T(8,128)(2,1)S(1)}, bf16[392,512]{1,0:T(8,128)(2,1)S(1)}, u32[]{:S(2)}, u32[]{:S(2)}) collective-permute-start(bf16[392,512]{1,0:T(8,128)(2,1)S(1)} %get-tuple-element.110), channel_id=1, source_target_pairs={{0,8},{8,0},{16,24},{24,16},{1,9},{9,1},{17,25},{25,17},{2,10},{10... | collective-permute-start | bytes 1204232 | tf_op jit(solution)/shard_map/ppermute | solution.py:504
  142.6 11.4 %collective-permute-start.51 = (bf16[392,512]{1,0:T(8,128)(2,1)S(1)}, bf16[392,512]{1,0:T(8,128)(2,1)S(1)}, u32[]{:S(2)}, u32[]{:S(2)}) collective-permute-start(bf16[392,512]{1,0:T(8,128)(2,1)S(1)} %add_convert_fusion), channel_id=1, source_target_pairs={{0,16},{8,24},{16,0},{24,8},{1,17},{9,25},{17,1},{25,9},{2,18},{10... | collective-permute-start | bytes 1204232 | tf_op jit(solution)/shard_map/ppermute | solution.py:508
  171.4 22.8 %collective-permute-start.70 = (bf16[392,512]{1,0:T(8,128)(2,1)S(1)}, bf16[392,512]{1,0:T(8,128)(2,1)S(1)}, u32[]{:S(2)}, u32[]{:S(2)}) collective-permute-start(bf16[392,512]{1,0:T(8,128)(2,1)S(1)} %get-tuple-element.131.g0), channel_id=1, source_target_pairs={{0,16},{8,24},{16,0},{24,8},{1,17},{9,25},{17,1},{25,9},{2,18},{10... | collective-permute-start | bytes 1204232 | tf_op jit(solution)/shard_map/ppermute | solution.py:508
  194.7 17.6 %collective-permute-start.83 = (bf16[256,1152]{1,0:T(8,128)(2,1)S(1)}, bf16[256,1152]{1,0:T(8,128)(2,1)S(1)}, u32[]{:S(2)}, u32[]{:S(2)}) collective-permute-start(bf16[256,1152]{1,0:T(8,128)(2,1)S(1)} %get-tuple-element.136), channel_id=1, source_target_pairs={{0,1},{1,0},{2,3},{3,2},{4,5},{5,4},{6,7},{7,6},{8,9},{9,8},{10,11... | collective-permute-start | bytes 1769480 | tf_op jit(solution)/shard_map/ppermute | solution.py:512
  207.5 11.9 %collective-permute-start.80 = (bf16[256,128]{1,0:T(8,128)(2,1)S(1)}, bf16[256,128]{1,0:T(8,128)(2,1)S(1)}, u32[]{:S(2)}, u32[]{:S(2)}) collective-permute-start(bf16[256,128]{1,0:T(8,128)(2,1)S(1)} %get-tuple-element.156), channel_id=1, source_target_pairs={{3,0},{2,1},{11,2},{10,3},{19,4},{18,5},{27,6},{26,7},{5,8},{4,9},... | collective-permute-start | bytes 196616 | tf_op jit(solution)/shard_map/ppermute | solution.py:715
  213.7 15.6 %collective-permute-start.78 = (bf16[256,128]{1,0:T(8,128)(2,1)S(1)}, bf16[256,128]{1,0:T(8,128)(2,1)S(1)}, u32[]{:S(2)}, u32[]{:S(2)}) collective-permute-start(bf16[256,128]{1,0:T(8,128)(2,1)S(1)} %get-tuple-element.158), channel_id=1, source_target_pairs={{6,0},{7,1},{14,2},{15,3},{22,4},{23,5},{30,6},{31,7},{0,8},{1,9},... | collective-permute-start | bytes 196616 | tf_op jit(solution)/shard_map/ppermute | solution.py:715
  214.0 15.5 %collective-permute-start.77 = (bf16[256,128]{1,0:T(8,128)(2,1)S(1)}, bf16[256,128]{1,0:T(8,128)(2,1)S(1)}, u32[]{:S(2)}, u32[]{:S(2)}) collective-permute-start(bf16[256,128]{1,0:T(8,128)(2,1)S(1)} %get-tuple-element.159), channel_id=1, source_target_pairs={{4,0},{5,1},{12,2},{13,3},{20,4},{21,5},{28,6},{29,7},{6,8},{7,9},... | collective-permute-start | bytes 196616 | tf_op jit(solution)/shard_map/ppermute | solution.py:715
  216.8 12.6 %collective-permute-start.76 = (bf16[256,128]{1,0:T(8,128)(2,1)S(1)}, bf16[256,128]{1,0:T(8,128)(2,1)S(1)}, u32[]{:S(2)}, u32[]{:S(2)}) collective-permute-start(bf16[256,128]{1,0:T(8,128)(2,1)S(1)} %get-tuple-element.160), channel_id=1, source_target_pairs={{2,0},{3,1},{10,2},{11,3},{18,4},{19,5},{26,6},{27,7},{4,8},{5,9},... | collective-permute-start | bytes 196616 | tf_op jit(solution)/shard_map/ppermute | solution.py:715
  220.9 24.4 %collective-permute-start.85 = (bf16[64,1664]{1,0:T(8,128)(2,1)S(1)}, bf16[64,1664]{1,0:T(8,128)(2,1)S(1)}, u32[]{:S(2)}, u32[]{:S(2)}) collective-permute-start(bf16[64,1664]{1,0:T(8,128)(2,1)S(1)} %get-tuple-element.143), channel_id=1, source_target_pairs={{0,4},{1,5},{2,6},{3,7},{4,0},{5,1},{6,2},{7,3},{8,12},{9,13},{10,... | collective-permute-start | bytes 638984 | tf_op jit(solution)/shard_map/ppermute | solution.py:512
  229.3 15.9 %collective-permute-start.86 = (bf16[64,1664]{1,0:T(8,128)(2,1)S(1)}, bf16[64,1664]{1,0:T(8,128)(2,1)S(1)}, u32[]{:S(2)}, u32[]{:S(2)}) collective-permute-start(bf16[64,1664]{1,0:T(8,128)(2,1)S(1)} %get-tuple-element.144), channel_id=1, source_target_pairs={{0,6},{1,7},{2,4},{3,5},{4,2},{5,3},{6,0},{7,1},{8,14},{9,15},{10,... | collective-permute-start | bytes 638984 | tf_op jit(solution)/shard_map/ppermute | solution.py:512
  (75 other events, 489.0 us)

commit v3 on v2

--- a/solution.py
+++ b/solution.py
@@ -107,17 +107,30 @@
         message[NARROW + k : NARROW + k + 1, :] = second[:, 128 * k : 128 * k + 128]
 
 
+def repeat_first(message):
+    block = message[0]
+    for place in range(1, message.shape[0]):
+        message[place] = block
+
+
+def sum_parts(parts):
+    total = parts[0]
+    for place in range(1, parts.shape[0]):
+        total = total + parts[place]
+    return total
+
+
 def first_product(x, *refs):
     pieces, (w_first, send_far, own_far, send_near, own_near) = refs[:-5], refs[-5:]
     n, z, y = position()
     if len(pieces) == 1:
         w_first[...] = pieces[0][...]
     else:
-        rows, cols = pieces[0].shape
-        for place, piece in enumerate(pieces):
-            half = y ^ (place // NARROW)
-            block = (z - place % NARROW) & 3
-            w_first[pl.ds(pl.multiple_of(half * rows, rows), rows), lane_block(block)] = piece[...]
+        rows = pieces[0].shape[0] // 2
+        for j, piece in enumerate(pieces):
+            for dy in range(2):
+                here = pl.ds(pl.multiple_of((y ^ dy) * rows, rows), rows)
+                w_first[here, lane_block((z - j) & 3)] = piece[dy * rows : (dy + 1) * rows, :]
     for ref, m in ((send_far, 3), (own_far, 2), (send_near, 1), (own_near, 0)):
         ref[...] = dot(x[n ^ m], w_first[...]).astype(ref.dtype)
 
@@ -223,14 +236,15 @@
             return acc[0] + fold(kept), acc[1] + fold(kept * values)
 
         sums = by_rows(rows, collect, zeros_acc(pre.shape[2]))
-        message[2 * m : 2 * m + 1, :] = column_sum(sums[0])
-        message[2 * m + 1 : 2 * m + 2, :] = column_sum(sums[1])
+        message[0, 2 * m : 2 * m + 1, :] = column_sum(sums[0])
+        message[0, 2 * m + 1 : 2 * m + 2, :] = column_sum(sums[1])
+    repeat_first(message)
 
 
 def block_output(pre, x, cotangent, parts, params, gain, shift, mask, out, grad, coef, message):
     n = position()[0]
     rows, channels = pre.shape[1:]
-    block = parts[...]
+    block = sum_parts(parts)
     for m in range(NARROW):
         b = n ^ m
         mean, scale, slope, offset = coefficients(
@@ -252,15 +266,16 @@
             return acc[0] + fold(local), acc[1] + fold(local * (values * scale - back))
 
         sums = by_rows(rows, body, zeros_acc(channels))
-        message[2 * m : 2 * m + 1, :] = column_sum(sums[0])
-        message[2 * m + 1 : 2 * m + 2, :] = column_sum(sums[1])
+        message[0, 2 * m : 2 * m + 1, :] = column_sum(sums[0])
+        message[0, 2 * m + 1 : 2 * m + 2, :] = column_sum(sums[1])
+    repeat_first(message)
 
 
 def last_backward(pre, grad, parts, params, coef, mask, weight,
                   grad_pre, send_far, own_far, send_near, own_near, level_sum, tilt_sum):
     n = position()[0]
     rows = pre.shape[1]
-    block = parts[...]
+    block = sum_parts(parts)
     for s, ref in enumerate((level_sum, tilt_sum)):
         acc = block[s : s + 1]
         for m in range(1, NARROW):
@@ -283,7 +298,7 @@
         ref[...] = dot_nt(grad_pre[m], weight[...]).astype(ref.dtype)
 
 
-def middle_join(own, near, far, pre, coef, mask, grad, own_q, near_q, far_q, last_q, message):
+def middle_join(own, near, far, pre, coef, mask, grad, own_q, near_q, far_q, message):
     b = position()[0]
     mean, scale, slope, offset = (coef[k : k + 1, :] for k in range(4))
     back = mean * scale
@@ -301,8 +316,8 @@
     send_stats(message, column_sum(sums[0]), column_sum(sums[1]))
     own_q[...] = grad[:, lane_block(b)].astype(BF)
     near_q[...] = grad[:, lane_block(b ^ 1)].astype(BF)
-    far_q[...] = grad[:, lane_block(b ^ 2)].astype(BF)
-    last_q[...] = grad[:, lane_block(b ^ 3)].astype(BF)
+    far_q[0] = grad[:, lane_block(b ^ 2)].astype(BF)
+    far_q[1] = grad[:, lane_block(b ^ 3)].astype(BF)
 
 
 def middle_backward(grad, pre, parts, params, coef, mask, first_pre, first_coef, to_canvas, to_rows,
@@ -350,8 +365,9 @@
     send_stats(message, column_sum(sums2[0]), column_sum(sums2[1]))
 
 
-def first_backward(g0, g1, g2, g3, p0, p1, p2, p3, sum0, sum1, sum2, sum3, params, coef, mask, x, grad, weight,
-                   grad_input, level_sum, tilt_sum, out, grad_pre, acc):
+def first_weight(g0, g1, g2, g3, p0, p1, p2, p3, sum0, sum1, sum2, sum3, params, coef, mask, x,
+                 level_sum, tilt_sum, grad_pre, *refs):
+    outs, acc = refs[:-1], refs[-1]
     n, z, y = position()
     rows, channels = g0.shape
     blocks = (sum0[...], sum1[...], sum2[...], sum3[...])
@@ -364,29 +380,30 @@
         level = wide_row(block, 0) * inverse
         tilt = wide_row(block, NARROW) * inverse
         level, tilt = level - mean * scale * tilt, scale * tilt
-
-        def body(ds, carry):
-            away = mask[b, ds, :] * (level + pre[ds, :].astype(F32) * tilt)
-            grad_pre[m, ds, :] = (slope * (g[ds, :].astype(F32) - away)).astype(BF)
-            return carry
-
-        by_rows(rows, body, 0)
+        away = mask[b] * (level + pre[...].astype(F32) * tilt)
+        grad_pre[m] = (slope * (g[...].astype(F32) - away)).astype(BF)
         product = dot_tn(x[b], grad_pre[m])
         if m == 0:
             acc[...] = product
         else:
             acc[...] += product
-    if len(out.shape) == 2:
-        out[...] = acc[...]
+    if len(outs) == 1:
+        outs[0][...] = acc[...]
     else:
-        half, cols = out.shape[1:]
-        for place in range(out.shape[0]):
-            top = pl.multiple_of((y ^ (place // NARROW)) * half, half)
-            out[place] = acc[pl.ds(top, half), lane_block((z - place % NARROW) & 3)].astype(BF)
-    for m in range(NARROW):
-        grad_input[n ^ m] = dot_nt(grad_pre[m], weight[...]) + grad[m]
+        half = acc.shape[0] // 2
+        for ref, h in zip(outs, (y, 1 - y)):
+            top = pl.multiple_of(h * half, half)
+            for j in range(NARROW):
+                block = acc[pl.ds(top, half), lane_block((z - j) & 3)]
+                ref[:, 128 * j : 128 * j + 128] = block.astype(ref.dtype)
     level_sum[...] = row_of(every, 0, n)
     tilt_sum[...] = row_of(every, NARROW, n)
+
+
+def input_gradient(grad_pre, weight, grad, out):
+    n = position()[0]
+    for m in range(NARROW):
+        out[n ^ m] = dot_nt(grad_pre[m], weight[...]) + grad[m]
 
 
 def last_weight(hidden, grad_pre, *refs):
@@ -414,7 +431,7 @@
             ref[place, :] = acc[pl.ds(pl.multiple_of(top, rows), rows), :].astype(ref.dtype)
 
 
-def middle_weight(hidden, q0, q1, q2, q3, pre, sum0, sum1, sum2, sum3, norm, params, mask, to_canvas,
+def middle_weight(hidden, q0, q1, far, last, pre, sum0, sum1, sum2, sum3, norm, params, mask, to_canvas,
                   level_sum, tilt_sum, *refs):
     outs, (acc, shifted, canvas) = refs[:-3], refs[-3:]
     n = position()[0]
@@ -428,7 +445,7 @@
     every = blocks[0] + blocks[1] + blocks[2] + blocks[3]
     level_sum[...] = row_of(every, 0, n)
     tilt_sum[...] = row_of(every, NARROW, n)
-    for m, piece in enumerate((q0, q1, q2, q3)):
+    for m, piece in enumerate((q0[...], q1[...], far[0], last[1])):
         b = n ^ m
         inverse = inverse_count(params, b, 128)
         mean, scale, slope, _ = coefficients(
@@ -439,7 +456,7 @@
         tilt = row_of(block, NARROW, n) * inverse
         level, tilt = level - mean * scale * tilt, scale * tilt
         away = mask[b] * (level + pre[m].astype(F32) * tilt)
-        grad_pre = (slope * (piece[...].astype(F32) - away)).astype(BF)
+        grad_pre = (slope * (piece.astype(F32) - away)).astype(BF)
         canvas[margin : margin + places, :] = dot(to_canvas[...], grad_pre)
         for tap in range(TAPS):
             start = margin - ((tap // 3 - 1) * PITCH + tap % 3 - 1) * img
@@ -463,14 +480,19 @@
                 out[here, 128 * tap : 128 * tap + 128] = stack[top : top + rows, :]
 
 
-def gather_last(*refs):
-    pieces, out = refs[:-1], refs[-1]
+def gather_last(near, far, out):
     _, z, y = position()
     rows = out.shape[0] // 8
-    for j, pair in enumerate(pieces):
-        for dy in range(2):
+    for dy, stack in enumerate((near, far)):
+        for j in range(4):
             here = pl.ds(pl.multiple_of(((z ^ j) * 2 + (y ^ dy)) * rows, rows), rows)
-            out[here, :] = pair[dy * rows : (dy + 1) * rows, :]
+            out[here, :] = stack[j * rows : (j + 1) * rows, :]
+
+
+def merge_first(own, away, *sends):
+    for j, send in enumerate(sends):
+        here = slice(128 * j, 128 * j + 128)
+        send[...] = (own[:, here] + away[:, here].astype(F32)).astype(BF)
 
 
 def add_tiles(*refs):
@@ -527,17 +549,17 @@
     return run(add_tiles, tiles, [arr(tiles[0].shape, F32)])[0]
 
 
-def sum_wide(values, wide, *beside):
+def sum_wide(values, wide, beside=(), late=()):
     if wide == 8:
         values = add(after(values, *beside) if beside else values, swap_wide(values, 1, wide))
-        if beside:
-            return values, add(values, *(swap_wide(values, step, wide) for step in (2, 4, 6)))
-        return add(values, *(swap_wide(values, step, wide) for step in (2, 4, 6)))
+        parts = [swap_wide(values, step, wide) for step in (2, 4, 6)]
+        total = add(after(values, *late) if late else values, *parts)
+        return values, total
     step = 1
     while step < wide:
         values = add(values, swap_wide(values, step, wide))
         step *= 2
-    return (values, values) if beside else values
+    return values, values
 
 
 def reduce_narrow(send_far, own_far, send_near, own_near, *others):
@@ -551,14 +573,13 @@
 
 def transposed_steps():
     steps = []
-    for dy in range(2):
-        for j in range(NARROW):
-            pairs = []
-            for k in range(NARROW):
-                for z in range(4):
-                    for y in range(2):
-                        pairs.append((k * 8 + 2 * z + y, z * 8 + 2 * ((k + j) % 4) + (y ^ dy)))
-            steps.append(pairs)
+    for j in range(NARROW):
+        pairs = []
+        for k in range(NARROW):
+            for z in range(4):
+                for y in range(2):
+                    pairs.append((k * 8 + 2 * z + y, z * 8 + 2 * ((k + j) % 4) + y))
+        steps.append(pairs)
     return steps
 
 
@@ -575,8 +596,11 @@
 
     spots = jnp.arange(rows, dtype=jnp.int32)
     spot_y, spot_x, spot_img = spots % 49 // 7, spots % 7, spots // 49
-    limit = jnp.repeat(sides, 49, axis=1)
-    mask = ((spot_y[None] < limit) & (spot_x[None] < limit)).astype(F32)[:, :, None]
+
+    def mask_of(limits):
+        limits = jnp.repeat(limits, 49, axis=1)
+        return ((spot_y[None] < limits) & (spot_x[None] < limits)).astype(F32)[:, :, None]
+
     place = (spot_y * PITCH + spot_x) * img + spot_img
     to_canvas = (jnp.arange(places, dtype=jnp.int32)[:, None] == place[None, :]).astype(BF)
     to_rows = (place[:, None] == jnp.arange(places, dtype=jnp.int32)[None, :]).astype(BF)
@@ -584,7 +608,11 @@
     if direct:
         steps = transposed_steps()
         share = w_last.shape[0]
-        first_pieces = [lax.ppermute(w_first, MESH, pairs) for pairs in steps]
+        packed = w_middle.reshape(TAPS * share, 128)
+        middle_near = [packed] + [swap_wide(packed, 2 * j, wide) for j in range(1, 4)]
+        first_pair = jnp.concatenate([w_first, swap_wide(w_first, 1, wide)], axis=0)
+        first_pieces = [lax.ppermute(first_pair, MESH, pairs) for pairs in steps]
+        first_pieces[0] = after(first_pieces[0], *middle_near)
     else:
         first_all = lax.all_gather(lax.all_gather(w_first, "narrow", axis=1, tiled=True), "wide", axis=0, tiled=True)
         first_pieces = [lax.dynamic_slice_in_dim(first_all, n * low, low, 0)]
@@ -599,7 +627,7 @@
     )
 
     tile = arr((8, 128), F32)
-    across = arr((8, low), F32)
+    across = arr((wide, 8, low), F32)
     flat = arr((rows, mid), BF)
     flat32 = arr((rows, mid), F32)
 
@@ -609,21 +637,23 @@
     )
     joined, begun = reduce_narrow(send_far, own_far, send_near, own_near)
     if direct:
-        flat_middle = after(w_middle.reshape(TAPS * share, 128), begun)
-        middle_near = jnp.concatenate([flat_middle] + [swap_wide(flat_middle, 2 * j, wide) for j in range(1, 4)], axis=0)
+        middle_near = jnp.concatenate([after(middle_near[0], begun)] + middle_near[1:], axis=0)
         middle_far = swap_wide(middle_near, 1, wide)
-        held = after(w_last, begun)
-        last_pair = jnp.concatenate([held, swap_wide(held, 1, wide)], axis=0)
-        last_pieces = [last_pair] + [swap_wide(last_pair, 2 * j, wide) for j in range(1, 4)]
-        joined = (after(joined[0], middle_near, last_pair), *joined[1:])
+    mask = mask_of(after(sides, begun))
+    beside = ()
+    if direct:
+        held = after(w_last, mask)
+        last_near = jnp.concatenate([held] + [swap_wide(held, 2 * j, wide) for j in range(1, 4)], axis=0)
+        beside = (middle_far, last_near)
     pre_one, message = run(first_join, (*joined, mask, small), [flat, arr((16, 128), F32)])
-    total = sum_wide(message, wide)
-    pre_ones = from_all(pre_one, total, *((middle_far,) if direct else ()))
+    begun, total = sum_wide(message, wide, beside=beside)
+    if direct:
+        last_far = swap_wide(after(last_near, begun), 1, wide)
+    pre_ones = from_all(pre_one, total)
     sums_one = from_all(total)
     if direct:
         middle_slice = run(gather_middle, (middle_near, middle_far), [arr((mid, TAPS * 128), BF)])[0]
-        last_slice = run(gather_last, last_pieces, [arr((mid, low), BF)])[0]
-        middle_slice = after(middle_slice, *last_pieces)
+        middle_slice = after(middle_slice, last_far)
 
     hidden_one, pre_two, coef_one, message, params = run(
         middle_forward, (*pre_ones, *sums_one, mask, to_canvas, to_rows, middle_slice),
@@ -631,7 +661,9 @@
         [pltpu.VMEM((rows, mid), BF), pltpu.VMEM((places + 2 * img * (PITCH + 1), TAPS * 128), F32), pltpu.VMEM((places, 128), BF)],
         flops=2 * micro * places * mid * TAPS * 128,
     )
-    total = sum_wide(message, wide)
+    if direct:
+        last_slice = run(gather_last, (last_near, last_far), [arr((mid, low), BF)])[0]
+    _, total = sum_wide(message, wide)
     pre_twos = from_all(pre_two, total)
     sums_two = from_all(total)
     held = after(middle_slice, pre_twos[3], sums_two[3])
@@ -642,20 +674,21 @@
         [arr((micro, rows, mid), BF), flat, arr((8, mid), F32), arr((micro, rows, low), F32), across],
         flops=2 * micro * rows * low * mid,
     )
-    parts_three = sum_wide(message, wide)
+    parts_three = lax.all_to_all(message, "wide", 0, 0, tiled=True)
     block_out, grad_sum, coef_three, message = run(
         block_output,
         (pre_three, inputs, cotangent, parts_three, params, gain_last[None], shift_last[None], mask),
         [arr(inputs.shape, BF), arr((micro, rows, low), F32), arr((micro, 8, low), F32), across],
     )
-    parts_four = sum_wide(message, wide)
+    parts_four = lax.all_to_all(message, "wide", 0, 0, tiled=True)
 
     grad_three, send_far, own_far, send_near, own_near, level_three, tilt_three = run(
         last_backward, (pre_three, grad_sum, parts_four, params, coef_three, mask, last_slice),
         [arr((micro, rows, low), BF), flat, flat32, flat, flat32, arr((1, low), F32), arr((1, low), F32)],
         flops=2 * micro * rows * low * mid,
     )
-    joined, _ = reduce_narrow(send_far, own_far, send_near, own_near, middle_away)
+    joined, begun = reduce_narrow(send_far, own_far, send_near, own_near, middle_away)
+    grad_three = after(grad_three, begun)
 
     def handed(channels):
         if direct:
@@ -671,11 +704,13 @@
     if direct:
         got_last_sum = swap_wide(last_sum[1], 1, wide)
         joined = (after(joined[0], got_last_sum), *joined[1:])
-    grad_two, own_q, near_q, far_q, last_q, message = run(
-        middle_join, (*joined, own_two, coef_two, mask), [flat32, slim, slim, slim, slim, tile]
-    )
-    total_five = sum_wide(message, wide)
-    got_far, got_last, got_near = swap_chip(far_q), swap_core(swap_chip(last_q)), swap_core(near_q)
+    grad_two, own_q, near_q, far_q, message = run(
+        middle_join, (*joined, own_two, coef_two, mask), [flat32, slim, slim, arr((2, rows, 128), BF), tile]
+    )
+    got_far = swap_chip(far_q)
+    _, total_five = sum_wide(message, wide, late=(got_far,))
+    near_q, got_far = lax.optimization_barrier((near_q, got_far, total_five))[:2]
+    got_near, got_last = swap_core(near_q), swap_core(got_far)
     middle_slices = (middle_slice, swap_core(held), middle_away, swap_core(middle_away))
     sums_five = from_all(total_five)
 
@@ -695,31 +730,36 @@
          pltpu.VMEM((places + 2 * img * (PITCH + 1), 128), F32)],
         flops=2 * micro * places * mid * TAPS * 128,
     )
-    begun, total = sum_wide(message, wide, *middle_sum)
+    begun, total = sum_wide(message, wide, beside=middle_sum)
     grad_ones = from_all(after(grad_one, sums_five[2]), total)
     sums_six = from_all(total)
     if direct:
         got_middle = swap_wide(after(middle_sum[1], begun), 1, wide)
 
-    out_first = arr((8, 2 * low // NARROW, cols), BF) if direct else arr((low, mid), F32)
-    input_grad, level_one, tilt_one, first_sum = run(
-        first_backward,
-        (*grad_ones, *pre_ones, *sums_six, params, coef_one, mask, inputs, grad_sum, w_rows),
-        [arr((micro, rows, low), F32), row, row, out_first],
-        [pltpu.VMEM((micro, rows, mid), BF), pltpu.VMEM((low, mid), F32)],
-        flops=4 * micro * rows * low * mid,
-    )
+    out_first = [arr((low // 2, mid), F32), arr((low // 2, mid), BF)] if direct else [arr((low, mid), F32)]
+    level_one, tilt_one, grad_pre_one, *first_sum = run(
+        first_weight,
+        (*grad_ones, *pre_ones, *sums_six, after(params, got_middle) if direct else params, coef_one, mask, inputs),
+        [row, row, arr((micro, rows, mid), BF), *out_first], [pltpu.VMEM((low, mid), F32)],
+        flops=2 * micro * rows * low * mid,
+    )
+    input_grad = run(
+        input_gradient, (grad_pre_one, w_rows, grad_sum), [arr((micro, rows, low), F32)],
+        flops=2 * micro * rows * low * mid,
+    )[0]
 
     if direct:
-        arrived = [
-            lax.ppermute(first_sum[k], MESH, [(dst, src) for src, dst in pairs]) for k, pairs in enumerate(steps)
-        ]
+        got_first = swap_wide(first_sum[1], 1, wide)
         channels = TAPS * 128
         keep, keep_last, *sends = run(
-            merge_wide, (middle_sum[0], after(got_middle, first_sum), last_sum[0], got_last_sum),
+            merge_wide, (middle_sum[0], after(got_middle, first_sum[1]), last_sum[0], got_last_sum),
             [arr((share, channels), F32), arr((share, low), F32)] + [arr((share, channels + low), BF)] * 3,
         )
         parts = [swap_wide(send, 2 * j + 2, wide) for j, send in enumerate(sends)]
+        sends = run(merge_first, (first_sum[0], after(got_first, *parts[0:2])), [arr((low // 2, cols), BF)] * NARROW)
+        arrived = [
+            lax.ppermute(send, MESH, [(dst, src) for src, dst in pairs]) for send, pairs in zip(sends, steps)
+        ]
         grad_middle, grad_last = run(
             finish_wide, (after(keep, arrived[0]), keep_last, *parts),
             [arr((TAPS, share, 128), F32), arr((share, low), F32)],
@@ -733,7 +773,7 @@
         grad_middle = lax.psum_scatter(middle_sum[0], "wide", scatter_dimension=0, tiled=True)
         share = grad_middle.shape[0]
         grad_middle = grad_middle.reshape(share, TAPS, 128).transpose(1, 0, 2).reshape(3, 3, share, 128)
-        whole = lax.psum(first_sum, "wide")
+        whole = lax.psum(first_sum[0], "wide")
         whole = lax.all_gather(whole, "narrow", axis=0, tiled=True)
         share = whole.shape[0] // wide
         grad_first = lax.dynamic_slice(whole, (w * share, n * cols), (share, cols))

time: 248 us -> 213 us (0.86)
  starting transfers between devices: 106 us -> 76.5 us
  waiting for transfers between devices: 101 us -> 71.8 us
  blocking collectives: 0 us -> 21.7 us
    ppermute x16 -> x8, starting transfers between devices: 33.7 us -> 9.68 us  [the longest x4 6.12 us: on_device(): first_pieces = [lax.ppermute(first_pair, MESH, pairs) for pairs in steps]]
    ppermute x37 -> x31, waiting for transfers between devices: 74.6 us -> 52.8 us  [swap_wide(): return lax.ppermute(values, 'wide', [(i, i ^ step) for i in range(wide)])]
    all_to_all x0 -> x2, blocking collectives: none -> 21.7 us  [the longest x1 11.9 us: on_device(): parts_three = lax.all_to_all(message, 'wide', 0, 0, tiled=True)]
    ppermute x12 -> x11, waiting for transfers between devices: 17.7 us -> 7.64 us  [swap_chip(): return lax.ppermute(values, 'narrow', [(i, i ^ 2) for i in range(NARROW)])]
    ppermute x37 -> x31, starting transfers between devices: 50.8 us -> 42.2 us  [swap_wide(): return lax.ppermute(values, 'wide', [(i, i ^ step) for i in range(wide)])]
    ppermute x16 -> x8, waiting for transfers between devices: 1.72 us -> 5.25 us  [the longest x4 3.61 us: on_device(): lax.ppermute(send, MESH, [(dst, src) for src, dst in pairs])]
    ppermute x12 -> x11, starting transfers between devices: 16.7 us -> 19.8 us  [swap_chip(): return lax.ppermute(values, 'narrow', [(i, i ^ 2) for i in range(NARROW)])]
    pallas_call x27 -> x25, Pallas kernels: 31.7 us -> 32.3 us  [run(): pl.pallas_call(kernel, out_shape=outs, name=kernel.__name__, in_specs=[pl...]
  transfers between devices with their start and end apart: 87 -> 72, of which waited for: 36 -> 34; matrix products, arithmetic and copies ran while one was open for 2% -> 3% of each run, Pallas kernels for 10% -> 11%
where the time goes in v3:
time: 213 us; the launch traced here: 211 us
  starting transfers between devices  76.5 us (36%)
  waiting for transfers between devices  71.8 us (34%)
  Pallas kernels  32.3 us (15%)
  blocking collectives  21.7 us (10%)
  local copies, waits for them, and re-layouts  3.9 us (2%)
  other arithmetic  3.45 us (2%)
    ppermute x31, waiting for transfers between devices, swap_wide(): return lax.ppermute(values, 'wide', [(i, i ^ step) for i in range(wide)])  52.8 us
    ppermute x31, starting transfers between devices, swap_wide(): return lax.ppermute(values, 'wide', [(i, i ^ step) for i in range(wide)])  42.2 us
    pallas_call x25, Pallas kernels, run(): pl.pallas_call(kernel, out_shape=outs, name=kernel.__name__, in_specs=[pl...  32.3 us
    ppermute x11, starting transfers between devices, swap_chip(): return lax.ppermute(values, 'narrow', [(i, i ^ 2) for i in range(NARROW)])  19.8 us
    all_to_all x1, blocking collectives, on_device(): parts_three = lax.all_to_all(message, 'wide', 0, 0, tiled=True)  11.9 us
    all_to_all x1, blocking collectives, on_device(): parts_four = lax.all_to_all(message, 'wide', 0, 0, tiled=True)  9.8 us
    ppermute x11, waiting for transfers between devices, swap_chip(): return lax.ppermute(values, 'narrow', [(i, i ^ 2) for i in range(NARROW)])  7.64 us
    ppermute x4, starting transfers between devices, on_device(): first_pieces = [lax.ppermute(first_pair, MESH, pairs) for pairs in steps]  6.12 us
  transfers between devices with their start and end apart: 72, of which 34 were waited for; matrix products, arithmetic and copies ran while one was open for 3% of the time, Pallas kernels for 11%

profile of v3, /device:TPU:0, one launch (start us, length us, event | category | flops | bytes accessed | tf_op | source)
XLA Modules:
  0.0 210.7 jit_solution(3175899883423567430)
XLA Ops:
  0.6 3.1 %collective-permute-start.2 = (bf16[576,128]{1,0:T(8,128)(2,1)}, bf16[576,128]{1,0:T(8,128)(2,1)S(1)}, u32[]{:S(2)}, u32[]{:S(2)}) collective-permute-start(bf16[576,128]{1,0:T(8,128)(2,1)} %bitcast.16), channel_id=1, source_target_pairs={{0,2},{1,3},{2,0},{3,1},{4,6},{5,7},{6,4},{7,5},{8,10},{9,11},{10,... | collective-permute-start | bytes 442376 | tf_op jit(solution)/shard_map/ppermute | solution.py:534
  13.7 3.2 %collective-permute-start.6 = (bf16[512,128]{1,0:T(8,128)(2,1)S(1)}, bf16[512,128]{1,0:T(8,128)(2,1)S(1)}, u32[]{:S(2)}, u32[]{:S(2)}) collective-permute-start(bf16[512,128]{1,0:T(8,128)(2,1)S(1)} %constant_dynamic-update-slice_fusion), channel_id=1, source_target_pairs={{0,4},{1,5},{2,12},{3,13},{4,20},{5,21},{6,28},{7,29},{8,6},{9,7},... | collective-permute-start | bytes 393224 | tf_op jit(solution)/shard_map/ppermute | solution.py:614
  16.9 5.2 %collective-permute-done.3 = bf16[576,128]{1,0:T(8,128)(2,1)S(1)} collective-permute-done((bf16[576,128]{1,0:T(8,128)(2,1)}, bf16[576,128]{1,0:T(8,128)(2,1)S(1)}, u32[]{:S(2)}, u32[]{:S(2)}) %collective-permute-start.3) | collective-permute-done | bytes 147488 | tf_op jit(solution)/shard_map/ppermute | solution.py:534
  29.9 5.7 %collective-permute-start.10 = (bf16[392,512]{1,0:T(8,128)(2,1)S(1)}, bf16[392,512]{1,0:T(8,128)(2,1)S(1)}, u32[]{:S(2)}, u32[]{:S(2)}) collective-permute-start(bf16[392,512]{1,0:T(8,128)(2,1)S(1)} %add_convert_fusion.1), channel_id=1, source_target_pairs={{0,16},{8,24},{16,0},{24,8},{1,17},{9,25},{17,1},{25,9},{2,18},{10... | collective-permute-start | bytes 1204232 | tf_op jit(solution)/shard_map/ppermute | solution.py:530
  49.6 2.6 %collective-permute-done.11.far = bf16[2304,128]{1,0:T(8,128)(2,1)S(1)} collective-permute-done((bf16[2304,128]{1,0:T(8,128)(2,1)S(1)}, bf16[2304,128]{1,0:T(8,128)(2,1)S(1)}, u32[]{:S(2)}, u32[]{:S(2)}) %collective-permute-start.11) | collective-permute-done | bytes 589856 | tf_op jit(solution)/shard_map/ppermute | solution.py:534
  58.8 2.8 %collective-permute-done.18.refs_3_ = f32[16,128]{1,0:T(8,128)S(1)} collective-permute-done((f32[16,128]{1,0:T(8,128)S(1)}, f32[16,128]{1,0:T(8,128)S(1)}, u32[]{:S(2)}, u32[]{:S(2)}) %collective-permute-start.18) | collective-permute-done | bytes 8224 | tf_op jit(solution)/shard_map/ppermute | solution.py:534
  66.5 5.6 %middle_forward.1 = (bf16[4,448,512]{2,1,0:T(8,128)(2,1)S(1)}, bf16[4,392,128]{2,1,0:T(8,128)(2,1)S(1)}, f32[4,8,512]{2,1,0:T(8,128)S(1)}, f32[8,128]{1,0:T(8,128)S(1)}, f32[4,8,128]{2,1,0:T(8,128)S(1)}) custom-call(bf16[392,512]{1,0:T(8,128)(2,1)S(1)} %get-tuple-element.106.pre0.first_pre.p0, bf16[392,512]{1,0:T(8,128)(2,1)S(1)} %collective-permute-done.19.pre1.p1, ...), custom_call_target="tpu_custom_call" | custom-call | flops 2113929216 | bytes 5849216 | tf_op jit(solution)/shard_map/middle_forward/pallas_call | solution.py:39
  78.4 3.6 %collective-permute-start.29 = (f32[8,128]{1,0:T(8,128)S(1)}, f32[8,128]{1,0:T(8,128)S(1)}, u32[]{:S(2)}, u32[]{:S(2)}) collective-permute-start(f32[8,128]{1,0:T(8,128)S(1)} %add_tiles.10.refs_0_), channel_id=1, source_target_pairs={{0,6},{1,7},{2,4},{3,5},{4,2},{5,3},{6,0},{7,1},{8,14},{9,15},{10,... | collective-permute-start | bytes 12296 | tf_op jit(solution)/shard_map/ppermute | solution.py:534
  94.0 11.9 %all_to_all.10.parts = f32[8,8,512]{2,1,0:T(8,128)S(1)} all-to-all(f32[8,8,512]{2,1,0:T(8,128)S(1)} %get-tuple-element.116), channel_id=1, replica_groups=mesh['narrow'=4,'wide'=8] {'wide'}, dimensions={0} | all-to-all | bytes 262144 | tf_op jit(solution)/shard_map/all_to_all | solution.py:677
  105.9 3.6 %block_output.1 = (bf16[4,392,512]{2,1,0:T(8,128)(2,1)}, f32[4,392,512]{2,1,0:T(8,128)S(1)}, f32[4,8,512]{2,1,0:T(8,128)S(1)}, f32[8,8,512]{2,1,0:T(8,128)S(1)}) custom-call(f32[4,392,512]{2,1,0:T(8,128)S(1)} %get-tuple-element.115.pre, bf16[4,392,512]{2,1,0:T(8,128)(2,1)S(1)} %copy-done.1, bf16[4,392,512]{2,1,0:T(8,128)(2,1)S(1)} %copy-done.2, ...), custom_call_target="tpu_custom_call" | custom-call | bytes 11593856 | tf_op jit(solution)/shard_map/block_output/pallas_call | solution.py:39
  109.5 9.8 %all_to_all.11.parts = f32[8,8,512]{2,1,0:T(8,128)S(1)} all-to-all(f32[8,8,512]{2,1,0:T(8,128)S(1)} %get-tuple-element.119), channel_id=1, replica_groups=mesh['narrow'=4,'wide'=8] {'wide'}, dimensions={0} | all-to-all | bytes 262144 | tf_op jit(solution)/shard_map/all_to_all | solution.py:683
  126.7 7.8 %collective-permute-done.38.away_last = bf16[256,512]{1,0:T(8,128)(2,1)S(1)} collective-permute-done((bf16[256,512]{1,0:T(8,128)(2,1)S(1)}, bf16[256,512]{1,0:T(8,128)(2,1)S(1)}, u32[]{:S(2)}, u32[]{:S(2)}) %collective-permute-start.38) | collective-permute-done | bytes 262176 | tf_op jit(solution)/shard_map/ppermute | solution.py:534
  137.4 3.4 %collective-permute-done.41.refs_1_ = f32[8,128]{1,0:T(8,128)S(1)} collective-permute-done((f32[8,128]{1,0:T(8,128)S(1)}, f32[8,128]{1,0:T(8,128)S(1)}, u32[]{:S(2)}, u32[]{:S(2)}) %collective-permute-start.41) | collective-permute-done | bytes 4128 | tf_op jit(solution)/shard_map/ppermute | solution.py:534
  141.9 3.3 %collective-permute-start.45 = (f32[8,128]{1,0:T(8,128)S(1)}, f32[8,128]{1,0:T(8,128)S(1)}, u32[]{:S(2)}, u32[]{:S(2)}) collective-permute-start(f32[8,128]{1,0:T(8,128)S(1)} %add_tiles.12.refs_0_), channel_id=1, source_target_pairs={{0,6},{1,7},{2,4},{3,5},{4,2},{5,3},{6,0},{7,1},{8,14},{9,15},{10,... | collective-permute-start | bytes 12296 | tf_op jit(solution)/shard_map/ppermute | solution.py:534
  149.3 4.1 %middle_backward.1 = (bf16[392,512]{1,0:T(8,128)(2,1)S(1)}, f32[8,128]{1,0:T(8,128)S(1)}) custom-call(f32[392,512]{1,0:T(8,128)S(1)} %get-tuple-element.134.grad, bf16[392,512]{1,0:T(8,128)(2,1)S(1)} %get-tuple-element.132.pre, f32[8,128]{1,0:T(8,128)S(1)} %add_tiles.13.parts.sum0, f32[4,8,128]{2,1,0:T(8,128)S(1)} %get-tuple-element.153.params, ...), custom_call_target="tpu_custom_call" | custom-call | flops 2113929216 | bytes 7540864 | tf_op jit(solution)/shard_map/middle_backward/pallas_call | solution.py:39
  156.4 5.0 %middle_weight.1 = (f32[1,128]{1,0:T(1,128)}, f32[1,128]{1,0:T(1,128)}, f32[256,1152]{1,0:T(8,128)S(1)}, bf16[256,1152]{1,0:T(8,128)(2,1)S(1)}) custom-call(bf16[4,448,512]{2,1,0:T(8,128)(2,1)S(1)} %get-tuple-element.142.hidden, bf16[392,128]{1,0:T(8,128)(2,1)S(1)} %get-tuple-element.143.q0, bf16[392,128]{1,0:T(8,128)(2,1)S(1)} %collective-permute-done.49.q1, ...), custom_call_target="tpu_custom_call" | custom-call | flops 2113929216 | bytes 5003392 | tf_op jit(solution)/shard_map/middle_weight/pallas_call | solution.py:39
  162.4 3.8 %collective-permute-start.55 = (f32[8,128]{1,0:T(8,128)S(1)}, f32[8,128]{1,0:T(8,128)S(1)}, u32[]{:S(2)}, u32[]{:S(2)}) collective-permute-start(f32[8,128]{1,0:T(8,128)S(1)} %add_tiles.14.refs_0_), channel_id=1, source_target_pairs={{0,4},{1,5},{2,6},{3,7},{4,0},{5,1},{6,2},{7,3},{8,12},{9,13},{10,... | collective-permute-start | bytes 12296 | tf_op jit(solution)/shard_map/ppermute | solution.py:534
  167.7 3.8 %collective-permute-done.56.refs_3_ = f32[8,128]{1,0:T(8,128)S(1)} collective-permute-done((f32[8,128]{1,0:T(8,128)S(1)}, f32[8,128]{1,0:T(8,128)S(1)}, u32[]{:S(2)}, u32[]{:S(2)}) %collective-permute-start.56) | collective-permute-done | bytes 4128 | tf_op jit(solution)/shard_map/ppermute | solution.py:534
  172.4 3.3 %collective-permute-done.61.sum2 = f32[8,128]{1,0:T(8,128)S(1)} collective-permute-done((f32[8,128]{1,0:T(8,128)S(1)}, f32[8,128]{1,0:T(8,128)S(1)}, u32[]{:S(2)}, u32[]{:S(2)}) %collective-permute-start.61) | collective-permute-done | bytes 4128 | tf_op jit(solution)/shard_map/ppermute | solution.py:530
  180.1 3.8 %collective-permute-start.66 = (bf16[64,1664]{1,0:T(8,128)(2,1)S(1)}, bf16[64,1664]{1,0:T(8,128)(2,1)S(1)}, u32[]{:S(2)}, u32[]{:S(2)}) collective-permute-start(bf16[64,1664]{1,0:T(8,128)(2,1)S(1)} %get-tuple-element.161), channel_id=1, source_target_pairs={{0,4},{1,5},{2,6},{3,7},{4,0},{5,1},{6,2},{7,3},{8,12},{9,13},{10,... | collective-permute-start | bytes 638984 | tf_op jit(solution)/shard_map/ppermute | solution.py:534
  184.4 5.6 %collective-permute-done.65.p1 = bf16[64,1664]{1,0:T(8,128)(2,1)S(1)} collective-permute-done((bf16[64,1664]{1,0:T(8,128)(2,1)S(1)}, bf16[64,1664]{1,0:T(8,128)(2,1)S(1)}, u32[]{:S(2)}, u32[]{:S(2)}) %collective-permute-start.65) | collective-permute-done | bytes 213024 | tf_op jit(solution)/shard_map/ppermute | solution.py:534
  190.1 9.1 %collective-permute-done.66.p2 = bf16[64,1664]{1,0:T(8,128)(2,1)S(1)} collective-permute-done((bf16[64,1664]{1,0:T(8,128)(2,1)S(1)}, bf16[64,1664]{1,0:T(8,128)(2,1)S(1)}, u32[]{:S(2)}, u32[]{:S(2)}) %collective-permute-start.66) | collective-permute-done | bytes 213024 | tf_op jit(solution)/shard_map/ppermute | solution.py:534
  202.8 2.7 %input_gradient.1 = f32[4,392,512]{2,1,0:T(8,128)} custom-call(bf16[4,392,512]{2,1,0:T(8,128)(2,1)S(1)} %get-tuple-element.154.grad_pre, bf16[512,512]{1,0:T(8,128)(2,1)S(1)} %get-tuple-element.155.weight, f32[4,392,512]{2,1,0:T(8,128)S(1)} %get-tuple-element.118.grad), custom_call_target="tpu_custom_call" | custom-call | flops 822083584 | bytes 8552448 | tf_op jit(solution)/shard_map/input_gradient/pallas_call | solution.py:39
  205.6 3.6 %collective-permute-done.69 = bf16[256,128]{1,0:T(8,128)(2,1)S(1)} collective-permute-done((bf16[256,128]{1,0:T(8,128)(2,1)S(1)}, bf16[256,128]{1,0:T(8,128)(2,1)S(1)}, u32[]{:S(2)}, u32[]{:S(2)}) %collective-permute-start.69) | collective-permute-done | bytes 65568 | tf_op jit(solution)/shard_map/ppermute | solution.py:761
  (195 shorter events, 93.2 us)
Async XLA Ops:
  0.6 13.1 %collective-permute-start.2 = (bf16[576,128]{1,0:T(8,128)(2,1)}, bf16[576,128]{1,0:T(8,128)(2,1)S(1)}, u32[]{:S(2)}, u32[]{:S(2)}) collective-permute-start(bf16[576,128]{1,0:T(8,128)(2,1)} %bitcast.16), channel_id=1, source_target_pairs={{0,2},{1,3},{2,0},{3,1},{4,6},{5,7},{6,4},{7,5},{8,10},{9,11},{10,... | collective-permute-start | bytes 442376 | tf_op jit(solution)/shard_map/ppermute | solution.py:534
  3.7 18.4 %collective-permute-start.3 = (bf16[576,128]{1,0:T(8,128)(2,1)}, bf16[576,128]{1,0:T(8,128)(2,1)S(1)}, u32[]{:S(2)}, u32[]{:S(2)}) collective-permute-start(bf16[576,128]{1,0:T(8,128)(2,1)} %bitcast.17), channel_id=1, source_target_pairs={{0,4},{1,5},{2,6},{3,7},{4,0},{5,1},{6,2},{7,3},{8,12},{9,13},{10,... | collective-permute-start | bytes 442376 | tf_op jit(solution)/shard_map/ppermute | solution.py:534
  6.3 16.7 %collective-permute-start.4 = (bf16[576,128]{1,0:T(8,128)(2,1)}, bf16[576,128]{1,0:T(8,128)(2,1)S(1)}, u32[]{:S(2)}, u32[]{:S(2)}) collective-permute-start(bf16[576,128]{1,0:T(8,128)(2,1)} %bitcast.18), channel_id=1, source_target_pairs={{0,6},{1,7},{2,4},{3,5},{4,2},{5,3},{6,0},{7,1},{8,14},{9,15},{10,... | collective-permute-start | bytes 442376 | tf_op jit(solution)/shard_map/ppermute | solution.py:534
  10.8 12.2 %collective-permute-start.1 = (bf16[512,128]{1,0:T(8,128)(2,1)S(1)}, bf16[512,128]{1,0:T(8,128)(2,1)S(1)}, u32[]{:S(2)}, u32[]{:S(2)}) collective-permute-start(bf16[512,128]{1,0:T(8,128)(2,1)S(1)} %constant_dynamic-update-slice_fusion), channel_id=1, source_target_pairs={{0,0},{1,1},{2,8},{3,9},{4,16},{5,17},{6,24},{7,25},{8,2},{9,3},{1... | collective-permute-start | bytes 393224 | tf_op jit(solution)/shard_map/ppermute | solution.py:614
  11.5 11.5 %collective-permute-start.5 = (bf16[512,128]{1,0:T(8,128)(2,1)S(1)}, bf16[512,128]{1,0:T(8,128)(2,1)S(1)}, u32[]{:S(2)}, u32[]{:S(2)}) collective-permute-start(bf16[512,128]{1,0:T(8,128)(2,1)S(1)} %constant_dynamic-update-slice_fusion), channel_id=1, source_target_pairs={{0,2},{1,3},{2,10},{3,11},{4,18},{5,19},{6,26},{7,27},{8,4},{9,5},... | collective-permute-start | bytes 393224 | tf_op jit(solution)/shard_map/ppermute | solution.py:614
  13.7 9.3 %collective-permute-start.6 = (bf16[512,128]{1,0:T(8,128)(2,1)S(1)}, bf16[512,128]{1,0:T(8,128)(2,1)S(1)}, u32[]{:S(2)}, u32[]{:S(2)}) collective-permute-start(bf16[512,128]{1,0:T(8,128)(2,1)S(1)} %constant_dynamic-update-slice_fusion), channel_id=1, source_target_pairs={{0,4},{1,5},{2,12},{3,13},{4,20},{5,21},{6,28},{7,29},{8,6},{9,7},... | collective-permute-start | bytes 393224 | tf_op jit(solution)/shard_map/ppermute | solution.py:614
  28.5 14.9 %collective-permute-start.8 = (bf16[392,512]{1,0:T(8,128)(2,1)S(1)}, bf16[392,512]{1,0:T(8,128)(2,1)S(1)}, u32[]{:S(2)}, u32[]{:S(2)}) collective-permute-start(bf16[392,512]{1,0:T(8,128)(2,1)S(1)} %get-tuple-element.97), channel_id=1, source_target_pairs={{0,8},{8,0},{16,24},{24,16},{1,9},{9,1},{17,25},{25,17},{2,10},{10... | collective-permute-start | bytes 1204232 | tf_op jit(solution)/shard_map/ppermute | solution.py:526
  29.9 15.3 %collective-permute-start.10 = (bf16[392,512]{1,0:T(8,128)(2,1)S(1)}, bf16[392,512]{1,0:T(8,128)(2,1)S(1)}, u32[]{:S(2)}, u32[]{:S(2)}) collective-permute-start(bf16[392,512]{1,0:T(8,128)(2,1)S(1)} %add_convert_fusion.1), channel_id=1, source_target_pairs={{0,16},{8,24},{16,0},{24,8},{1,17},{9,25},{17,1},{25,9},{2,18},{10... | collective-permute-start | bytes 1204232 | tf_op jit(solution)/shard_map/ppermute | solution.py:530
  37.1 15.2 %collective-permute-start.11 = (bf16[2304,128]{1,0:T(8,128)(2,1)S(1)}, bf16[2304,128]{1,0:T(8,128)(2,1)S(1)}, u32[]{:S(2)}, u32[]{:S(2)}) collective-permute-start(bf16[2304,128]{1,0:T(8,128)(2,1)S(1)} %constant_dynamic-update-slice_fusion.2.near), channel_id=1, source_target_pairs={{0,1},{1,0},{2,3},{3,2},{4,5},{5,4},{6,7},{7,6},{8,9},{9,8},{10,11... | collective-permute-start | bytes 1769480 | tf_op jit(solution)/shard_map/ppermute | solution.py:534
  45.4 18.0 %collective-permute-start.20 = (bf16[392,512]{1,0:T(8,128)(2,1)S(1)}, bf16[392,512]{1,0:T(8,128)(2,1)S(1)}, u32[]{:S(2)}, u32[]{:S(2)}) collective-permute-start(bf16[392,512]{1,0:T(8,128)(2,1)S(1)} %get-tuple-element.106.pre0.first_pre.p0), channel_id=1, source_target_pairs={{0,16},{8,24},{16,0},{24,8},{1,17},{9,25},{17,1},{25,9},{2,18},{10... | collective-permute-start | bytes 1204232 | tf_op jit(solution)/shard_map/ppermute | solution.py:530
  72.1 11.6 %collective-permute-start.31 = (bf16[4,392,128]{2,1,0:T(8,128)(2,1)S(1)}, bf16[4,392,128]{2,1,0:T(8,128)(2,1)S(1)}, u32[]{:S(2)}, u32[]{:S(2)}) collective-permute-start(bf16[4,392,128]{2,1,0:T(8,128)(2,1)S(1)} %get-tuple-element.112.src0.pre), channel_id=1, source_target_pairs={{0,16},{8,24},{16,0},{24,8},{1,17},{9,25},{17,1},{25,9},{2,18},{10... | collective-permute-start | bytes 1204232 | tf_op jit(solution)/shard_map/ppermute | solution.py:530
  88.7 33.2 %collective-permute-start.37 = (bf16[512,1152]{1,0:T(8,128)(2,1)S(1)}, bf16[512,1152]{1,0:T(8,128)(2,1)S(1)}, u32[]{:S(2)}, u32[]{:S(2)}) collective-permute-start(bf16[512,1152]{1,0:T(8,128)(2,1)S(1)} %gather_middle.1.weight.w0), channel_id=1, source_target_pairs={{0,16},{8,24},{16,0},{24,8},{1,17},{9,25},{17,1},{25,9},{2,18},{10... | collective-permute-start | bytes 3538952 | tf_op jit(solution)/shard_map/ppermute | solution.py:530
  121.4 27.9 %collective-permute-start.46 = (bf16[512,1152]{1,0:T(8,128)(2,1)S(1)}, bf16[512,1152]{1,0:T(8,128)(2,1)S(1)}, u32[]{:S(2)}, u32[]{:S(2)}) collective-permute-start(bf16[512,1152]{1,0:T(8,128)(2,1)S(1)} %gather_middle.1.weight.w0), channel_id=1, source_target_pairs={{0,8},{8,0},{16,24},{24,16},{1,9},{9,1},{17,25},{25,17},{2,10},{10... | collective-permute-start | bytes 3538952 | tf_op jit(solution)/shard_map/ppermute | solution.py:526
  121.9 27.4 %collective-permute-start.47 = (bf16[512,1152]{1,0:T(8,128)(2,1)S(1)}, bf16[512,1152]{1,0:T(8,128)(2,1)S(1)}, u32[]{:S(2)}, u32[]{:S(2)}) collective-permute-start(bf16[512,1152]{1,0:T(8,128)(2,1)S(1)} %collective-permute-done.37.w2), channel_id=1, source_target_pairs={{0,8},{8,0},{16,24},{24,16},{1,9},{9,1},{17,25},{25,17},{2,10},{10... | collective-permute-start | bytes 3538952 | tf_op jit(solution)/shard_map/ppermute | solution.py:526
  121.9 12.6 %collective-permute-start.39 = (bf16[392,512]{1,0:T(8,128)(2,1)S(1)}, bf16[392,512]{1,0:T(8,128)(2,1)S(1)}, u32[]{:S(2)}, u32[]{:S(2)}) collective-permute-start(bf16[392,512]{1,0:T(8,128)(2,1)S(1)} %get-tuple-element.131), channel_id=1, source_target_pairs={{0,8},{8,0},{16,24},{24,16},{1,9},{9,1},{17,25},{25,17},{2,10},{10... | collective-permute-start | bytes 1204232 | tf_op jit(solution)/shard_map/ppermute | solution.py:526
  123.3 11.4 %collective-permute-start.40 = (bf16[392,512]{1,0:T(8,128)(2,1)S(1)}, bf16[392,512]{1,0:T(8,128)(2,1)S(1)}, u32[]{:S(2)}, u32[]{:S(2)}) collective-permute-start(bf16[392,512]{1,0:T(8,128)(2,1)S(1)} %add_convert_fusion), channel_id=1, source_target_pairs={{0,16},{8,24},{16,0},{24,8},{1,17},{9,25},{17,1},{25,9},{2,18},{10... | collective-permute-start | bytes 1204232 | tf_op jit(solution)/shard_map/ppermute | solution.py:530
  153.5 18.1 %collective-permute-start.58 = (bf16[392,512]{1,0:T(8,128)(2,1)S(1)}, bf16[392,512]{1,0:T(8,128)(2,1)S(1)}, u32[]{:S(2)}, u32[]{:S(2)}) collective-permute-start(bf16[392,512]{1,0:T(8,128)(2,1)S(1)} %get-tuple-element.150.g0), channel_id=1, source_target_pairs={{0,16},{8,24},{16,0},{24,8},{1,17},{9,25},{17,1},{25,9},{2,18},{10... | collective-permute-start | bytes 1204232 | tf_op jit(solution)/shard_map/ppermute | solution.py:530
  161.3 15.2 %collective-permute-start.63 = (bf16[256,1152]{1,0:T(8,128)(2,1)S(1)}, bf16[256,1152]{1,0:T(8,128)(2,1)S(1)}, u32[]{:S(2)}, u32[]{:S(2)}) collective-permute-start(bf16[256,1152]{1,0:T(8,128)(2,1)S(1)} %get-tuple-element.152), channel_id=1, source_target_pairs={{0,1},{1,0},{2,3},{3,2},{4,5},{5,4},{6,7},{7,6},{8,9},{9,8},{10,11... | collective-permute-start | bytes 1769480 | tf_op jit(solution)/shard_map/ppermute | solution.py:534
  179.1 20.0 %collective-permute-start.64 = (bf16[256,512]{1,0:T(8,128)(2,1)S(1)}, bf16[256,512]{1,0:T(8,128)(2,1)S(1)}, u32[]{:S(2)}, u32[]{:S(2)}) collective-permute-start(bf16[256,512]{1,0:T(8,128)(2,1)S(1)} %get-tuple-element.157), channel_id=1, source_target_pairs={{0,1},{1,0},{2,3},{3,2},{4,5},{5,4},{6,7},{7,6},{8,9},{9,8},{10,11... | collective-permute-start | bytes 786440 | tf_op jit(solution)/shard_map/ppermute | solution.py:534
  180.0 10.1 %collective-permute-start.65 = (bf16[64,1664]{1,0:T(8,128)(2,1)S(1)}, bf16[64,1664]{1,0:T(8,128)(2,1)S(1)}, u32[]{:S(2)}, u32[]{:S(2)}) collective-permute-start(bf16[64,1664]{1,0:T(8,128)(2,1)S(1)} %get-tuple-element.160), channel_id=1, source_target_pairs={{0,2},{1,3},{2,0},{3,1},{4,6},{5,7},{6,4},{7,5},{8,10},{9,11},{10,... | collective-permute-start | bytes 638984 | tf_op jit(solution)/shard_map/ppermute | solution.py:534
  180.1 19.1 %collective-permute-start.66 = (bf16[64,1664]{1,0:T(8,128)(2,1)S(1)}, bf16[64,1664]{1,0:T(8,128)(2,1)S(1)}, u32[]{:S(2)}, u32[]{:S(2)}) collective-permute-start(bf16[64,1664]{1,0:T(8,128)(2,1)S(1)} %get-tuple-element.161), channel_id=1, source_target_pairs={{0,4},{1,5},{2,6},{3,7},{4,0},{5,1},{6,2},{7,3},{8,12},{9,13},{10,... | collective-permute-start | bytes 638984 | tf_op jit(solution)/shard_map/ppermute | solution.py:534
  183.9 26.0 %collective-permute-start.71 = (bf16[64,1664]{1,0:T(8,128)(2,1)S(1)}, bf16[64,1664]{1,0:T(8,128)(2,1)S(1)}, u32[]{:S(2)}, u32[]{:S(2)}) collective-permute-start(bf16[64,1664]{1,0:T(8,128)(2,1)S(1)} %get-tuple-element.170), channel_id=1, source_target_pairs={{0,6},{1,7},{2,4},{3,5},{4,2},{5,3},{6,0},{7,1},{8,14},{9,15},{10,... | collective-permute-start | bytes 638984 | tf_op jit(solution)/shard_map/ppermute | solution.py:534
  199.3 9.8 %collective-permute-start.69 = (bf16[256,128]{1,0:T(8,128)(2,1)S(1)}, bf16[256,128]{1,0:T(8,128)(2,1)S(1)}, u32[]{:S(2)}, u32[]{:S(2)}) collective-permute-start(bf16[256,128]{1,0:T(8,128)(2,1)S(1)} %get-tuple-element.165), channel_id=1, source_target_pairs={{4,0},{5,1},{12,2},{13,3},{20,4},{21,5},{28,6},{29,7},{6,8},{7,9},... | collective-permute-start | bytes 196616 | tf_op jit(solution)/shard_map/ppermute | solution.py:761
  199.8 9.3 %collective-permute-start.68 = (bf16[256,128]{1,0:T(8,128)(2,1)S(1)}, bf16[256,128]{1,0:T(8,128)(2,1)S(1)}, u32[]{:S(2)}, u32[]{:S(2)}) collective-permute-start(bf16[256,128]{1,0:T(8,128)(2,1)S(1)} %get-tuple-element.164), channel_id=1, source_target_pairs={{2,0},{3,1},{10,2},{11,3},{18,4},{19,5},{26,6},{27,7},{4,8},{5,9},... | collective-permute-start | bytes 196616 | tf_op jit(solution)/shard_map/ppermute | solution.py:761
  (60 other events, 367.9 us)

commit v4 on v3

--- a/solution.py
+++ b/solution.py
@@ -111,6 +111,13 @@
     block = message[0]
     for place in range(1, message.shape[0]):
         message[place] = block
+
+
+def total_of(parts, index):
+    total = parts[index]
+    for place in range(NARROW, parts.shape[0], NARROW):
+        total = total + parts[place + index]
+    return total
 
 
 def sum_parts(parts):
@@ -198,16 +205,17 @@
             return acc[0] + fold(kept), acc[1] + fold(kept * values)
 
         sums = by_rows(rows, collect, zeros_acc(128))
-        message[2 * m : 2 * m + 1, :] = column_sum(sums[0])
-        message[2 * m + 1 : 2 * m + 2, :] = column_sum(sums[1])
-
-
-def last_forward(src0, src1, src2, src3, sum0, sum1, sum2, sum3, params, mask, weight,
+        message[0, 2 * m : 2 * m + 1, :] = column_sum(sums[0])
+        message[0, 2 * m + 1 : 2 * m + 2, :] = column_sum(sums[1])
+    repeat_first(message)
+
+
+def last_forward(src0, src1, src2, src3, parts, params, mask, weight,
                  hidden, own, coef, pre, message):
     n = position()[0]
     rows = own.shape[0]
     sources = (src0, src1, src2, src3)
-    blocks = (sum0[...], sum1[...], sum2[...], sum3[...])
+    blocks = [total_of(parts, n ^ i) for i in range(NARROW)]
     for m in range(NARROW):
         b = n ^ m
         for i in range(NARROW):
@@ -313,7 +321,8 @@
         return acc[0] + fold(local), acc[1] + fold(local * (values * scale - back))
 
     sums = by_rows(own.shape[0], body, zeros_acc(own.shape[1]))
-    send_stats(message, column_sum(sums[0]), column_sum(sums[1]))
+    send_stats(message.at[0], column_sum(sums[0]), column_sum(sums[1]))
+    repeat_first(message)
     own_q[...] = grad[:, lane_block(b)].astype(BF)
     near_q[...] = grad[:, lane_block(b ^ 1)].astype(BF)
     far_q[0] = grad[:, lane_block(b ^ 2)].astype(BF)
@@ -327,7 +336,7 @@
     rows, places = grad.shape[0], to_canvas.shape[0]
     img = places // (SIDE * PITCH)
     margin = img * (PITCH + 1)
-    block = parts[...]
+    block = sum_parts(parts)
     mean, scale, slope = (coef[k : k + 1, :] for k in range(3))
     inverse = inverse_count(params, n, grad.shape[1])
     level = wide_row(block, 0) * inverse
@@ -440,7 +449,7 @@
     margin = img * (PITCH + 1)
     canvas[0:margin, :] = jnp.zeros((margin, 128), F32)
     canvas[margin + places :, :] = jnp.zeros((margin, 128), F32)
-    norms = norm[...]
+    norms = total_of(norm, n)
     blocks = (sum0[...], sum1[...], sum2[...], sum3[...])
     every = blocks[0] + blocks[1] + blocks[2] + blocks[3]
     level_sum[...] = row_of(every, 0, n)
@@ -502,6 +511,10 @@
     refs[-1][...] = total
 
 
+def add_parts(parts, out):
+    out[...] = sum_parts(parts)
+
+
 def merge_wide(own, away, own_last, away_last, keep, keep_last, *sends):
     rows, middle = keep.shape
     keep[...] = own[0:rows, :] + away[0:rows, :].astype(F32)
@@ -520,6 +533,10 @@
     out_last[...] = (
         keep_last[...] + p1[:, middle:].astype(F32) + p2[:, middle:].astype(F32) + p3[:, middle:].astype(F32)
     )
+
+
+def exchange(message):
+    return lax.all_to_all(message, ("wide", "narrow"), 0, 0, tiled=True)
 
 
 def swap_core(values):
@@ -657,20 +674,19 @@
 
     hidden_one, pre_two, coef_one, message, params = run(
         middle_forward, (*pre_ones, *sums_one, mask, to_canvas, to_rows, middle_slice),
-        [arr((micro, places, mid), BF), arr((micro, rows, 128), BF), arr((micro, 8, mid), F32), tile, arr((NARROW, 8, 128), F32)],
+        [arr((micro, places, mid), BF), arr((micro, rows, 128), BF), arr((micro, 8, mid), F32), arr((wide * NARROW, 8, 128), F32), arr((NARROW, 8, 128), F32)],
         [pltpu.VMEM((rows, mid), BF), pltpu.VMEM((places + 2 * img * (PITCH + 1), TAPS * 128), F32), pltpu.VMEM((places, 128), BF)],
         flops=2 * micro * places * mid * TAPS * 128,
     )
     if direct:
         last_slice = run(gather_last, (last_near, last_far), [arr((mid, low), BF)])[0]
-    _, total = sum_wide(message, wide)
-    pre_twos = from_all(pre_two, total)
-    sums_two = from_all(total)
-    held = after(middle_slice, pre_twos[3], sums_two[3])
+    parts_two = exchange(message)
+    pre_twos = from_all(pre_two, parts_two)
+    held = after(middle_slice, pre_twos[3], parts_two)
     middle_away = swap_chip(held)
 
     hidden_two, own_two, coef_two, pre_three, message = run(
-        last_forward, (*pre_twos, *sums_two, params, mask, last_slice),
+        last_forward, (*pre_twos, parts_two, params, mask, last_slice),
         [arr((micro, rows, mid), BF), flat, arr((8, mid), F32), arr((micro, rows, low), F32), across],
         flops=2 * micro * rows * low * mid,
     )
@@ -705,18 +721,19 @@
         got_last_sum = swap_wide(last_sum[1], 1, wide)
         joined = (after(joined[0], got_last_sum), *joined[1:])
     grad_two, own_q, near_q, far_q, message = run(
-        middle_join, (*joined, own_two, coef_two, mask), [flat32, slim, slim, arr((2, rows, 128), BF), tile]
+        middle_join, (*joined, own_two, coef_two, mask), [flat32, slim, slim, arr((2, rows, 128), BF), arr((wide, 8, 128), F32)]
     )
     got_far = swap_chip(far_q)
-    _, total_five = sum_wide(message, wide, late=(got_far,))
-    near_q, got_far = lax.optimization_barrier((near_q, got_far, total_five))[:2]
+    middle_slices = (middle_slice, swap_core(held), middle_away, swap_core(middle_away))
+    parts_five = lax.all_to_all(after(message, *middle_slices), "wide", 0, 0, tiled=True)
+    total_five = run(add_parts, (parts_five,), [tile])[0]
+    near_q, got_far = lax.optimization_barrier((near_q, got_far, parts_five))[:2]
     got_near, got_last = swap_core(near_q), swap_core(got_far)
-    middle_slices = (middle_slice, swap_core(held), middle_away, swap_core(middle_away))
     sums_five = from_all(total_five)
 
     grad_one, message = run(
         middle_backward,
-        (grad_two, own_two, total_five, params, coef_two, mask, pre_one, coef_one, to_canvas, to_rows, *middle_slices),
+        (grad_two, own_two, parts_five, params, coef_two, mask, pre_one, coef_one, to_canvas, to_rows, *middle_slices),
         [flat, tile],
         [pltpu.VMEM((rows, mid), BF), pltpu.VMEM((TAPS, mid, mid), BF),
          pltpu.VMEM((places + 2 * img * (PITCH + 1), mid), F32), pltpu.VMEM((places, mid), F32)],
@@ -724,7 +741,7 @@
     )
     level_two, tilt_two, *middle_sum = run(
         middle_weight,
-        (hidden_one, own_q, got_near, got_far, got_last, pre_two, *sums_five, sums_two[0], params, mask, to_canvas),
+        (hidden_one, own_q, got_near, got_far, got_last, pre_two, *sums_five, parts_two, params, mask, to_canvas),
         [row, row, *handed(TAPS * 128)],
         [pltpu.VMEM((mid, TAPS * 128), F32), pltpu.VMEM((places, TAPS * 128), BF),
          pltpu.VMEM((places + 2 * img * (PITCH + 1), 128), F32)],

time: 213 us -> 207 us (0.972)
  blocking collectives: 21.7 us -> 40.8 us
  waiting for transfers between devices: 71.8 us -> 57.9 us
  starting transfers between devices: 76.5 us -> 64.8 us
    all_to_all x0 -> x2, blocking collectives: none -> 21 us  [the longest x1 12 us: exchange(): return lax.all_to_all(message, ('wide', 'narrow'), 0, 0, tiled=True)]
    ppermute x31 -> x23, waiting for transfers between devices: 52.8 us -> 41.7 us  [swap_wide(): return lax.ppermute(values, 'wide', [(i, i ^ step) for i in range(wide)])]
    ppermute x31 -> x23, starting transfers between devices: 42.2 us -> 32.4 us  [swap_wide(): return lax.ppermute(values, 'wide', [(i, i ^ step) for i in range(wide)])]
    ppermute x11 -> x10, starting transfers between devices: 19.8 us -> 17.3 us  [swap_chip(): return lax.ppermute(values, 'narrow', [(i, i ^ 2) for i in range(NARROW)])]
    ppermute x11 -> x10, waiting for transfers between devices: 7.64 us -> 5.41 us  [swap_chip(): return lax.ppermute(values, 'narrow', [(i, i ^ 2) for i in range(NARROW)])]
    ppermute x22 -> x20, waiting for transfers between devices: 6.05 us -> 6.79 us  [swap_core(): return lax.ppermute(values, 'narrow', [(i, i ^ 1) for i in range(NARROW)])]
    ppermute x22 -> x20, starting transfers between devices: 4.92 us -> 4.34 us  [swap_core(): return lax.ppermute(values, 'narrow', [(i, i ^ 1) for i in range(NARROW)])]
    pallas_call x25 -> x22, Pallas kernels: 32.3 us -> 32.2 us  [run(): pl.pallas_call(kernel, out_shape=outs, name=kernel.__name__, in_specs=[pl...]
  transfers between devices with their start and end apart: 72 -> 61, of which waited for: 34 -> 26; matrix products, arithmetic and copies ran while one was open for 3% -> 3% of each run, Pallas kernels for 11% -> 11%
where the time goes in v4:
time: 207 us; the launch traced here: 204 us
  starting transfers between devices  64.8 us (31%)
  waiting for transfers between devices  57.9 us (28%)
  blocking collectives  40.8 us (20%)
  Pallas kernels  32.2 us (16%)
  local copies, waits for them, and re-layouts  3.9 us (2%)
  other arithmetic  3.45 us (2%)
    ppermute x23, waiting for transfers between devices, swap_wide(): return lax.ppermute(values, 'wide', [(i, i ^ step) for i in range(wide)])  41.7 us
    ppermute x23, starting transfers between devices, swap_wide(): return lax.ppermute(values, 'wide', [(i, i ^ step) for i in range(wide)])  32.4 us
    pallas_call x22, Pallas kernels, run(): pl.pallas_call(kernel, out_shape=outs, name=kernel.__name__, in_specs=[pl...  32.2 us
    ppermute x10, starting transfers between devices, swap_chip(): return lax.ppermute(values, 'narrow', [(i, i ^ 2) for i in range(NARROW)])  17.3 us
    all_to_all x1, blocking collectives, exchange(): return lax.all_to_all(message, ('wide', 'narrow'), 0, 0, tiled=True)  12 us
    all_to_all x1, blocking collectives, on_device(): parts_three = lax.all_to_all(message, 'wide', 0, 0, tiled=True)  9.96 us
    all_to_all x1, blocking collectives, on_device(): parts_four = lax.all_to_all(message, 'wide', 0, 0, tiled=True)  9.83 us
    all_to_all x1, blocking collectives, on_device(): lax.all_to_all(after(message, *middle_slices), 'wide', 0, 0, tiled=True)  9.05 us
  transfers between devices with their start and end apart: 61, of which 26 were waited for; matrix products, arithmetic and copies ran while one was open for 3% of the time, Pallas kernels for 11%

profile of v4, /device:TPU:0, one launch (start us, length us, event | category | flops | bytes accessed | tf_op | source)
XLA Modules:
  0.0 204.0 jit_solution(3812473361719123328)
XLA Ops:
  0.6 3.1 %collective-permute-start.2 = (bf16[576,128]{1,0:T(8,128)(2,1)}, bf16[576,128]{1,0:T(8,128)(2,1)S(1)}, u32[]{:S(2)}, u32[]{:S(2)}) collective-permute-start(bf16[576,128]{1,0:T(8,128)(2,1)} %bitcast.16), channel_id=1, source_target_pairs={{0,2},{1,3},{2,0},{3,1},{4,6},{5,7},{6,4},{7,5},{8,10},{9,11},{10,... | collective-permute-start | bytes 442376 | tf_op jit(solution)/shard_map/ppermute | solution.py:551
  3.7 2.6 %collective-permute-start.3 = (bf16[576,128]{1,0:T(8,128)(2,1)}, bf16[576,128]{1,0:T(8,128)(2,1)S(1)}, u32[]{:S(2)}, u32[]{:S(2)}) collective-permute-start(bf16[576,128]{1,0:T(8,128)(2,1)} %bitcast.17), channel_id=1, source_target_pairs={{0,4},{1,5},{2,6},{3,7},{4,0},{5,1},{6,2},{7,3},{8,12},{9,13},{10,... | collective-permute-start | bytes 442376 | tf_op jit(solution)/shard_map/ppermute | solution.py:551
  13.7 3.2 %collective-permute-start.6 = (bf16[512,128]{1,0:T(8,128)(2,1)S(1)}, bf16[512,128]{1,0:T(8,128)(2,1)S(1)}, u32[]{:S(2)}, u32[]{:S(2)}) collective-permute-start(bf16[512,128]{1,0:T(8,128)(2,1)S(1)} %constant_dynamic-update-slice_fusion), channel_id=1, source_target_pairs={{0,4},{1,5},{2,12},{3,13},{4,20},{5,21},{6,28},{7,29},{8,6},{9,7},... | collective-permute-start | bytes 393224 | tf_op jit(solution)/shard_map/ppermute | solution.py:631
  16.9 5.2 %collective-permute-done.3 = bf16[576,128]{1,0:T(8,128)(2,1)S(1)} collective-permute-done((bf16[576,128]{1,0:T(8,128)(2,1)}, bf16[576,128]{1,0:T(8,128)(2,1)S(1)}, u32[]{:S(2)}, u32[]{:S(2)}) %collective-permute-start.3) | collective-permute-done | bytes 147488 | tf_op jit(solution)/shard_map/ppermute | solution.py:551
  29.9 5.7 %collective-permute-start.10 = (bf16[392,512]{1,0:T(8,128)(2,1)S(1)}, bf16[392,512]{1,0:T(8,128)(2,1)S(1)}, u32[]{:S(2)}, u32[]{:S(2)}) collective-permute-start(bf16[392,512]{1,0:T(8,128)(2,1)S(1)} %add_convert_fusion.1), channel_id=1, source_target_pairs={{0,16},{8,24},{16,0},{24,8},{1,17},{9,25},{17,1},{25,9},{2,18},{10... | collective-permute-start | bytes 1204232 | tf_op jit(solution)/shard_map/ppermute | solution.py:547
  49.6 2.6 %collective-permute-done.11.far = bf16[2304,128]{1,0:T(8,128)(2,1)S(1)} collective-permute-done((bf16[2304,128]{1,0:T(8,128)(2,1)S(1)}, bf16[2304,128]{1,0:T(8,128)(2,1)S(1)}, u32[]{:S(2)}, u32[]{:S(2)}) %collective-permute-start.11) | collective-permute-done | bytes 589856 | tf_op jit(solution)/shard_map/ppermute | solution.py:551
  58.8 2.8 %collective-permute-done.18.refs_3_ = f32[16,128]{1,0:T(8,128)S(1)} collective-permute-done((f32[16,128]{1,0:T(8,128)S(1)}, f32[16,128]{1,0:T(8,128)S(1)}, u32[]{:S(2)}, u32[]{:S(2)}) %collective-permute-start.18) | collective-permute-done | bytes 8224 | tf_op jit(solution)/shard_map/ppermute | solution.py:551
  66.5 5.6 %middle_forward.1 = (bf16[4,448,512]{2,1,0:T(8,128)(2,1)S(1)}, bf16[4,392,128]{2,1,0:T(8,128)(2,1)S(1)}, f32[4,8,512]{2,1,0:T(8,128)S(1)}, f32[32,8,128]{2,1,0:T(8,128)S(1)}, f32[4,8,128]{2,1,0:T(8,128)S(1)}) custom-call(bf16[392,512]{1,0:T(8,128)(2,1)S(1)} %get-tuple-element.106.pre0.first_pre.p0, bf16[392,512]{1,0:T(8,128)(2,1)S(1)} %collective-permute-done.19.pre1.p1, ...), custom_call_target="tpu_custom_call" | custom-call | flops 2113929216 | bytes 5976192 | tf_op jit(solution)/shard_map/middle_forward/pallas_call | solution.py:39
  73.9 12.0 %all_to_all.20.parts.norm = f32[32,8,128]{2,1,0:T(8,128)S(1)} all-to-all(f32[32,8,128]{2,1,0:T(8,128)S(1)} %get-tuple-element.111), channel_id=1, replica_groups=mesh['narrow'=4,'wide'=8] {'wide','narrow'}, dimensions={0} | all-to-all | bytes 262144 | tf_op jit(solution)/shard_map/all_to_all | solution.py:539
  93.3 10.0 %all_to_all.21.parts = f32[8,8,512]{2,1,0:T(8,128)S(1)} all-to-all(f32[8,8,512]{2,1,0:T(8,128)S(1)} %get-tuple-element.116), channel_id=1, replica_groups=mesh['narrow'=4,'wide'=8] {'wide'}, dimensions={0} | all-to-all | bytes 262144 | tf_op jit(solution)/shard_map/all_to_all | solution.py:693
  103.3 3.6 %block_output.1 = (bf16[4,392,512]{2,1,0:T(8,128)(2,1)}, f32[4,392,512]{2,1,0:T(8,128)S(1)}, f32[4,8,512]{2,1,0:T(8,128)S(1)}, f32[8,8,512]{2,1,0:T(8,128)S(1)}) custom-call(f32[4,392,512]{2,1,0:T(8,128)S(1)} %get-tuple-element.115.pre, bf16[4,392,512]{2,1,0:T(8,128)(2,1)S(1)} %copy-done.1, bf16[4,392,512]{2,1,0:T(8,128)(2,1)S(1)} %copy-done.2, ...), custom_call_target="tpu_custom_call" | custom-call | bytes 11593856 | tf_op jit(solution)/shard_map/block_output/pallas_call | solution.py:39
  106.9 9.8 %all_to_all.22.parts = f32[8,8,512]{2,1,0:T(8,128)S(1)} all-to-all(f32[8,8,512]{2,1,0:T(8,128)S(1)} %get-tuple-element.119), channel_id=1, replica_groups=mesh['narrow'=4,'wide'=8] {'wide'}, dimensions={0} | all-to-all | bytes 262144 | tf_op jit(solution)/shard_map/all_to_all | solution.py:699
  122.7 7.9 %collective-permute-done.31.away_last = bf16[256,512]{1,0:T(8,128)(2,1)S(1)} collective-permute-done((bf16[256,512]{1,0:T(8,128)(2,1)S(1)}, bf16[256,512]{1,0:T(8,128)(2,1)S(1)}, u32[]{:S(2)}, u32[]{:S(2)}) %collective-permute-start.31) | collective-permute-done | bytes 262176 | tf_op jit(solution)/shard_map/ppermute | solution.py:551
  133.2 9.1 %all_to_all.23.parts = f32[8,8,128]{2,1,0:T(8,128)S(1)} all-to-all(f32[8,8,128]{2,1,0:T(8,128)S(1)} %get-tuple-element.136), channel_id=1, replica_groups=mesh['narrow'=4,'wide'=8] {'wide'}, dimensions={0} | all-to-all | bytes 65536 | tf_op jit(solution)/shard_map/all_to_all | solution.py:728
  144.4 4.1 %middle_backward.1 = (bf16[392,512]{1,0:T(8,128)(2,1)S(1)}, f32[8,128]{1,0:T(8,128)S(1)}) custom-call(f32[392,512]{1,0:T(8,128)S(1)} %get-tuple-element.134.grad, bf16[392,512]{1,0:T(8,128)(2,1)S(1)} %get-tuple-element.132.pre, f32[8,8,128]{2,1,0:T(8,128)S(1)} %all_to_all.23.parts, f32[4,8,128]{2,1,0:T(8,128)S(1)} %get-tuple-element.153.params, ...), custom_call_target="tpu_custom_call" | custom-call | flops 2113929216 | bytes 7569536 | tf_op jit(solution)/shard_map/middle_backward/pallas_call | solution.py:39
  150.7 4.9 %middle_weight.1 = (f32[1,128]{1,0:T(1,128)}, f32[1,128]{1,0:T(1,128)}, f32[256,1152]{1,0:T(8,128)S(1)}, bf16[256,1152]{1,0:T(8,128)(2,1)S(1)}) custom-call(bf16[4,448,512]{2,1,0:T(8,128)(2,1)S(1)} %get-tuple-element.141.hidden, bf16[392,128]{1,0:T(8,128)(2,1)S(1)} %get-tuple-element.142.q0, bf16[392,128]{1,0:T(8,128)(2,1)S(1)} %collective-permute-done.38.q1, ...), custom_call_target="tpu_custom_call" | custom-call | flops 2113929216 | bytes 5130368 | tf_op jit(solution)/shard_map/middle_weight/pallas_call | solution.py:39
  158.4 3.3 %collective-permute-start.45 = (f32[8,128]{1,0:T(8,128)S(1)}, f32[8,128]{1,0:T(8,128)S(1)}, u32[]{:S(2)}, u32[]{:S(2)}) collective-permute-start(f32[8,128]{1,0:T(8,128)S(1)} %add_tiles.6.refs_0_), channel_id=1, source_target_pairs={{0,6},{1,7},{2,4},{3,5},{4,2},{5,3},{6,0},{7,1},{8,14},{9,15},{10,... | collective-permute-start | bytes 12296 | tf_op jit(solution)/shard_map/ppermute | solution.py:551
  167.9 3.0 %collective-permute-done.52.away = bf16[256,1152]{1,0:T(8,128)(2,1)S(1)} collective-permute-done((bf16[256,1152]{1,0:T(8,128)(2,1)S(1)}, bf16[256,1152]{1,0:T(8,128)(2,1)S(1)}, u32[]{:S(2)}, u32[]{:S(2)}) %collective-permute-start.52) | collective-permute-done | bytes 589856 | tf_op jit(solution)/shard_map/ppermute | solution.py:551
  175.9 3.3 %collective-permute-start.60 = (bf16[64,1664]{1,0:T(8,128)(2,1)S(1)}, bf16[64,1664]{1,0:T(8,128)(2,1)S(1)}, u32[]{:S(2)}, u32[]{:S(2)}) collective-permute-start(bf16[64,1664]{1,0:T(8,128)(2,1)S(1)} %get-tuple-element.170), channel_id=1, source_target_pairs={{0,6},{1,7},{2,4},{3,5},{4,2},{5,3},{6,0},{7,1},{8,14},{9,15},{10,... | collective-permute-start | bytes 638984 | tf_op jit(solution)/shard_map/ppermute | solution.py:551
  179.2 5.4 %collective-permute-done.54.p1 = bf16[64,1664]{1,0:T(8,128)(2,1)S(1)} collective-permute-done((bf16[64,1664]{1,0:T(8,128)(2,1)S(1)}, bf16[64,1664]{1,0:T(8,128)(2,1)S(1)}, u32[]{:S(2)}, u32[]{:S(2)}) %collective-permute-start.54) | collective-permute-done | bytes 213024 | tf_op jit(solution)/shard_map/ppermute | solution.py:551
  184.6 8.1 %collective-permute-done.55.p2 = bf16[64,1664]{1,0:T(8,128)(2,1)S(1)} collective-permute-done((bf16[64,1664]{1,0:T(8,128)(2,1)S(1)}, bf16[64,1664]{1,0:T(8,128)(2,1)S(1)}, u32[]{:S(2)}, u32[]{:S(2)}) %collective-permute-start.55) | collective-permute-done | bytes 213024 | tf_op jit(solution)/shard_map/ppermute | solution.py:551
  194.5 2.3 %collective-permute-start.57 = (bf16[256,128]{1,0:T(8,128)(2,1)S(1)}, bf16[256,128]{1,0:T(8,128)(2,1)S(1)}, u32[]{:S(2)}, u32[]{:S(2)}) collective-permute-start(bf16[256,128]{1,0:T(8,128)(2,1)S(1)} %get-tuple-element.164), channel_id=1, source_target_pairs={{2,0},{3,1},{10,2},{11,3},{18,4},{19,5},{26,6},{27,7},{4,8},{5,9},... | collective-permute-start | bytes 196616 | tf_op jit(solution)/shard_map/ppermute | solution.py:778
  197.5 2.7 %input_gradient.1 = f32[4,392,512]{2,1,0:T(8,128)} custom-call(bf16[4,392,512]{2,1,0:T(8,128)(2,1)S(1)} %get-tuple-element.154.grad_pre, bf16[512,512]{1,0:T(8,128)(2,1)S(1)} %get-tuple-element.155.weight, f32[4,392,512]{2,1,0:T(8,128)S(1)} %get-tuple-element.118.grad), custom_call_target="tpu_custom_call" | custom-call | flops 822083584 | bytes 8552448 | tf_op jit(solution)/shard_map/input_gradient/pallas_call | solution.py:39
  200.2 2.3 %collective-permute-done.58 = bf16[256,128]{1,0:T(8,128)(2,1)S(1)} collective-permute-done((bf16[256,128]{1,0:T(8,128)(2,1)S(1)}, bf16[256,128]{1,0:T(8,128)(2,1)S(1)}, u32[]{:S(2)}, u32[]{:S(2)}) %collective-permute-start.58) | collective-permute-done | bytes 65568 | tf_op jit(solution)/shard_map/ppermute | solution.py:778
  (172 shorter events, 80.3 us)
Async XLA Ops:
  0.6 13.1 %collective-permute-start.2 = (bf16[576,128]{1,0:T(8,128)(2,1)}, bf16[576,128]{1,0:T(8,128)(2,1)S(1)}, u32[]{:S(2)}, u32[]{:S(2)}) collective-permute-start(bf16[576,128]{1,0:T(8,128)(2,1)} %bitcast.16), channel_id=1, source_target_pairs={{0,2},{1,3},{2,0},{3,1},{4,6},{5,7},{6,4},{7,5},{8,10},{9,11},{10,... | collective-permute-start | bytes 442376 | tf_op jit(solution)/shard_map/ppermute | solution.py:551
  3.7 18.4 %collective-permute-start.3 = (bf16[576,128]{1,0:T(8,128)(2,1)}, bf16[576,128]{1,0:T(8,128)(2,1)S(1)}, u32[]{:S(2)}, u32[]{:S(2)}) collective-permute-start(bf16[576,128]{1,0:T(8,128)(2,1)} %bitcast.17), channel_id=1, source_target_pairs={{0,4},{1,5},{2,6},{3,7},{4,0},{5,1},{6,2},{7,3},{8,12},{9,13},{10,... | collective-permute-start | bytes 442376 | tf_op jit(solution)/shard_map/ppermute | solution.py:551
  6.3 16.7 %collective-permute-start.4 = (bf16[576,128]{1,0:T(8,128)(2,1)}, bf16[576,128]{1,0:T(8,128)(2,1)S(1)}, u32[]{:S(2)}, u32[]{:S(2)}) collective-permute-start(bf16[576,128]{1,0:T(8,128)(2,1)} %bitcast.18), channel_id=1, source_target_pairs={{0,6},{1,7},{2,4},{3,5},{4,2},{5,3},{6,0},{7,1},{8,14},{9,15},{10,... | collective-permute-start | bytes 442376 | tf_op jit(solution)/shard_map/ppermute | solution.py:551
  10.8 12.2 %collective-permute-start.1 = (bf16[512,128]{1,0:T(8,128)(2,1)S(1)}, bf16[512,128]{1,0:T(8,128)(2,1)S(1)}, u32[]{:S(2)}, u32[]{:S(2)}) collective-permute-start(bf16[512,128]{1,0:T(8,128)(2,1)S(1)} %constant_dynamic-update-slice_fusion), channel_id=1, source_target_pairs={{0,0},{1,1},{2,8},{3,9},{4,16},{5,17},{6,24},{7,25},{8,2},{9,3},{1... | collective-permute-start | bytes 393224 | tf_op jit(solution)/shard_map/ppermute | solution.py:631
  11.5 11.5 %collective-permute-start.5 = (bf16[512,128]{1,0:T(8,128)(2,1)S(1)}, bf16[512,128]{1,0:T(8,128)(2,1)S(1)}, u32[]{:S(2)}, u32[]{:S(2)}) collective-permute-start(bf16[512,128]{1,0:T(8,128)(2,1)S(1)} %constant_dynamic-update-slice_fusion), channel_id=1, source_target_pairs={{0,2},{1,3},{2,10},{3,11},{4,18},{5,19},{6,26},{7,27},{8,4},{9,5},... | collective-permute-start | bytes 393224 | tf_op jit(solution)/shard_map/ppermute | solution.py:631
  13.7 9.3 %collective-permute-start.6 = (bf16[512,128]{1,0:T(8,128)(2,1)S(1)}, bf16[512,128]{1,0:T(8,128)(2,1)S(1)}, u32[]{:S(2)}, u32[]{:S(2)}) collective-permute-start(bf16[512,128]{1,0:T(8,128)(2,1)S(1)} %constant_dynamic-update-slice_fusion), channel_id=1, source_target_pairs={{0,4},{1,5},{2,12},{3,13},{4,20},{5,21},{6,28},{7,29},{8,6},{9,7},... | collective-permute-start | bytes 393224 | tf_op jit(solution)/shard_map/ppermute | solution.py:631
  28.5 14.9 %collective-permute-start.8 = (bf16[392,512]{1,0:T(8,128)(2,1)S(1)}, bf16[392,512]{1,0:T(8,128)(2,1)S(1)}, u32[]{:S(2)}, u32[]{:S(2)}) collective-permute-start(bf16[392,512]{1,0:T(8,128)(2,1)S(1)} %get-tuple-element.97), channel_id=1, source_target_pairs={{0,8},{8,0},{16,24},{24,16},{1,9},{9,1},{17,25},{25,17},{2,10},{10... | collective-permute-start | bytes 1204232 | tf_op jit(solution)/shard_map/ppermute | solution.py:543
  29.9 15.3 %collective-permute-start.10 = (bf16[392,512]{1,0:T(8,128)(2,1)S(1)}, bf16[392,512]{1,0:T(8,128)(2,1)S(1)}, u32[]{:S(2)}, u32[]{:S(2)}) collective-permute-start(bf16[392,512]{1,0:T(8,128)(2,1)S(1)} %add_convert_fusion.1), channel_id=1, source_target_pairs={{0,16},{8,24},{16,0},{24,8},{1,17},{9,25},{17,1},{25,9},{2,18},{10... | collective-permute-start | bytes 1204232 | tf_op jit(solution)/shard_map/ppermute | solution.py:547
  37.1 15.2 %collective-permute-start.11 = (bf16[2304,128]{1,0:T(8,128)(2,1)S(1)}, bf16[2304,128]{1,0:T(8,128)(2,1)S(1)}, u32[]{:S(2)}, u32[]{:S(2)}) collective-permute-start(bf16[2304,128]{1,0:T(8,128)(2,1)S(1)} %constant_dynamic-update-slice_fusion.2.near), channel_id=1, source_target_pairs={{0,1},{1,0},{2,3},{3,2},{4,5},{5,4},{6,7},{7,6},{8,9},{9,8},{10,11... | collective-permute-start | bytes 1769480 | tf_op jit(solution)/shard_map/ppermute | solution.py:551
  45.4 18.0 %collective-permute-start.20 = (bf16[392,512]{1,0:T(8,128)(2,1)S(1)}, bf16[392,512]{1,0:T(8,128)(2,1)S(1)}, u32[]{:S(2)}, u32[]{:S(2)}) collective-permute-start(bf16[392,512]{1,0:T(8,128)(2,1)S(1)} %get-tuple-element.106.pre0.first_pre.p0), channel_id=1, source_target_pairs={{0,16},{8,24},{16,0},{24,8},{1,17},{9,25},{17,1},{25,9},{2,18},{10... | collective-permute-start | bytes 1204232 | tf_op jit(solution)/shard_map/ppermute | solution.py:547
  72.2 13.8 %collective-permute-start.27 = (bf16[4,392,128]{2,1,0:T(8,128)(2,1)S(1)}, bf16[4,392,128]{2,1,0:T(8,128)(2,1)S(1)}, u32[]{:S(2)}, u32[]{:S(2)}) collective-permute-start(bf16[4,392,128]{2,1,0:T(8,128)(2,1)S(1)} %get-tuple-element.112.src0.pre), channel_id=1, source_target_pairs={{0,16},{8,24},{16,0},{24,8},{1,17},{9,25},{17,1},{25,9},{2,18},{10... | collective-permute-start | bytes 1204232 | tf_op jit(solution)/shard_map/ppermute | solution.py:547
  87.7 31.5 %collective-permute-start.30 = (bf16[512,1152]{1,0:T(8,128)(2,1)S(1)}, bf16[512,1152]{1,0:T(8,128)(2,1)S(1)}, u32[]{:S(2)}, u32[]{:S(2)}) collective-permute-start(bf16[512,1152]{1,0:T(8,128)(2,1)S(1)} %gather_middle.1.weight.w0), channel_id=1, source_target_pairs={{0,16},{8,24},{16,0},{24,8},{1,17},{9,25},{17,1},{25,9},{2,18},{10... | collective-permute-start | bytes 3538952 | tf_op jit(solution)/shard_map/ppermute | solution.py:547
  118.7 14.5 %collective-permute-start.34 = (bf16[512,1152]{1,0:T(8,128)(2,1)S(1)}, bf16[512,1152]{1,0:T(8,128)(2,1)S(1)}, u32[]{:S(2)}, u32[]{:S(2)}) collective-permute-start(bf16[512,1152]{1,0:T(8,128)(2,1)S(1)} %gather_middle.1.weight.w0), channel_id=1, source_target_pairs={{0,8},{8,0},{16,24},{24,16},{1,9},{9,1},{17,25},{25,17},{2,10},{10... | collective-permute-start | bytes 3538952 | tf_op jit(solution)/shard_map/ppermute | solution.py:543
  119.2 14.0 %collective-permute-start.35 = (bf16[512,1152]{1,0:T(8,128)(2,1)S(1)}, bf16[512,1152]{1,0:T(8,128)(2,1)S(1)}, u32[]{:S(2)}, u32[]{:S(2)}) collective-permute-start(bf16[512,1152]{1,0:T(8,128)(2,1)S(1)} %collective-permute-done.30.w2), channel_id=1, source_target_pairs={{0,8},{8,0},{16,24},{24,16},{1,9},{9,1},{17,25},{25,17},{2,10},{10... | collective-permute-start | bytes 3538952 | tf_op jit(solution)/shard_map/ppermute | solution.py:543
  119.2 11.3 %collective-permute-start.32 = (bf16[392,512]{1,0:T(8,128)(2,1)S(1)}, bf16[392,512]{1,0:T(8,128)(2,1)S(1)}, u32[]{:S(2)}, u32[]{:S(2)}) collective-permute-start(bf16[392,512]{1,0:T(8,128)(2,1)S(1)} %get-tuple-element.131), channel_id=1, source_target_pairs={{0,8},{8,0},{16,24},{24,16},{1,9},{9,1},{17,25},{25,17},{2,10},{10... | collective-permute-start | bytes 1204232 | tf_op jit(solution)/shard_map/ppermute | solution.py:543
  120.6 11.4 %collective-permute-start.33 = (bf16[392,512]{1,0:T(8,128)(2,1)S(1)}, bf16[392,512]{1,0:T(8,128)(2,1)S(1)}, u32[]{:S(2)}, u32[]{:S(2)}) collective-permute-start(bf16[392,512]{1,0:T(8,128)(2,1)S(1)} %add_convert_fusion), channel_id=1, source_target_pairs={{0,16},{8,24},{16,0},{24,8},{1,17},{9,25},{17,1},{25,9},{2,18},{10... | collective-permute-start | bytes 1204232 | tf_op jit(solution)/shard_map/ppermute | solution.py:547
  132.7 11.2 %collective-permute-start.37 = (bf16[2,392,128]{2,1,0:T(8,128)(2,1)S(1)}, bf16[2,392,128]{2,1,0:T(8,128)(2,1)S(1)}, u32[]{:S(2)}, u32[]{:S(2)}) collective-permute-start(bf16[2,392,128]{2,1,0:T(8,128)(2,1)S(1)} %get-tuple-element.144), channel_id=1, source_target_pairs={{0,16},{8,24},{16,0},{24,8},{1,17},{9,25},{17,1},{25,9},{2,18},{10... | collective-permute-start | bytes 602120 | tf_op jit(solution)/shard_map/ppermute | solution.py:547
  148.5 15.3 %collective-permute-start.47 = (bf16[392,512]{1,0:T(8,128)(2,1)S(1)}, bf16[392,512]{1,0:T(8,128)(2,1)S(1)}, u32[]{:S(2)}, u32[]{:S(2)}) collective-permute-start(bf16[392,512]{1,0:T(8,128)(2,1)S(1)} %get-tuple-element.150.g0), channel_id=1, source_target_pairs={{0,16},{8,24},{16,0},{24,8},{1,17},{9,25},{17,1},{25,9},{2,18},{10... | collective-permute-start | bytes 1204232 | tf_op jit(solution)/shard_map/ppermute | solution.py:547
  155.7 15.3 %collective-permute-start.52 = (bf16[256,1152]{1,0:T(8,128)(2,1)S(1)}, bf16[256,1152]{1,0:T(8,128)(2,1)S(1)}, u32[]{:S(2)}, u32[]{:S(2)}) collective-permute-start(bf16[256,1152]{1,0:T(8,128)(2,1)S(1)} %get-tuple-element.152), channel_id=1, source_target_pairs={{0,1},{1,0},{2,3},{3,2},{4,5},{5,4},{6,7},{7,6},{8,9},{9,8},{10,11... | collective-permute-start | bytes 1769480 | tf_op jit(solution)/shard_map/ppermute | solution.py:551
  173.1 19.6 %collective-permute-start.53 = (bf16[256,512]{1,0:T(8,128)(2,1)S(1)}, bf16[256,512]{1,0:T(8,128)(2,1)S(1)}, u32[]{:S(2)}, u32[]{:S(2)}) collective-permute-start(bf16[256,512]{1,0:T(8,128)(2,1)S(1)} %get-tuple-element.157), channel_id=1, source_target_pairs={{0,1},{1,0},{2,3},{3,2},{4,5},{5,4},{6,7},{7,6},{8,9},{9,8},{10,11... | collective-permute-start | bytes 786440 | tf_op jit(solution)/shard_map/ppermute | solution.py:551
  174.7 9.9 %collective-permute-start.54 = (bf16[64,1664]{1,0:T(8,128)(2,1)S(1)}, bf16[64,1664]{1,0:T(8,128)(2,1)S(1)}, u32[]{:S(2)}, u32[]{:S(2)}) collective-permute-start(bf16[64,1664]{1,0:T(8,128)(2,1)S(1)} %get-tuple-element.160), channel_id=1, source_target_pairs={{0,2},{1,3},{2,0},{3,1},{4,6},{5,7},{6,4},{7,5},{8,10},{9,11},{10,... | collective-permute-start | bytes 638984 | tf_op jit(solution)/shard_map/ppermute | solution.py:551
  175.2 17.6 %collective-permute-start.55 = (bf16[64,1664]{1,0:T(8,128)(2,1)S(1)}, bf16[64,1664]{1,0:T(8,128)(2,1)S(1)}, u32[]{:S(2)}, u32[]{:S(2)}) collective-permute-start(bf16[64,1664]{1,0:T(8,128)(2,1)S(1)} %get-tuple-element.161), channel_id=1, source_target_pairs={{0,4},{1,5},{2,6},{3,7},{4,0},{5,1},{6,2},{7,3},{8,12},{9,13},{10,... | collective-permute-start | bytes 638984 | tf_op jit(solution)/shard_map/ppermute | solution.py:551
  175.9 27.3 %collective-permute-start.60 = (bf16[64,1664]{1,0:T(8,128)(2,1)S(1)}, bf16[64,1664]{1,0:T(8,128)(2,1)S(1)}, u32[]{:S(2)}, u32[]{:S(2)}) collective-permute-start(bf16[64,1664]{1,0:T(8,128)(2,1)S(1)} %get-tuple-element.170), channel_id=1, source_target_pairs={{0,6},{1,7},{2,4},{3,5},{4,2},{5,3},{6,0},{7,1},{8,14},{9,15},{10,... | collective-permute-start | bytes 638984 | tf_op jit(solution)/shard_map/ppermute | solution.py:551
  192.9 9.7 %collective-permute-start.58 = (bf16[256,128]{1,0:T(8,128)(2,1)S(1)}, bf16[256,128]{1,0:T(8,128)(2,1)S(1)}, u32[]{:S(2)}, u32[]{:S(2)}) collective-permute-start(bf16[256,128]{1,0:T(8,128)(2,1)S(1)} %get-tuple-element.165), channel_id=1, source_target_pairs={{4,0},{5,1},{12,2},{13,3},{20,4},{21,5},{28,6},{29,7},{6,8},{7,9},... | collective-permute-start | bytes 196616 | tf_op jit(solution)/shard_map/ppermute | solution.py:778
  (49 other events, 320.6 us)

commit v5 on v4

--- a/solution.py
+++ b/solution.py
@@ -127,17 +127,21 @@
     return total
 
 
+def place_columns(p0, p1, p2, p3, out):
+    z = position()[1]
+    for j, piece in enumerate((p0, p1, p2, p3)):
+        out[:, lane_block((z - j) & 3)] = piece[...]
+
+
 def first_product(x, *refs):
     pieces, (w_first, send_far, own_far, send_near, own_near) = refs[:-5], refs[-5:]
     n, z, y = position()
     if len(pieces) == 1:
         w_first[...] = pieces[0][...]
     else:
-        rows = pieces[0].shape[0] // 2
-        for j, piece in enumerate(pieces):
-            for dy in range(2):
-                here = pl.ds(pl.multiple_of((y ^ dy) * rows, rows), rows)
-                w_first[here, lane_block((z - j) & 3)] = piece[dy * rows : (dy + 1) * rows, :]
+        rows = pieces[0].shape[0]
+        for dy, piece in enumerate(pieces):
+            w_first[pl.ds(pl.multiple_of((y ^ dy) * rows, rows), rows), :] = piece[...]
     for ref, m in ((send_far, 3), (own_far, 2), (send_near, 1), (own_near, 0)):
         ref[...] = dot(x[n ^ m], w_first[...]).astype(ref.dtype)
 
@@ -260,7 +264,6 @@
         )
         for k, row in enumerate((mean, scale, slope, offset)):
             coef[m, k : k + 1, :] = row
-        back = mean * scale
 
         def body(ds, acc):
             values = pre[m, ds, :]
@@ -271,11 +274,12 @@
             out[b, ds, :] = (inside * value).astype(BF)
             local = inside * cotangent[b, ds, :].astype(F32) * (gate + value * (1.0 - gate))
             grad[m, ds, :] = local
-            return acc[0] + fold(local), acc[1] + fold(local * (values * scale - back))
+            return acc[0] + fold(local), acc[1] + fold(local * values)
 
         sums = by_rows(rows, body, zeros_acc(channels))
-        message[0, 2 * m : 2 * m + 1, :] = column_sum(sums[0])
-        message[0, 2 * m + 1 : 2 * m + 2, :] = column_sum(sums[1])
+        first, second = column_sum(sums[0]), column_sum(sums[1])
+        message[0, 2 * m : 2 * m + 1, :] = first
+        message[0, 2 * m + 1 : 2 * m + 2, :] = scale * (second - mean * first)
     repeat_first(message)
 
 
@@ -391,11 +395,10 @@
         level, tilt = level - mean * scale * tilt, scale * tilt
         away = mask[b] * (level + pre[...].astype(F32) * tilt)
         grad_pre[m] = (slope * (g[...].astype(F32) - away)).astype(BF)
-        product = dot_tn(x[b], grad_pre[m])
-        if m == 0:
-            acc[...] = product
-        else:
-            acc[...] += product
+    total = dot_tn(x[n], grad_pre[0])
+    for m in range(1, NARROW):
+        total = total + dot_tn(x[n ^ m], grad_pre[m])
+    acc[...] = total
     if len(outs) == 1:
         outs[0][...] = acc[...]
     else:
@@ -442,13 +445,11 @@
 
 def middle_weight(hidden, q0, q1, far, last, pre, sum0, sum1, sum2, sum3, norm, params, mask, to_canvas,
                   level_sum, tilt_sum, *refs):
-    outs, (acc, shifted, canvas) = refs[:-3], refs[-3:]
+    outs, (acc, shifted, canvases) = refs[:-3], refs[-3:]
     n = position()[0]
     places = to_canvas.shape[0]
     img = places // (SIDE * PITCH)
     margin = img * (PITCH + 1)
-    canvas[0:margin, :] = jnp.zeros((margin, 128), F32)
-    canvas[margin + places :, :] = jnp.zeros((margin, 128), F32)
     norms = total_of(norm, n)
     blocks = (sum0[...], sum1[...], sum2[...], sum3[...])
     every = blocks[0] + blocks[1] + blocks[2] + blocks[3]
@@ -466,15 +467,15 @@
         level, tilt = level - mean * scale * tilt, scale * tilt
         away = mask[b] * (level + pre[m].astype(F32) * tilt)
         grad_pre = (slope * (piece.astype(F32) - away)).astype(BF)
+        canvas = canvases.at[m]
+        canvas[0:margin, :] = jnp.zeros((margin, 128), F32)
+        canvas[margin + places :, :] = jnp.zeros((margin, 128), F32)
         canvas[margin : margin + places, :] = dot(to_canvas[...], grad_pre)
         for tap in range(TAPS):
             start = margin - ((tap // 3 - 1) * PITCH + tap % 3 - 1) * img
-            shifted[:, 128 * tap : 128 * tap + 128] = canvas[start : start + places, :].astype(BF)
-        product = dot_tn(hidden[m], shifted[...])
-        if m == 0:
-            acc[...] = product
-        else:
-            acc[...] += product
+            here = slice(m * places, (m + 1) * places)
+            shifted[here, 128 * tap : 128 * tap + 128] = canvas[start : start + places, :].astype(BF)
+    acc[...] = dot_tn(hidden[...].reshape(NARROW * places, hidden.shape[2]), shifted[...])
     hand_out(acc, outs)
 
 
@@ -627,9 +628,9 @@
         share = w_last.shape[0]
         packed = w_middle.reshape(TAPS * share, 128)
         middle_near = [packed] + [swap_wide(packed, 2 * j, wide) for j in range(1, 4)]
-        first_pair = jnp.concatenate([w_first, swap_wide(w_first, 1, wide)], axis=0)
-        first_pieces = [lax.ppermute(first_pair, MESH, pairs) for pairs in steps]
-        first_pieces[0] = after(first_pieces[0], *middle_near)
+        first_pieces = [lax.ppermute(w_first, MESH, pairs) for pairs in steps]
+        first_half = run(place_columns, first_pieces, [arr((w_first.shape[0], mid), BF)])[0]
+        first_pieces = [first_half, swap_wide(first_half, 1, wide)]
     else:
         first_all = lax.all_gather(lax.all_gather(w_first, "narrow", axis=1, tiled=True), "wide", axis=0, tiled=True)
         first_pieces = [lax.dynamic_slice_in_dim(first_all, n * low, low, 0)]
@@ -652,14 +653,14 @@
         first_product, (inputs, *first_pieces),
         [arr((low, mid), BF), flat, flat32, flat, flat32], flops=2 * micro * rows * low * mid,
     )
-    joined, begun = reduce_narrow(send_far, own_far, send_near, own_near)
+    joined, begun = reduce_narrow(send_far, own_far, send_near, own_near, *(middle_near[:2] if direct else ()))
     if direct:
         middle_near = jnp.concatenate([after(middle_near[0], begun)] + middle_near[1:], axis=0)
         middle_far = swap_wide(middle_near, 1, wide)
     mask = mask_of(after(sides, begun))
     beside = ()
     if direct:
-        held = after(w_last, mask)
+        held = after(w_last, middle_near)
         last_near = jnp.concatenate([held] + [swap_wide(held, 2 * j, wide) for j in range(1, 4)], axis=0)
         beside = (middle_far, last_near)
     pre_one, message = run(first_join, (*joined, mask, small), [flat, arr((16, 128), F32)])
@@ -743,8 +744,8 @@
         middle_weight,
         (hidden_one, own_q, got_near, got_far, got_last, pre_two, *sums_five, parts_two, params, mask, to_canvas),
         [row, row, *handed(TAPS * 128)],
-        [pltpu.VMEM((mid, TAPS * 128), F32), pltpu.VMEM((places, TAPS * 128), BF),
-         pltpu.VMEM((places + 2 * img * (PITCH + 1), 128), F32)],
+        [pltpu.VMEM((mid, TAPS * 128), F32), pltpu.VMEM((micro * places, TAPS * 128), BF),
+         pltpu.VMEM((micro, places + 2 * img * (PITCH + 1), 128), F32)],
         flops=2 * micro * places * mid * TAPS * 128,
     )
     begun, total = sum_wide(message, wide, beside=middle_sum)

time: 207 us -> 199 us (0.961)
  waiting for transfers between devices: 57.9 us -> 52.4 us
  starting transfers between devices: 64.8 us -> 62.6 us
    ppermute x23, waiting for transfers between devices: 41.7 us -> 34.7 us  [swap_wide(): return lax.ppermute(values, 'wide', [(i, i ^ step) for i in range(wide)])]
    ppermute x10, starting transfers between devices: 17.3 us -> 11.5 us  [swap_chip(): return lax.ppermute(values, 'narrow', [(i, i ^ 2) for i in range(NARROW)])]
    ppermute x4, starting transfers between devices: 6.12 us -> 11 us  [on_device(): first_pieces = [lax.ppermute(w_first, MESH, pairs) for pairs in steps]]
    pallas_call x22 -> x23, Pallas kernels: 32.2 us -> 31.5 us  [run(): pl.pallas_call(kernel, out_shape=outs, name=kernel.__name__, in_specs=[pl...]
  transfers between devices with their start and end apart: 61 -> 61, of which waited for: 26 -> 26; matrix products, arithmetic and copies ran while one was open for 3% -> 3% of each run, Pallas kernels for 11% -> 12%
where the time goes in v5:
time: 199 us; the launch traced here: 196 us
  starting transfers between devices  62.6 us (31%)
  waiting for transfers between devices  52.4 us (26%)
  blocking collectives  41.1 us (21%)
  Pallas kernels  31.5 us (16%)
  other arithmetic  4.21 us (2%)
  local copies, waits for them, and re-layouts  3.01 us (2%)
    ppermute x23, waiting for transfers between devices, swap_wide(): return lax.ppermute(values, 'wide', [(i, i ^ step) for i in range(wide)])  34.7 us
    ppermute x23, starting transfers between devices, swap_wide(): return lax.ppermute(values, 'wide', [(i, i ^ step) for i in range(wide)])  31.9 us
    pallas_call x23, Pallas kernels, run(): pl.pallas_call(kernel, out_shape=outs, name=kernel.__name__, in_specs=[pl...  31.5 us
    all_to_all x1, blocking collectives, exchange(): return lax.all_to_all(message, ('wide', 'narrow'), 0, 0, tiled=True)  12 us
    ppermute x10, starting transfers between devices, swap_chip(): return lax.ppermute(values, 'narrow', [(i, i ^ 2) for i in range(NARROW)])  11.5 us
    ppermute x4, starting transfers between devices, on_device(): first_pieces = [lax.ppermute(w_first, MESH, pairs) for pairs in steps]  11 us
    all_to_all x1, blocking collectives, on_device(): parts_three = lax.all_to_all(message, 'wide', 0, 0, tiled=True)  10.3 us
    all_to_all x1, blocking collectives, on_device(): parts_four = lax.all_to_all(message, 'wide', 0, 0, tiled=True)  9.77 us
  transfers between devices with their start and end apart: 61, of which 26 were waited for; matrix products, arithmetic and copies ran while one was open for 3% of the time, Pallas kernels for 12%

profile of v5, /device:TPU:0, one launch (start us, length us, event | category | flops | bytes accessed | tf_op | source)
XLA Modules:
  0.0 195.9 jit_solution(6887355881981513161)
XLA Ops:
  2.1 3.5 %collective-permute-start.1 = (bf16[256,128]{1,0:T(8,128)(2,1)}, bf16[256,128]{1,0:T(8,128)(2,1)S(1)}, u32[]{:S(2)}, u32[]{:S(2)}) collective-permute-start(bf16[256,128]{1,0:T(8,128)(2,1)} %param.14), channel_id=1, source_target_pairs={{0,2},{1,3},{2,10},{3,11},{4,18},{5,19},{6,26},{7,27},{8,4},{9,5},... | collective-permute-start | bytes 196616 | tf_op jit(solution)/shard_map/ppermute | solution.py:631
  5.7 3.4 %collective-permute-start.2 = (bf16[256,128]{1,0:T(8,128)(2,1)}, bf16[256,128]{1,0:T(8,128)(2,1)S(1)}, u32[]{:S(2)}, u32[]{:S(2)}) collective-permute-start(bf16[256,128]{1,0:T(8,128)(2,1)} %param.14), channel_id=1, source_target_pairs={{0,4},{1,5},{2,12},{3,13},{4,20},{5,21},{6,28},{7,29},{8,6},{9,7},... | collective-permute-start | bytes 196616 | tf_op jit(solution)/shard_map/ppermute | solution.py:631
  9.0 2.6 %collective-permute-start.3 = (bf16[256,128]{1,0:T(8,128)(2,1)}, bf16[256,128]{1,0:T(8,128)(2,1)S(1)}, u32[]{:S(2)}, u32[]{:S(2)}) collective-permute-start(bf16[256,128]{1,0:T(8,128)(2,1)} %param.14), channel_id=1, source_target_pairs={{0,6},{1,7},{2,14},{3,15},{4,22},{5,23},{6,30},{7,31},{8,0},{9,1},... | collective-permute-start | bytes 196616 | tf_op jit(solution)/shard_map/ppermute | solution.py:631
  17.2 3.1 %collective-permute-start.9 = (bf16[576,128]{1,0:T(8,128)(2,1)}, bf16[576,128]{1,0:T(8,128)(2,1)S(1)}, u32[]{:S(2)}, u32[]{:S(2)}) collective-permute-start(bf16[576,128]{1,0:T(8,128)(2,1)} %bitcast.17), channel_id=1, source_target_pairs={{0,4},{1,5},{2,6},{3,7},{4,0},{5,1},{6,2},{7,3},{8,12},{9,13},{10,... | collective-permute-start | bytes 442376 | tf_op jit(solution)/shard_map/ppermute | solution.py:552
  32.2 2.5 %collective-permute-start.12 = (bf16[64,512]{1,0:T(8,128)(2,1)S(1)}, bf16[64,512]{1,0:T(8,128)(2,1)S(1)}, u32[]{:S(2)}, u32[]{:S(2)}) collective-permute-start(bf16[64,512]{1,0:T(8,128)(2,1)S(1)} %copy-done.6), channel_id=1, source_target_pairs={{0,2},{1,3},{2,0},{3,1},{4,6},{5,7},{6,4},{7,5},{8,10},{9,11},{10,... | collective-permute-start | bytes 196616 | tf_op jit(solution)/shard_map/ppermute | solution.py:552
  45.8 2.6 %collective-permute-start.16 = (f32[16,128]{1,0:T(8,128)S(1)}, f32[16,128]{1,0:T(8,128)S(1)}, u32[]{:S(2)}, u32[]{:S(2)}) collective-permute-start(f32[16,128]{1,0:T(8,128)S(1)} %add_tiles.4.refs_0_), channel_id=1, source_target_pairs={{0,2},{1,3},{2,0},{3,1},{4,6},{5,7},{6,4},{7,5},{8,10},{9,11},{10,... | collective-permute-start | bytes 24584 | tf_op jit(solution)/shard_map/ppermute | solution.py:552
  59.6 5.6 %middle_forward.1 = (bf16[4,448,512]{2,1,0:T(8,128)(2,1)S(1)}, bf16[4,392,128]{2,1,0:T(8,128)(2,1)S(1)}, f32[4,8,512]{2,1,0:T(8,128)S(1)}, f32[32,8,128]{2,1,0:T(8,128)S(1)}, f32[4,8,128]{2,1,0:T(8,128)S(1)}) custom-call(bf16[392,512]{1,0:T(8,128)(2,1)S(1)} %get-tuple-element.106.pre0.first_pre.p0, bf16[392,512]{1,0:T(8,128)(2,1)S(1)} %collective-permute-done.19.pre1.p1, ...), custom_call_target="tpu_custom_call" | custom-call | flops 2113929216 | bytes 5976192 | tf_op jit(solution)/shard_map/middle_forward/pallas_call | solution.py:39
  66.3 12.0 %all_to_all.20.parts.norm = f32[32,8,128]{2,1,0:T(8,128)S(1)} all-to-all(f32[32,8,128]{2,1,0:T(8,128)S(1)} %get-tuple-element.111), channel_id=1, replica_groups=mesh['narrow'=4,'wide'=8] {'wide','narrow'}, dimensions={0} | all-to-all | bytes 262144 | tf_op jit(solution)/shard_map/all_to_all | solution.py:540
  83.4 2.3 %last_forward.1 = (bf16[4,392,512]{2,1,0:T(8,128)(2,1)S(1)}, bf16[392,512]{1,0:T(8,128)(2,1)S(1)}, f32[8,512]{1,0:T(8,128)S(1)}, f32[4,392,512]{2,1,0:T(8,128)S(1)}, f32[8,8,512]{2,1,0:T(8,128)S(1)}) custom-call(bf16[4,392,128]{2,1,0:T(8,128)(2,1)S(1)} %get-tuple-element.112.src0.pre, bf16[4,392,128]{2,1,0:T(8,128)(2,1)S(1)} %collective-permute-done.26.src1, ...), custom_call_target="tpu_custom_call" | custom-call | flops 822083584 | bytes 7649408 | tf_op jit(solution)/shard_map/last_forward/pallas_call | solution.py:39
  85.7 10.3 %all_to_all.21.parts = f32[8,8,512]{2,1,0:T(8,128)S(1)} all-to-all(f32[8,8,512]{2,1,0:T(8,128)S(1)} %get-tuple-element.116), channel_id=1, replica_groups=mesh['narrow'=4,'wide'=8] {'wide'}, dimensions={0} | all-to-all | bytes 262144 | tf_op jit(solution)/shard_map/all_to_all | solution.py:694
  96.0 3.4 %block_output.1 = (bf16[4,392,512]{2,1,0:T(8,128)(2,1)}, f32[4,392,512]{2,1,0:T(8,128)S(1)}, f32[4,8,512]{2,1,0:T(8,128)S(1)}, f32[8,8,512]{2,1,0:T(8,128)S(1)}) custom-call(f32[4,392,512]{2,1,0:T(8,128)S(1)} %get-tuple-element.115.pre, bf16[4,392,512]{2,1,0:T(8,128)(2,1)S(1)} %copy-done.1, bf16[4,392,512]{2,1,0:T(8,128)(2,1)S(1)} %copy-done.2, ...), custom_call_target="tpu_custom_call" | custom-call | bytes 11593856 | tf_op jit(solution)/shard_map/block_output/pallas_call | solution.py:39
  99.4 9.8 %all_to_all.22.parts = f32[8,8,512]{2,1,0:T(8,128)S(1)} all-to-all(f32[8,8,512]{2,1,0:T(8,128)S(1)} %get-tuple-element.119), channel_id=1, replica_groups=mesh['narrow'=4,'wide'=8] {'wide'}, dimensions={0} | all-to-all | bytes 262144 | tf_op jit(solution)/shard_map/all_to_all | solution.py:700
  115.5 7.9 %collective-permute-done.31.away_last = bf16[256,512]{1,0:T(8,128)(2,1)S(1)} collective-permute-done((bf16[256,512]{1,0:T(8,128)(2,1)S(1)}, bf16[256,512]{1,0:T(8,128)(2,1)S(1)}, u32[]{:S(2)}, u32[]{:S(2)}) %collective-permute-start.31) | collective-permute-done | bytes 262176 | tf_op jit(solution)/shard_map/ppermute | solution.py:552
  126.0 9.1 %all_to_all.23.parts = f32[8,8,128]{2,1,0:T(8,128)S(1)} all-to-all(f32[8,8,128]{2,1,0:T(8,128)S(1)} %get-tuple-element.136), channel_id=1, replica_groups=mesh['narrow'=4,'wide'=8] {'wide'}, dimensions={0} | all-to-all | bytes 65536 | tf_op jit(solution)/shard_map/all_to_all | solution.py:729
  136.9 4.1 %middle_backward.1 = (bf16[392,512]{1,0:T(8,128)(2,1)S(1)}, f32[8,128]{1,0:T(8,128)S(1)}) custom-call(f32[392,512]{1,0:T(8,128)S(1)} %get-tuple-element.134.grad, bf16[392,512]{1,0:T(8,128)(2,1)S(1)} %get-tuple-element.132.pre, f32[8,8,128]{2,1,0:T(8,128)S(1)} %all_to_all.23.parts, f32[4,8,128]{2,1,0:T(8,128)S(1)} %get-tuple-element.153.params, ...), custom_call_target="tpu_custom_call" | custom-call | flops 2113929216 | bytes 7569536 | tf_op jit(solution)/shard_map/middle_backward/pallas_call | solution.py:39
  143.4 4.0 %middle_weight.1 = (f32[1,128]{1,0:T(1,128)}, f32[1,128]{1,0:T(1,128)}, f32[256,1152]{1,0:T(8,128)S(1)}, bf16[256,1152]{1,0:T(8,128)(2,1)S(1)}) custom-call(bf16[4,448,512]{2,1,0:T(8,128)(2,1)S(1)} %get-tuple-element.141.hidden, bf16[392,128]{1,0:T(8,128)(2,1)S(1)} %get-tuple-element.142.q0, bf16[392,128]{1,0:T(8,128)(2,1)S(1)} %collective-permute-done.38.q1, ...), custom_call_target="tpu_custom_call" | custom-call | flops 2113929216 | bytes 5130368 | tf_op jit(solution)/shard_map/middle_weight/pallas_call | solution.py:39
  150.1 3.3 %collective-permute-start.45 = (f32[8,128]{1,0:T(8,128)S(1)}, f32[8,128]{1,0:T(8,128)S(1)}, u32[]{:S(2)}, u32[]{:S(2)}) collective-permute-start(f32[8,128]{1,0:T(8,128)S(1)} %add_tiles.6.refs_0_), channel_id=1, source_target_pairs={{0,6},{1,7},{2,4},{3,5},{4,2},{5,3},{6,0},{7,1},{8,14},{9,15},{10,... | collective-permute-start | bytes 12296 | tf_op jit(solution)/shard_map/ppermute | solution.py:552
  159.7 3.0 %collective-permute-done.52.away = bf16[256,1152]{1,0:T(8,128)(2,1)S(1)} collective-permute-done((bf16[256,1152]{1,0:T(8,128)(2,1)S(1)}, bf16[256,1152]{1,0:T(8,128)(2,1)S(1)}, u32[]{:S(2)}, u32[]{:S(2)}) %collective-permute-start.52) | collective-permute-done | bytes 589856 | tf_op jit(solution)/shard_map/ppermute | solution.py:552
  167.5 3.3 %collective-permute-start.60 = (bf16[64,1664]{1,0:T(8,128)(2,1)S(1)}, bf16[64,1664]{1,0:T(8,128)(2,1)S(1)}, u32[]{:S(2)}, u32[]{:S(2)}) collective-permute-start(bf16[64,1664]{1,0:T(8,128)(2,1)S(1)} %get-tuple-element.170), channel_id=1, source_target_pairs={{0,6},{1,7},{2,4},{3,5},{4,2},{5,3},{6,0},{7,1},{8,14},{9,15},{10,... | collective-permute-start | bytes 638984 | tf_op jit(solution)/shard_map/ppermute | solution.py:552
  170.8 5.4 %collective-permute-done.54.p1 = bf16[64,1664]{1,0:T(8,128)(2,1)S(1)} collective-permute-done((bf16[64,1664]{1,0:T(8,128)(2,1)S(1)}, bf16[64,1664]{1,0:T(8,128)(2,1)S(1)}, u32[]{:S(2)}, u32[]{:S(2)}) %collective-permute-start.54) | collective-permute-done | bytes 213024 | tf_op jit(solution)/shard_map/ppermute | solution.py:552
  176.2 8.1 %collective-permute-done.55.p2 = bf16[64,1664]{1,0:T(8,128)(2,1)S(1)} collective-permute-done((bf16[64,1664]{1,0:T(8,128)(2,1)S(1)}, bf16[64,1664]{1,0:T(8,128)(2,1)S(1)}, u32[]{:S(2)}, u32[]{:S(2)}) %collective-permute-start.55) | collective-permute-done | bytes 213024 | tf_op jit(solution)/shard_map/ppermute | solution.py:552
  186.0 2.3 %collective-permute-start.57 = (bf16[256,128]{1,0:T(8,128)(2,1)S(1)}, bf16[256,128]{1,0:T(8,128)(2,1)S(1)}, u32[]{:S(2)}, u32[]{:S(2)}) collective-permute-start(bf16[256,128]{1,0:T(8,128)(2,1)S(1)} %get-tuple-element.164), channel_id=1, source_target_pairs={{2,0},{3,1},{10,2},{11,3},{18,4},{19,5},{26,6},{27,7},{4,8},{5,9},... | collective-permute-start | bytes 196616 | tf_op jit(solution)/shard_map/ppermute | solution.py:779
  188.9 2.7 %input_gradient.1 = f32[4,392,512]{2,1,0:T(8,128)} custom-call(bf16[4,392,512]{2,1,0:T(8,128)(2,1)S(1)} %get-tuple-element.154.grad_pre, bf16[512,512]{1,0:T(8,128)(2,1)S(1)} %get-tuple-element.155.weight, f32[4,392,512]{2,1,0:T(8,128)S(1)} %get-tuple-element.118.grad), custom_call_target="tpu_custom_call" | custom-call | flops 822083584 | bytes 8552448 | tf_op jit(solution)/shard_map/input_gradient/pallas_call | solution.py:39
  191.7 2.7 %collective-permute-done.58 = bf16[256,128]{1,0:T(8,128)(2,1)S(1)} collective-permute-done((bf16[256,128]{1,0:T(8,128)(2,1)S(1)}, bf16[256,128]{1,0:T(8,128)(2,1)S(1)}, u32[]{:S(2)}, u32[]{:S(2)}) %collective-permute-start.58) | collective-permute-done | bytes 65568 | tf_op jit(solution)/shard_map/ppermute | solution.py:779
  (171 shorter events, 78.0 us)
Async XLA Ops:
  0.6 11.0 %collective-permute-start = (bf16[256,128]{1,0:T(8,128)(2,1)}, bf16[256,128]{1,0:T(8,128)(2,1)S(1)}, u32[]{:S(2)}, u32[]{:S(2)}) collective-permute-start(bf16[256,128]{1,0:T(8,128)(2,1)} %param.14), channel_id=1, source_target_pairs={{0,0},{1,1},{2,8},{3,9},{4,16},{5,17},{6,24},{7,25},{8,2},{9,3},{1... | collective-permute-start | bytes 196616 | tf_op jit(solution)/shard_map/ppermute | solution.py:631
  2.1 9.5 %collective-permute-start.1 = (bf16[256,128]{1,0:T(8,128)(2,1)}, bf16[256,128]{1,0:T(8,128)(2,1)S(1)}, u32[]{:S(2)}, u32[]{:S(2)}) collective-permute-start(bf16[256,128]{1,0:T(8,128)(2,1)} %param.14), channel_id=1, source_target_pairs={{0,2},{1,3},{2,10},{3,11},{4,18},{5,19},{6,26},{7,27},{8,4},{9,5},... | collective-permute-start | bytes 196616 | tf_op jit(solution)/shard_map/ppermute | solution.py:631
  15.6 13.1 %collective-permute-start.7 = (bf16[576,128]{1,0:T(8,128)(2,1)}, bf16[576,128]{1,0:T(8,128)(2,1)S(1)}, u32[]{:S(2)}, u32[]{:S(2)}) collective-permute-start(bf16[576,128]{1,0:T(8,128)(2,1)} %bitcast.16), channel_id=1, source_target_pairs={{0,2},{1,3},{2,0},{3,1},{4,6},{5,7},{6,4},{7,5},{8,10},{9,11},{10,... | collective-permute-start | bytes 442376 | tf_op jit(solution)/shard_map/ppermute | solution.py:552
  17.2 14.4 %collective-permute-start.9 = (bf16[576,128]{1,0:T(8,128)(2,1)}, bf16[576,128]{1,0:T(8,128)(2,1)S(1)}, u32[]{:S(2)}, u32[]{:S(2)}) collective-permute-start(bf16[576,128]{1,0:T(8,128)(2,1)} %bitcast.17), channel_id=1, source_target_pairs={{0,4},{1,5},{2,6},{3,7},{4,0},{5,1},{6,2},{7,3},{8,12},{9,13},{10,... | collective-permute-start | bytes 442376 | tf_op jit(solution)/shard_map/ppermute | solution.py:552
  20.3 11.3 %collective-permute-start.10 = (bf16[576,128]{1,0:T(8,128)(2,1)}, bf16[576,128]{1,0:T(8,128)(2,1)S(1)}, u32[]{:S(2)}, u32[]{:S(2)}) collective-permute-start(bf16[576,128]{1,0:T(8,128)(2,1)} %bitcast.18), channel_id=1, source_target_pairs={{0,6},{1,7},{2,4},{3,5},{4,2},{5,3},{6,0},{7,1},{8,14},{9,15},{10,... | collective-permute-start | bytes 442376 | tf_op jit(solution)/shard_map/ppermute | solution.py:552
  26.5 11.8 %collective-permute-start.5 = (bf16[392,512]{1,0:T(8,128)(2,1)}, bf16[392,512]{1,0:T(8,128)(2,1)S(1)}, u32[]{:S(2)}, u32[]{:S(2)}) collective-permute-start(bf16[392,512]{1,0:T(8,128)(2,1)} %get-tuple-element.96), channel_id=1, source_target_pairs={{0,8},{8,0},{16,24},{24,16},{1,9},{9,1},{17,25},{25,17},{2,10},{10... | collective-permute-start | bytes 1204232 | tf_op jit(solution)/shard_map/ppermute | solution.py:544
  28.6 11.8 %collective-permute-start.8 = (bf16[392,512]{1,0:T(8,128)(2,1)}, bf16[392,512]{1,0:T(8,128)(2,1)S(1)}, u32[]{:S(2)}, u32[]{:S(2)}) collective-permute-start(bf16[392,512]{1,0:T(8,128)(2,1)} %add_convert_fusion.1), channel_id=1, source_target_pairs={{0,16},{8,24},{16,0},{24,8},{1,17},{9,25},{17,1},{25,9},{2,18},{10... | collective-permute-start | bytes 1204232 | tf_op jit(solution)/shard_map/ppermute | solution.py:548
  31.6 13.9 %collective-permute-start.11 = (bf16[2304,128]{1,0:T(8,128)(2,1)S(1)}, bf16[2304,128]{1,0:T(8,128)(2,1)S(1)}, u32[]{:S(2)}, u32[]{:S(2)}) collective-permute-start(bf16[2304,128]{1,0:T(8,128)(2,1)S(1)} %constant_dynamic-update-slice_fusion.near), channel_id=1, source_target_pairs={{0,1},{1,0},{2,3},{3,2},{4,5},{5,4},{6,7},{7,6},{8,9},{9,8},{10,11... | collective-permute-start | bytes 1769480 | tf_op jit(solution)/shard_map/ppermute | solution.py:552
  32.2 9.9 %collective-permute-start.12 = (bf16[64,512]{1,0:T(8,128)(2,1)S(1)}, bf16[64,512]{1,0:T(8,128)(2,1)S(1)}, u32[]{:S(2)}, u32[]{:S(2)}) collective-permute-start(bf16[64,512]{1,0:T(8,128)(2,1)S(1)} %copy-done.6), channel_id=1, source_target_pairs={{0,2},{1,3},{2,0},{3,1},{4,6},{5,7},{6,4},{7,5},{8,10},{9,11},{10,... | collective-permute-start | bytes 196616 | tf_op jit(solution)/shard_map/ppermute | solution.py:552
  40.7 15.1 %collective-permute-start.20 = (bf16[392,512]{1,0:T(8,128)(2,1)S(1)}, bf16[392,512]{1,0:T(8,128)(2,1)S(1)}, u32[]{:S(2)}, u32[]{:S(2)}) collective-permute-start(bf16[392,512]{1,0:T(8,128)(2,1)S(1)} %get-tuple-element.106.pre0.first_pre.p0), channel_id=1, source_target_pairs={{0,16},{8,24},{16,0},{24,8},{1,17},{9,25},{17,1},{25,9},{2,18},{10... | collective-permute-start | bytes 1204232 | tf_op jit(solution)/shard_map/ppermute | solution.py:548
  65.2 13.1 %collective-permute-start.27 = (bf16[4,392,128]{2,1,0:T(8,128)(2,1)S(1)}, bf16[4,392,128]{2,1,0:T(8,128)(2,1)S(1)}, u32[]{:S(2)}, u32[]{:S(2)}) collective-permute-start(bf16[4,392,128]{2,1,0:T(8,128)(2,1)S(1)} %get-tuple-element.112.src0.pre), channel_id=1, source_target_pairs={{0,16},{8,24},{16,0},{24,8},{1,17},{9,25},{17,1},{25,9},{2,18},{10... | collective-permute-start | bytes 1204232 | tf_op jit(solution)/shard_map/ppermute | solution.py:548
  80.1 31.7 %collective-permute-start.30 = (bf16[512,1152]{1,0:T(8,128)(2,1)S(1)}, bf16[512,1152]{1,0:T(8,128)(2,1)S(1)}, u32[]{:S(2)}, u32[]{:S(2)}) collective-permute-start(bf16[512,1152]{1,0:T(8,128)(2,1)S(1)} %gather_middle.1.weight.w0), channel_id=1, source_target_pairs={{0,16},{8,24},{16,0},{24,8},{1,17},{9,25},{17,1},{25,9},{2,18},{10... | collective-permute-start | bytes 3538952 | tf_op jit(solution)/shard_map/ppermute | solution.py:548
  111.3 14.7 %collective-permute-start.34 = (bf16[512,1152]{1,0:T(8,128)(2,1)S(1)}, bf16[512,1152]{1,0:T(8,128)(2,1)S(1)}, u32[]{:S(2)}, u32[]{:S(2)}) collective-permute-start(bf16[512,1152]{1,0:T(8,128)(2,1)S(1)} %gather_middle.1.weight.w0), channel_id=1, source_target_pairs={{0,8},{8,0},{16,24},{24,16},{1,9},{9,1},{17,25},{25,17},{2,10},{10... | collective-permute-start | bytes 3538952 | tf_op jit(solution)/shard_map/ppermute | solution.py:544
  111.8 14.2 %collective-permute-start.35 = (bf16[512,1152]{1,0:T(8,128)(2,1)S(1)}, bf16[512,1152]{1,0:T(8,128)(2,1)S(1)}, u32[]{:S(2)}, u32[]{:S(2)}) collective-permute-start(bf16[512,1152]{1,0:T(8,128)(2,1)S(1)} %collective-permute-done.30.w2), channel_id=1, source_target_pairs={{0,8},{8,0},{16,24},{24,16},{1,9},{9,1},{17,25},{25,17},{2,10},{10... | collective-permute-start | bytes 3538952 | tf_op jit(solution)/shard_map/ppermute | solution.py:544
  111.8 11.5 %collective-permute-start.32 = (bf16[392,512]{1,0:T(8,128)(2,1)S(1)}, bf16[392,512]{1,0:T(8,128)(2,1)S(1)}, u32[]{:S(2)}, u32[]{:S(2)}) collective-permute-start(bf16[392,512]{1,0:T(8,128)(2,1)S(1)} %get-tuple-element.131), channel_id=1, source_target_pairs={{0,8},{8,0},{16,24},{24,16},{1,9},{9,1},{17,25},{25,17},{2,10},{10... | collective-permute-start | bytes 1204232 | tf_op jit(solution)/shard_map/ppermute | solution.py:544
  113.1 11.4 %collective-permute-start.33 = (bf16[392,512]{1,0:T(8,128)(2,1)S(1)}, bf16[392,512]{1,0:T(8,128)(2,1)S(1)}, u32[]{:S(2)}, u32[]{:S(2)}) collective-permute-start(bf16[392,512]{1,0:T(8,128)(2,1)S(1)} %add_convert_fusion), channel_id=1, source_target_pairs={{0,16},{8,24},{16,0},{24,8},{1,17},{9,25},{17,1},{25,9},{2,18},{10... | collective-permute-start | bytes 1204232 | tf_op jit(solution)/shard_map/ppermute | solution.py:548
  125.2 11.2 %collective-permute-start.37 = (bf16[2,392,128]{2,1,0:T(8,128)(2,1)S(1)}, bf16[2,392,128]{2,1,0:T(8,128)(2,1)S(1)}, u32[]{:S(2)}, u32[]{:S(2)}) collective-permute-start(bf16[2,392,128]{2,1,0:T(8,128)(2,1)S(1)} %get-tuple-element.144), channel_id=1, source_target_pairs={{0,16},{8,24},{16,0},{24,8},{1,17},{9,25},{17,1},{25,9},{2,18},{10... | collective-permute-start | bytes 602120 | tf_op jit(solution)/shard_map/ppermute | solution.py:548
  141.0 14.5 %collective-permute-start.47 = (bf16[392,512]{1,0:T(8,128)(2,1)S(1)}, bf16[392,512]{1,0:T(8,128)(2,1)S(1)}, u32[]{:S(2)}, u32[]{:S(2)}) collective-permute-start(bf16[392,512]{1,0:T(8,128)(2,1)S(1)} %get-tuple-element.150.g0), channel_id=1, source_target_pairs={{0,16},{8,24},{16,0},{24,8},{1,17},{9,25},{17,1},{25,9},{2,18},{10... | collective-permute-start | bytes 1204232 | tf_op jit(solution)/shard_map/ppermute | solution.py:548
  147.4 15.3 %collective-permute-start.52 = (bf16[256,1152]{1,0:T(8,128)(2,1)S(1)}, bf16[256,1152]{1,0:T(8,128)(2,1)S(1)}, u32[]{:S(2)}, u32[]{:S(2)}) collective-permute-start(bf16[256,1152]{1,0:T(8,128)(2,1)S(1)} %get-tuple-element.152), channel_id=1, source_target_pairs={{0,1},{1,0},{2,3},{3,2},{4,5},{5,4},{6,7},{7,6},{8,9},{9,8},{10,11... | collective-permute-start | bytes 1769480 | tf_op jit(solution)/shard_map/ppermute | solution.py:552
  164.8 19.6 %collective-permute-start.53 = (bf16[256,512]{1,0:T(8,128)(2,1)S(1)}, bf16[256,512]{1,0:T(8,128)(2,1)S(1)}, u32[]{:S(2)}, u32[]{:S(2)}) collective-permute-start(bf16[256,512]{1,0:T(8,128)(2,1)S(1)} %get-tuple-element.157), channel_id=1, source_target_pairs={{0,1},{1,0},{2,3},{3,2},{4,5},{5,4},{6,7},{7,6},{8,9},{9,8},{10,11... | collective-permute-start | bytes 786440 | tf_op jit(solution)/shard_map/ppermute | solution.py:552
  166.3 9.9 %collective-permute-start.54 = (bf16[64,1664]{1,0:T(8,128)(2,1)S(1)}, bf16[64,1664]{1,0:T(8,128)(2,1)S(1)}, u32[]{:S(2)}, u32[]{:S(2)}) collective-permute-start(bf16[64,1664]{1,0:T(8,128)(2,1)S(1)} %get-tuple-element.160), channel_id=1, source_target_pairs={{0,2},{1,3},{2,0},{3,1},{4,6},{5,7},{6,4},{7,5},{8,10},{9,11},{10,... | collective-permute-start | bytes 638984 | tf_op jit(solution)/shard_map/ppermute | solution.py:552
  166.8 17.6 %collective-permute-start.55 = (bf16[64,1664]{1,0:T(8,128)(2,1)S(1)}, bf16[64,1664]{1,0:T(8,128)(2,1)S(1)}, u32[]{:S(2)}, u32[]{:S(2)}) collective-permute-start(bf16[64,1664]{1,0:T(8,128)(2,1)S(1)} %get-tuple-element.161), channel_id=1, source_target_pairs={{0,4},{1,5},{2,6},{3,7},{4,0},{5,1},{6,2},{7,3},{8,12},{9,13},{10,... | collective-permute-start | bytes 638984 | tf_op jit(solution)/shard_map/ppermute | solution.py:552
  167.5 27.5 %collective-permute-start.60 = (bf16[64,1664]{1,0:T(8,128)(2,1)S(1)}, bf16[64,1664]{1,0:T(8,128)(2,1)S(1)}, u32[]{:S(2)}, u32[]{:S(2)}) collective-permute-start(bf16[64,1664]{1,0:T(8,128)(2,1)S(1)} %get-tuple-element.170), channel_id=1, source_target_pairs={{0,6},{1,7},{2,4},{3,5},{4,2},{5,3},{6,0},{7,1},{8,14},{9,15},{10,... | collective-permute-start | bytes 638984 | tf_op jit(solution)/shard_map/ppermute | solution.py:552
  184.5 9.9 %collective-permute-start.58 = (bf16[256,128]{1,0:T(8,128)(2,1)S(1)}, bf16[256,128]{1,0:T(8,128)(2,1)S(1)}, u32[]{:S(2)}, u32[]{:S(2)}) collective-permute-start(bf16[256,128]{1,0:T(8,128)(2,1)S(1)} %get-tuple-element.165), channel_id=1, source_target_pairs={{4,0},{5,1},{12,2},{13,3},{20,4},{21,5},{28,6},{29,7},{6,8},{7,9},... | collective-permute-start | bytes 196616 | tf_op jit(solution)/shard_map/ppermute | solution.py:779
  (49 other events, 301.8 us)

commit v6 on v5

--- a/solution.py
+++ b/solution.py
@@ -406,7 +406,7 @@
         for ref, h in zip(outs, (y, 1 - y)):
             top = pl.multiple_of(h * half, half)
             for j in range(NARROW):
-                block = acc[pl.ds(top, half), lane_block((z - j) & 3)]
+                block = acc[pl.ds(top, half), lane_block(n ^ j)]
                 ref[:, 128 * j : 128 * j + 128] = block.astype(ref.dtype)
     level_sum[...] = row_of(every, 0, n)
     tilt_sum[...] = row_of(every, NARROW, n)
@@ -499,10 +499,26 @@
             out[here, :] = stack[j * rows : (j + 1) * rows, :]
 
 
-def merge_first(own, away, *sends):
+def merge_first(own, away, keep, near, far):
+    parts = [own[:, 128 * i : 128 * i + 128] + away[:, 128 * i : 128 * i + 128].astype(F32) for i in range(NARROW)]
+    keep[...] = parts[0]
+    near[...] = parts[1].astype(BF)
+    far[0] = parts[2].astype(BF)
+    far[1] = parts[3].astype(BF)
+
+
+def sort_first(own, near, far, last, keep, *refs):
+    sends, pieces = refs[:-1], refs[-1]
+    n, z, _ = position()
+    for i, piece in enumerate((own[...], near[...], far[0], last[1])):
+        pieces[i] = piece.astype(F32)
+    keep[...] = pieces[n ^ z]
     for j, send in enumerate(sends):
-        here = slice(128 * j, 128 * j + 128)
-        send[...] = (own[:, here] + away[:, here].astype(F32)).astype(BF)
+        send[...] = pieces[n ^ z ^ (j + 1)].astype(BF)
+
+
+def finish_first(keep, p1, p2, p3, out):
+    out[...] = keep[...] + p1[...].astype(F32) + p2[...].astype(F32) + p3[...].astype(F32)
 
 
 def add_tiles(*refs):
@@ -757,7 +773,7 @@
     out_first = [arr((low // 2, mid), F32), arr((low // 2, mid), BF)] if direct else [arr((low, mid), F32)]
     level_one, tilt_one, grad_pre_one, *first_sum = run(
         first_weight,
-        (*grad_ones, *pre_ones, *sums_six, after(params, got_middle) if direct else params, coef_one, mask, inputs),
+        (*grad_ones, *pre_ones, *sums_six, params, coef_one, mask, inputs),
         [row, row, arr((micro, rows, mid), BF), *out_first], [pltpu.VMEM((low, mid), F32)],
         flops=2 * micro * rows * low * mid,
     )
@@ -767,25 +783,27 @@
     )[0]
 
     if direct:
-        got_first = swap_wide(first_sum[1], 1, wide)
+        got_first = swap_wide(after(first_sum[1], got_middle), 1, wide)
         channels = TAPS * 128
         keep, keep_last, *sends = run(
             merge_wide, (middle_sum[0], after(got_middle, first_sum[1]), last_sum[0], got_last_sum),
             [arr((share, channels), F32), arr((share, low), F32)] + [arr((share, channels + low), BF)] * 3,
         )
         parts = [swap_wide(send, 2 * j + 2, wide) for j, send in enumerate(sends)]
-        sends = run(merge_first, (first_sum[0], after(got_first, *parts[0:2])), [arr((low // 2, cols), BF)] * NARROW)
-        arrived = [
-            lax.ppermute(send, MESH, [(dst, src) for src, dst in pairs]) for send, pairs in zip(sends, steps)
-        ]
+        piece, half = arr((low // 2, cols), BF), arr((low // 2, cols), F32)
+        keep_first, near, far = run(merge_first, (first_sum[0], after(got_first, parts[0])), [half, piece, arr((2, low // 2, cols), BF)])
+        far = after(swap_chip(far), *parts[0:2])
+        keep_first, *sends = run(
+            sort_first, (keep_first, swap_core(near), far, swap_core(far)), [half, piece, piece, piece],
+            [pltpu.VMEM((NARROW, low // 2, cols), F32)],
+        )
+        arrived = [swap_wide(send, 2 * j + 2, wide) for j, send in enumerate(sends)]
+        grad_first = run(finish_first, (keep_first, *arrived), [half])[0]
         grad_middle, grad_last = run(
-            finish_wide, (after(keep, arrived[0]), keep_last, *parts),
+            finish_wide, (keep, keep_last, *parts),
             [arr((TAPS, share, 128), F32), arr((share, low), F32)],
         )
         grad_middle = grad_middle.reshape(3, 3, share, 128)
-        grad_first = arrived[0].astype(F32)
-        for piece in arrived[1:]:
-            grad_first = grad_first + piece.astype(F32)
     else:
         grad_last = lax.psum_scatter(last_sum[0], "wide", scatter_dimension=0, tiled=True)
         grad_middle = lax.psum_scatter(middle_sum[0], "wide", scatter_dimension=0, tiled=True)

time: 199 us -> 193 us (0.970)
  waiting for transfers between devices: 52.4 us -> 46.2 us
    ppermute x23 -> x26, waiting for transfers between devices: 34.7 us -> 26.9 us  [swap_wide(): return lax.ppermute(values, 'wide', [(i, i ^ step) for i in range(wide)])]
    ppermute x4 -> x0, starting transfers between devices: 4.48 us -> none  [on_device(): lax.ppermute(send, MESH, [(dst, src) for src, dst in pairs])]
    ppermute x23 -> x26, starting transfers between devices: 31.9 us -> 36.3 us  [swap_wide(): return lax.ppermute(values, 'wide', [(i, i ^ step) for i in range(wide)])]
    ppermute x4 -> x0, waiting for transfers between devices: 2.72 us -> none  [on_device(): lax.ppermute(send, MESH, [(dst, src) for src, dst in pairs])]
    ppermute x10 -> x11, waiting for transfers between devices: 6.01 us -> 8.21 us  [swap_chip(): return lax.ppermute(values, 'narrow', [(i, i ^ 2) for i in range(NARROW)])]
    ppermute x20 -> x22, waiting for transfers between devices: 6.76 us -> 8.85 us  [swap_core(): return lax.ppermute(values, 'narrow', [(i, i ^ 1) for i in range(NARROW)])]
    ppermute x10 -> x11, starting transfers between devices: 11.5 us -> 12.9 us  [swap_chip(): return lax.ppermute(values, 'narrow', [(i, i ^ 2) for i in range(NARROW)])]
    pallas_call x23 -> x25, Pallas kernels: 31.5 us -> 32.2 us  [run(): pl.pallas_call(kernel, out_shape=outs, name=kernel.__name__, in_specs=[pl...]
  transfers between devices with their start and end apart: 61 -> 63, of which waited for: 26 -> 27; matrix products, arithmetic and copies ran while one was open for 3% -> 3% of each run, Pallas kernels for 12% -> 13%
where the time goes in v6:
time: 193 us; the launch traced here: 191 us
  starting transfers between devices  64.4 us (33%)
  waiting for transfers between devices  46.2 us (24%)
  blocking collectives  41.2 us (21%)
  Pallas kernels  32.2 us (17%)
  other arithmetic  3.52 us (2%)
  local copies, waits for them, and re-layouts  3.01 us (2%)
    ppermute x26, starting transfers between devices, swap_wide(): return lax.ppermute(values, 'wide', [(i, i ^ step) for i in range(wide)])  36.3 us
    pallas_call x25, Pallas kernels, run(): pl.pallas_call(kernel, out_shape=outs, name=kernel.__name__, in_specs=[pl...  32.2 us
    ppermute x26, waiting for transfers between devices, swap_wide(): return lax.ppermute(values, 'wide', [(i, i ^ step) for i in range(wide)])  26.9 us
    ppermute x11, starting transfers between devices, swap_chip(): return lax.ppermute(values, 'narrow', [(i, i ^ 2) for i in range(NARROW)])  12.9 us
    all_to_all x1, blocking collectives, exchange(): return lax.all_to_all(message, ('wide', 'narrow'), 0, 0, tiled=True)  12 us
    ppermute x4, starting transfers between devices, on_device(): first_pieces = [lax.ppermute(w_first, MESH, pairs) for pairs in steps]  11 us
    all_to_all x1, blocking collectives, on_device(): parts_three = lax.all_to_all(message, 'wide', 0, 0, tiled=True)  10.4 us
    all_to_all x1, blocking collectives, on_device(): parts_four = lax.all_to_all(message, 'wide', 0, 0, tiled=True)  9.79 us
  transfers between devices with their start and end apart: 63, of which 27 were waited for; matrix products, arithmetic and copies ran while one was open for 3% of the time, Pallas kernels for 13%

profile of v6, /device:TPU:0, one launch (start us, length us, event | category | flops | bytes accessed | tf_op | source)
XLA Modules:
  0.0 191.4 jit_solution(13143565349310585532)
XLA Ops:
  2.1 3.5 %collective-permute-start.1 = (bf16[256,128]{1,0:T(8,128)(2,1)}, bf16[256,128]{1,0:T(8,128)(2,1)S(1)}, u32[]{:S(2)}, u32[]{:S(2)}) collective-permute-start(bf16[256,128]{1,0:T(8,128)(2,1)} %param.14), channel_id=1, source_target_pairs={{0,2},{1,3},{2,10},{3,11},{4,18},{5,19},{6,26},{7,27},{8,4},{9,5},... | collective-permute-start | bytes 196616 | tf_op jit(solution)/shard_map/ppermute | solution.py:647
  5.7 3.4 %collective-permute-start.2 = (bf16[256,128]{1,0:T(8,128)(2,1)}, bf16[256,128]{1,0:T(8,128)(2,1)S(1)}, u32[]{:S(2)}, u32[]{:S(2)}) collective-permute-start(bf16[256,128]{1,0:T(8,128)(2,1)} %param.14), channel_id=1, source_target_pairs={{0,4},{1,5},{2,12},{3,13},{4,20},{5,21},{6,28},{7,29},{8,6},{9,7},... | collective-permute-start | bytes 196616 | tf_op jit(solution)/shard_map/ppermute | solution.py:647
  9.0 2.6 %collective-permute-start.3 = (bf16[256,128]{1,0:T(8,128)(2,1)}, bf16[256,128]{1,0:T(8,128)(2,1)S(1)}, u32[]{:S(2)}, u32[]{:S(2)}) collective-permute-start(bf16[256,128]{1,0:T(8,128)(2,1)} %param.14), channel_id=1, source_target_pairs={{0,6},{1,7},{2,14},{3,15},{4,22},{5,23},{6,30},{7,31},{8,0},{9,1},... | collective-permute-start | bytes 196616 | tf_op jit(solution)/shard_map/ppermute | solution.py:647
  17.2 3.1 %collective-permute-start.9 = (bf16[576,128]{1,0:T(8,128)(2,1)}, bf16[576,128]{1,0:T(8,128)(2,1)S(1)}, u32[]{:S(2)}, u32[]{:S(2)}) collective-permute-start(bf16[576,128]{1,0:T(8,128)(2,1)} %bitcast.17), channel_id=1, source_target_pairs={{0,4},{1,5},{2,6},{3,7},{4,0},{5,1},{6,2},{7,3},{8,12},{9,13},{10,... | collective-permute-start | bytes 442376 | tf_op jit(solution)/shard_map/ppermute | solution.py:568
  32.2 2.5 %collective-permute-start.12 = (bf16[64,512]{1,0:T(8,128)(2,1)S(1)}, bf16[64,512]{1,0:T(8,128)(2,1)S(1)}, u32[]{:S(2)}, u32[]{:S(2)}) collective-permute-start(bf16[64,512]{1,0:T(8,128)(2,1)S(1)} %copy-done.6), channel_id=1, source_target_pairs={{0,2},{1,3},{2,0},{3,1},{4,6},{5,7},{6,4},{7,5},{8,10},{9,11},{10,... | collective-permute-start | bytes 196616 | tf_op jit(solution)/shard_map/ppermute | solution.py:568
  45.8 2.7 %collective-permute-start.16 = (f32[16,128]{1,0:T(8,128)S(1)}, f32[16,128]{1,0:T(8,128)S(1)}, u32[]{:S(2)}, u32[]{:S(2)}) collective-permute-start(f32[16,128]{1,0:T(8,128)S(1)} %add_tiles.4.refs_0_), channel_id=1, source_target_pairs={{0,2},{1,3},{2,0},{3,1},{4,6},{5,7},{6,4},{7,5},{8,10},{9,11},{10,... | collective-permute-start | bytes 24584 | tf_op jit(solution)/shard_map/ppermute | solution.py:568
  59.6 5.6 %middle_forward.1 = (bf16[4,448,512]{2,1,0:T(8,128)(2,1)S(1)}, bf16[4,392,128]{2,1,0:T(8,128)(2,1)S(1)}, f32[4,8,512]{2,1,0:T(8,128)S(1)}, f32[32,8,128]{2,1,0:T(8,128)S(1)}, f32[4,8,128]{2,1,0:T(8,128)S(1)}) custom-call(bf16[392,512]{1,0:T(8,128)(2,1)S(1)} %get-tuple-element.109.pre0.first_pre.p0, bf16[392,512]{1,0:T(8,128)(2,1)S(1)} %collective-permute-done.19.pre1.p1, ...), custom_call_target="tpu_custom_call" | custom-call | flops 2113929216 | bytes 5976192 | tf_op jit(solution)/shard_map/middle_forward/pallas_call | solution.py:39
  66.3 12.0 %all_to_all.20.parts.norm = f32[32,8,128]{2,1,0:T(8,128)S(1)} all-to-all(f32[32,8,128]{2,1,0:T(8,128)S(1)} %get-tuple-element.114), channel_id=1, replica_groups=mesh['narrow'=4,'wide'=8] {'wide','narrow'}, dimensions={0} | all-to-all | bytes 262144 | tf_op jit(solution)/shard_map/all_to_all | solution.py:556
  83.4 2.2 %last_forward.1 = (bf16[4,392,512]{2,1,0:T(8,128)(2,1)S(1)}, bf16[392,512]{1,0:T(8,128)(2,1)S(1)}, f32[8,512]{1,0:T(8,128)S(1)}, f32[4,392,512]{2,1,0:T(8,128)S(1)}, f32[8,8,512]{2,1,0:T(8,128)S(1)}) custom-call(bf16[4,392,128]{2,1,0:T(8,128)(2,1)S(1)} %get-tuple-element.115.src0.pre, bf16[4,392,128]{2,1,0:T(8,128)(2,1)S(1)} %collective-permute-done.26.src1, ...), custom_call_target="tpu_custom_call" | custom-call | flops 822083584 | bytes 7649408 | tf_op jit(solution)/shard_map/last_forward/pallas_call | solution.py:39
  85.6 10.4 %all_to_all.21.parts = f32[8,8,512]{2,1,0:T(8,128)S(1)} all-to-all(f32[8,8,512]{2,1,0:T(8,128)S(1)} %get-tuple-element.119), channel_id=1, replica_groups=mesh['narrow'=4,'wide'=8] {'wide'}, dimensions={0} | all-to-all | bytes 262144 | tf_op jit(solution)/shard_map/all_to_all | solution.py:710
  96.0 3.4 %block_output.1 = (bf16[4,392,512]{2,1,0:T(8,128)(2,1)}, f32[4,392,512]{2,1,0:T(8,128)S(1)}, f32[4,8,512]{2,1,0:T(8,128)S(1)}, f32[8,8,512]{2,1,0:T(8,128)S(1)}) custom-call(f32[4,392,512]{2,1,0:T(8,128)S(1)} %get-tuple-element.118.pre, bf16[4,392,512]{2,1,0:T(8,128)(2,1)S(1)} %copy-done.1, bf16[4,392,512]{2,1,0:T(8,128)(2,1)S(1)} %copy-done.2, ...), custom_call_target="tpu_custom_call" | custom-call | bytes 11593856 | tf_op jit(solution)/shard_map/block_output/pallas_call | solution.py:39
  99.4 9.8 %all_to_all.22.parts = f32[8,8,512]{2,1,0:T(8,128)S(1)} all-to-all(f32[8,8,512]{2,1,0:T(8,128)S(1)} %get-tuple-element.122), channel_id=1, replica_groups=mesh['narrow'=4,'wide'=8] {'wide'}, dimensions={0} | all-to-all | bytes 262144 | tf_op jit(solution)/shard_map/all_to_all | solution.py:716
  115.4 7.9 %collective-permute-done.31.away_last = bf16[256,512]{1,0:T(8,128)(2,1)S(1)} collective-permute-done((bf16[256,512]{1,0:T(8,128)(2,1)S(1)}, bf16[256,512]{1,0:T(8,128)(2,1)S(1)}, u32[]{:S(2)}, u32[]{:S(2)}) %collective-permute-start.31) | collective-permute-done | bytes 262176 | tf_op jit(solution)/shard_map/ppermute | solution.py:568
  125.9 9.1 %all_to_all.23.parts = f32[8,8,128]{2,1,0:T(8,128)S(1)} all-to-all(f32[8,8,128]{2,1,0:T(8,128)S(1)} %get-tuple-element.139), channel_id=1, replica_groups=mesh['narrow'=4,'wide'=8] {'wide'}, dimensions={0} | all-to-all | bytes 65536 | tf_op jit(solution)/shard_map/all_to_all | solution.py:745
  136.8 4.1 %middle_backward.1 = (bf16[392,512]{1,0:T(8,128)(2,1)S(1)}, f32[8,128]{1,0:T(8,128)S(1)}) custom-call(f32[392,512]{1,0:T(8,128)S(1)} %get-tuple-element.137.grad, bf16[392,512]{1,0:T(8,128)(2,1)S(1)} %get-tuple-element.135.pre, f32[8,8,128]{2,1,0:T(8,128)S(1)} %all_to_all.23.parts, f32[4,8,128]{2,1,0:T(8,128)S(1)} %get-tuple-element.117.params, ...), custom_call_target="tpu_custom_call" | custom-call | flops 2113929216 | bytes 7569536 | tf_op jit(solution)/shard_map/middle_backward/pallas_call | solution.py:39
  143.4 4.0 %middle_weight.1 = (f32[1,128]{1,0:T(1,128)}, f32[1,128]{1,0:T(1,128)}, f32[256,1152]{1,0:T(8,128)S(1)}, bf16[256,1152]{1,0:T(8,128)(2,1)S(1)}) custom-call(bf16[4,448,512]{2,1,0:T(8,128)(2,1)S(1)} %get-tuple-element.144.hidden, bf16[392,128]{1,0:T(8,128)(2,1)S(1)} %get-tuple-element.145.q0, bf16[392,128]{1,0:T(8,128)(2,1)S(1)} %collective-permute-done.38.q1, ...), custom_call_target="tpu_custom_call" | custom-call | flops 2113929216 | bytes 5130368 | tf_op jit(solution)/shard_map/middle_weight/pallas_call | solution.py:39
  150.1 3.3 %collective-permute-start.45 = (f32[8,128]{1,0:T(8,128)S(1)}, f32[8,128]{1,0:T(8,128)S(1)}, u32[]{:S(2)}, u32[]{:S(2)}) collective-permute-start(f32[8,128]{1,0:T(8,128)S(1)} %add_tiles.6.refs_0_), channel_id=1, source_target_pairs={{0,6},{1,7},{2,4},{3,5},{4,2},{5,3},{6,0},{7,1},{8,14},{9,15},{10,... | collective-permute-start | bytes 12296 | tf_op jit(solution)/shard_map/ppermute | solution.py:568
  157.4 2.2 %collective-permute-done.50.sum2 = f32[8,128]{1,0:T(8,128)S(1)} collective-permute-done((f32[8,128]{1,0:T(8,128)S(1)}, f32[8,128]{1,0:T(8,128)S(1)}, u32[]{:S(2)}, u32[]{:S(2)}) %collective-permute-start.50) | collective-permute-done | bytes 4128 | tf_op jit(solution)/shard_map/ppermute | solution.py:564
  160.8 2.1 %first_weight.1 = (f32[1,128]{1,0:T(1,128)}, f32[1,128]{1,0:T(1,128)}, bf16[4,392,512]{2,1,0:T(8,128)(2,1)S(1)}, f32[256,512]{1,0:T(8,128)S(1)}, bf16[256,512]{1,0:T(8,128)(2,1)S(1)}) custom-call(bf16[392,512]{1,0:T(8,128)(2,1)S(1)} %get-tuple-element.153.g0, bf16[392,512]{1,0:T(8,128)(2,1)S(1)} %collective-permute-done.46.g1, ...), custom_call_target="tpu_custom_call" | custom-call | flops 822083584 | bytes 7314560 | tf_op jit(solution)/shard_map/first_weight/pallas_call | solution.py:39
  164.7 2.7 %collective-permute-start.57 = (bf16[64,1664]{1,0:T(8,128)(2,1)S(1)}, bf16[64,1664]{1,0:T(8,128)(2,1)S(1)}, u32[]{:S(2)}, u32[]{:S(2)}) collective-permute-start(bf16[64,1664]{1,0:T(8,128)(2,1)S(1)} %get-tuple-element.168), channel_id=1, source_target_pairs={{0,4},{1,5},{2,6},{3,7},{4,0},{5,1},{6,2},{7,3},{8,12},{9,13},{10,... | collective-permute-start | bytes 638984 | tf_op jit(solution)/shard_map/ppermute | solution.py:568
  167.4 7.8 %collective-permute-done.54.p1 = bf16[64,1664]{1,0:T(8,128)(2,1)S(1)} collective-permute-done((bf16[64,1664]{1,0:T(8,128)(2,1)S(1)}, bf16[64,1664]{1,0:T(8,128)(2,1)S(1)}, u32[]{:S(2)}, u32[]{:S(2)}) %collective-permute-start.54) | collective-permute-done | bytes 213024 | tf_op jit(solution)/shard_map/ppermute | solution.py:568
  178.1 2.2 %collective-permute-done.56.far = bf16[2,256,128]{2,1,0:T(8,128)(2,1)S(1)} collective-permute-done((bf16[2,256,128]{2,1,0:T(8,128)(2,1)S(1)}, bf16[2,256,128]{2,1,0:T(8,128)(2,1)S(1)}, u32[]{:S(2)}, u32[]{:S(2)}) %collective-permute-start.56) | collective-permute-done | bytes 131104 | tf_op jit(solution)/shard_map/ppermute | solution.py:564
  183.8 2.4 %collective-permute-start.61 = (bf16[256,128]{1,0:T(8,128)(2,1)S(1)}, bf16[256,128]{1,0:T(8,128)(2,1)S(1)}, u32[]{:S(2)}, u32[]{:S(2)}) collective-permute-start(bf16[256,128]{1,0:T(8,128)(2,1)S(1)} %get-tuple-element.173), channel_id=1, source_target_pairs={{0,6},{1,7},{2,4},{3,5},{4,2},{5,3},{6,0},{7,1},{8,14},{9,15},{10,... | collective-permute-start | bytes 196616 | tf_op jit(solution)/shard_map/ppermute | solution.py:568
  186.2 2.7 %input_gradient.1 = f32[4,392,512]{2,1,0:T(8,128)} custom-call(bf16[4,392,512]{2,1,0:T(8,128)(2,1)S(1)} %get-tuple-element.155.grad_pre, bf16[512,512]{1,0:T(8,128)(2,1)S(1)} %get-tuple-element.156.weight, f32[4,392,512]{2,1,0:T(8,128)S(1)} %get-tuple-element.121.grad), custom_call_target="tpu_custom_call" | custom-call | flops 822083584 | bytes 8552448 | tf_op jit(solution)/shard_map/input_gradient/pallas_call | solution.py:39
  (176 shorter events, 79.0 us)
Async XLA Ops:
  0.6 11.0 %collective-permute-start = (bf16[256,128]{1,0:T(8,128)(2,1)}, bf16[256,128]{1,0:T(8,128)(2,1)S(1)}, u32[]{:S(2)}, u32[]{:S(2)}) collective-permute-start(bf16[256,128]{1,0:T(8,128)(2,1)} %param.14), channel_id=1, source_target_pairs={{0,0},{1,1},{2,8},{3,9},{4,16},{5,17},{6,24},{7,25},{8,2},{9,3},{1... | collective-permute-start | bytes 196616 | tf_op jit(solution)/shard_map/ppermute | solution.py:647
  2.1 9.5 %collective-permute-start.1 = (bf16[256,128]{1,0:T(8,128)(2,1)}, bf16[256,128]{1,0:T(8,128)(2,1)S(1)}, u32[]{:S(2)}, u32[]{:S(2)}) collective-permute-start(bf16[256,128]{1,0:T(8,128)(2,1)} %param.14), channel_id=1, source_target_pairs={{0,2},{1,3},{2,10},{3,11},{4,18},{5,19},{6,26},{7,27},{8,4},{9,5},... | collective-permute-start | bytes 196616 | tf_op jit(solution)/shard_map/ppermute | solution.py:647
  14.0 8.9 %collective-permute-start.4 = (bf16[256,512]{1,0:T(8,128)(2,1)S(1)}, bf16[256,512]{1,0:T(8,128)(2,1)S(1)}, u32[]{:S(2)}, u32[]{:S(2)}) collective-permute-start(bf16[256,512]{1,0:T(8,128)(2,1)S(1)} %place_columns.1.refs_0_), channel_id=1, source_target_pairs={{0,1},{1,0},{2,3},{3,2},{4,5},{5,4},{6,7},{7,6},{8,9},{9,8},{10,11... | collective-permute-start | bytes 786440 | tf_op jit(solution)/shard_map/ppermute | solution.py:568
  15.6 13.1 %collective-permute-start.7 = (bf16[576,128]{1,0:T(8,128)(2,1)}, bf16[576,128]{1,0:T(8,128)(2,1)S(1)}, u32[]{:S(2)}, u32[]{:S(2)}) collective-permute-start(bf16[576,128]{1,0:T(8,128)(2,1)} %bitcast.16), channel_id=1, source_target_pairs={{0,2},{1,3},{2,0},{3,1},{4,6},{5,7},{6,4},{7,5},{8,10},{9,11},{10,... | collective-permute-start | bytes 442376 | tf_op jit(solution)/shard_map/ppermute | solution.py:568
  17.2 14.4 %collective-permute-start.9 = (bf16[576,128]{1,0:T(8,128)(2,1)}, bf16[576,128]{1,0:T(8,128)(2,1)S(1)}, u32[]{:S(2)}, u32[]{:S(2)}) collective-permute-start(bf16[576,128]{1,0:T(8,128)(2,1)} %bitcast.17), channel_id=1, source_target_pairs={{0,4},{1,5},{2,6},{3,7},{4,0},{5,1},{6,2},{7,3},{8,12},{9,13},{10,... | collective-permute-start | bytes 442376 | tf_op jit(solution)/shard_map/ppermute | solution.py:568
  20.3 11.3 %collective-permute-start.10 = (bf16[576,128]{1,0:T(8,128)(2,1)}, bf16[576,128]{1,0:T(8,128)(2,1)S(1)}, u32[]{:S(2)}, u32[]{:S(2)}) collective-permute-start(bf16[576,128]{1,0:T(8,128)(2,1)} %bitcast.18), channel_id=1, source_target_pairs={{0,6},{1,7},{2,4},{3,5},{4,2},{5,3},{6,0},{7,1},{8,14},{9,15},{10,... | collective-permute-start | bytes 442376 | tf_op jit(solution)/shard_map/ppermute | solution.py:568
  26.5 11.8 %collective-permute-start.5 = (bf16[392,512]{1,0:T(8,128)(2,1)}, bf16[392,512]{1,0:T(8,128)(2,1)S(1)}, u32[]{:S(2)}, u32[]{:S(2)}) collective-permute-start(bf16[392,512]{1,0:T(8,128)(2,1)} %get-tuple-element.99), channel_id=1, source_target_pairs={{0,8},{8,0},{16,24},{24,16},{1,9},{9,1},{17,25},{25,17},{2,10},{10... | collective-permute-start | bytes 1204232 | tf_op jit(solution)/shard_map/ppermute | solution.py:560
  28.6 11.8 %collective-permute-start.8 = (bf16[392,512]{1,0:T(8,128)(2,1)}, bf16[392,512]{1,0:T(8,128)(2,1)S(1)}, u32[]{:S(2)}, u32[]{:S(2)}) collective-permute-start(bf16[392,512]{1,0:T(8,128)(2,1)} %add_convert_fusion.1), channel_id=1, source_target_pairs={{0,16},{8,24},{16,0},{24,8},{1,17},{9,25},{17,1},{25,9},{2,18},{10... | collective-permute-start | bytes 1204232 | tf_op jit(solution)/shard_map/ppermute | solution.py:564
  31.6 13.9 %collective-permute-start.11 = (bf16[2304,128]{1,0:T(8,128)(2,1)S(1)}, bf16[2304,128]{1,0:T(8,128)(2,1)S(1)}, u32[]{:S(2)}, u32[]{:S(2)}) collective-permute-start(bf16[2304,128]{1,0:T(8,128)(2,1)S(1)} %constant_dynamic-update-slice_fusion.near), channel_id=1, source_target_pairs={{0,1},{1,0},{2,3},{3,2},{4,5},{5,4},{6,7},{7,6},{8,9},{9,8},{10,11... | collective-permute-start | bytes 1769480 | tf_op jit(solution)/shard_map/ppermute | solution.py:568
  32.2 9.8 %collective-permute-start.12 = (bf16[64,512]{1,0:T(8,128)(2,1)S(1)}, bf16[64,512]{1,0:T(8,128)(2,1)S(1)}, u32[]{:S(2)}, u32[]{:S(2)}) collective-permute-start(bf16[64,512]{1,0:T(8,128)(2,1)S(1)} %copy-done.6), channel_id=1, source_target_pairs={{0,2},{1,3},{2,0},{3,1},{4,6},{5,7},{6,4},{7,5},{8,10},{9,11},{10,... | collective-permute-start | bytes 196616 | tf_op jit(solution)/shard_map/ppermute | solution.py:568
  40.7 15.1 %collective-permute-start.20 = (bf16[392,512]{1,0:T(8,128)(2,1)S(1)}, bf16[392,512]{1,0:T(8,128)(2,1)S(1)}, u32[]{:S(2)}, u32[]{:S(2)}) collective-permute-start(bf16[392,512]{1,0:T(8,128)(2,1)S(1)} %get-tuple-element.109.pre0.first_pre.p0), channel_id=1, source_target_pairs={{0,16},{8,24},{16,0},{24,8},{1,17},{9,25},{17,1},{25,9},{2,18},{10... | collective-permute-start | bytes 1204232 | tf_op jit(solution)/shard_map/ppermute | solution.py:564
  65.2 13.1 %collective-permute-start.27 = (bf16[4,392,128]{2,1,0:T(8,128)(2,1)S(1)}, bf16[4,392,128]{2,1,0:T(8,128)(2,1)S(1)}, u32[]{:S(2)}, u32[]{:S(2)}) collective-permute-start(bf16[4,392,128]{2,1,0:T(8,128)(2,1)S(1)} %get-tuple-element.115.src0.pre), channel_id=1, source_target_pairs={{0,16},{8,24},{16,0},{24,8},{1,17},{9,25},{17,1},{25,9},{2,18},{10... | collective-permute-start | bytes 1204232 | tf_op jit(solution)/shard_map/ppermute | solution.py:564
  80.0 31.7 %collective-permute-start.30 = (bf16[512,1152]{1,0:T(8,128)(2,1)S(1)}, bf16[512,1152]{1,0:T(8,128)(2,1)S(1)}, u32[]{:S(2)}, u32[]{:S(2)}) collective-permute-start(bf16[512,1152]{1,0:T(8,128)(2,1)S(1)} %gather_middle.1.weight.w0), channel_id=1, source_target_pairs={{0,16},{8,24},{16,0},{24,8},{1,17},{9,25},{17,1},{25,9},{2,18},{10... | collective-permute-start | bytes 3538952 | tf_op jit(solution)/shard_map/ppermute | solution.py:564
  111.2 14.7 %collective-permute-start.34 = (bf16[512,1152]{1,0:T(8,128)(2,1)S(1)}, bf16[512,1152]{1,0:T(8,128)(2,1)S(1)}, u32[]{:S(2)}, u32[]{:S(2)}) collective-permute-start(bf16[512,1152]{1,0:T(8,128)(2,1)S(1)} %gather_middle.1.weight.w0), channel_id=1, source_target_pairs={{0,8},{8,0},{16,24},{24,16},{1,9},{9,1},{17,25},{25,17},{2,10},{10... | collective-permute-start | bytes 3538952 | tf_op jit(solution)/shard_map/ppermute | solution.py:560
  111.7 14.2 %collective-permute-start.35 = (bf16[512,1152]{1,0:T(8,128)(2,1)S(1)}, bf16[512,1152]{1,0:T(8,128)(2,1)S(1)}, u32[]{:S(2)}, u32[]{:S(2)}) collective-permute-start(bf16[512,1152]{1,0:T(8,128)(2,1)S(1)} %collective-permute-done.30.w2), channel_id=1, source_target_pairs={{0,8},{8,0},{16,24},{24,16},{1,9},{9,1},{17,25},{25,17},{2,10},{10... | collective-permute-start | bytes 3538952 | tf_op jit(solution)/shard_map/ppermute | solution.py:560
  111.7 11.5 %collective-permute-start.32 = (bf16[392,512]{1,0:T(8,128)(2,1)S(1)}, bf16[392,512]{1,0:T(8,128)(2,1)S(1)}, u32[]{:S(2)}, u32[]{:S(2)}) collective-permute-start(bf16[392,512]{1,0:T(8,128)(2,1)S(1)} %get-tuple-element.134), channel_id=1, source_target_pairs={{0,8},{8,0},{16,24},{24,16},{1,9},{9,1},{17,25},{25,17},{2,10},{10... | collective-permute-start | bytes 1204232 | tf_op jit(solution)/shard_map/ppermute | solution.py:560
  113.1 11.4 %collective-permute-start.33 = (bf16[392,512]{1,0:T(8,128)(2,1)S(1)}, bf16[392,512]{1,0:T(8,128)(2,1)S(1)}, u32[]{:S(2)}, u32[]{:S(2)}) collective-permute-start(bf16[392,512]{1,0:T(8,128)(2,1)S(1)} %add_convert_fusion), channel_id=1, source_target_pairs={{0,16},{8,24},{16,0},{24,8},{1,17},{9,25},{17,1},{25,9},{2,18},{10... | collective-permute-start | bytes 1204232 | tf_op jit(solution)/shard_map/ppermute | solution.py:564
  125.2 11.2 %collective-permute-start.37 = (bf16[2,392,128]{2,1,0:T(8,128)(2,1)S(1)}, bf16[2,392,128]{2,1,0:T(8,128)(2,1)S(1)}, u32[]{:S(2)}, u32[]{:S(2)}) collective-permute-start(bf16[2,392,128]{2,1,0:T(8,128)(2,1)S(1)} %get-tuple-element.147), channel_id=1, source_target_pairs={{0,16},{8,24},{16,0},{24,8},{1,17},{9,25},{17,1},{25,9},{2,18},{10... | collective-permute-start | bytes 602120 | tf_op jit(solution)/shard_map/ppermute | solution.py:564
  141.0 14.5 %collective-permute-start.47 = (bf16[392,512]{1,0:T(8,128)(2,1)S(1)}, bf16[392,512]{1,0:T(8,128)(2,1)S(1)}, u32[]{:S(2)}, u32[]{:S(2)}) collective-permute-start(bf16[392,512]{1,0:T(8,128)(2,1)S(1)} %get-tuple-element.153.g0), channel_id=1, source_target_pairs={{0,16},{8,24},{16,0},{24,8},{1,17},{9,25},{17,1},{25,9},{2,18},{10... | collective-permute-start | bytes 1204232 | tf_op jit(solution)/shard_map/ppermute | solution.py:564
  147.3 15.5 %collective-permute-start.52 = (bf16[256,1152]{1,0:T(8,128)(2,1)S(1)}, bf16[256,1152]{1,0:T(8,128)(2,1)S(1)}, u32[]{:S(2)}, u32[]{:S(2)}) collective-permute-start(bf16[256,1152]{1,0:T(8,128)(2,1)S(1)} %get-tuple-element.159), channel_id=1, source_target_pairs={{0,1},{1,0},{2,3},{3,2},{4,5},{5,4},{6,7},{7,6},{8,9},{9,8},{10,11... | collective-permute-start | bytes 1769480 | tf_op jit(solution)/shard_map/ppermute | solution.py:568
  162.8 12.3 %collective-permute-start.53 = (bf16[256,512]{1,0:T(8,128)(2,1)S(1)}, bf16[256,512]{1,0:T(8,128)(2,1)S(1)}, u32[]{:S(2)}, u32[]{:S(2)}) collective-permute-start(bf16[256,512]{1,0:T(8,128)(2,1)S(1)} %get-tuple-element.160), channel_id=1, source_target_pairs={{0,1},{1,0},{2,3},{3,2},{4,5},{5,4},{6,7},{7,6},{8,9},{9,8},{10,11... | collective-permute-start | bytes 786440 | tf_op jit(solution)/shard_map/ppermute | solution.py:568
  164.2 10.9 %collective-permute-start.54 = (bf16[64,1664]{1,0:T(8,128)(2,1)S(1)}, bf16[64,1664]{1,0:T(8,128)(2,1)S(1)}, u32[]{:S(2)}, u32[]{:S(2)}) collective-permute-start(bf16[64,1664]{1,0:T(8,128)(2,1)S(1)} %get-tuple-element.163), channel_id=1, source_target_pairs={{0,2},{1,3},{2,0},{3,1},{4,6},{5,7},{6,4},{7,5},{8,10},{9,11},{10,... | collective-permute-start | bytes 638984 | tf_op jit(solution)/shard_map/ppermute | solution.py:568
  164.7 13.4 %collective-permute-start.57 = (bf16[64,1664]{1,0:T(8,128)(2,1)S(1)}, bf16[64,1664]{1,0:T(8,128)(2,1)S(1)}, u32[]{:S(2)}, u32[]{:S(2)}) collective-permute-start(bf16[64,1664]{1,0:T(8,128)(2,1)S(1)} %get-tuple-element.168), channel_id=1, source_target_pairs={{0,4},{1,5},{2,6},{3,7},{4,0},{5,1},{6,2},{7,3},{8,12},{9,13},{10,... | collective-permute-start | bytes 638984 | tf_op jit(solution)/shard_map/ppermute | solution.py:568
  176.7 12.3 %collective-permute-start.62 = (bf16[64,1664]{1,0:T(8,128)(2,1)S(1)}, bf16[64,1664]{1,0:T(8,128)(2,1)S(1)}, u32[]{:S(2)}, u32[]{:S(2)}) collective-permute-start(bf16[64,1664]{1,0:T(8,128)(2,1)S(1)} %get-tuple-element.176), channel_id=1, source_target_pairs={{0,6},{1,7},{2,4},{3,5},{4,2},{5,3},{6,0},{7,1},{8,14},{9,15},{10,... | collective-permute-start | bytes 638984 | tf_op jit(solution)/shard_map/ppermute | solution.py:568
  (51 other events, 297.1 us)

commit v7 on v6

--- a/solution.py
+++ b/solution.py
@@ -682,12 +682,11 @@
     pre_one, message = run(first_join, (*joined, mask, small), [flat, arr((16, 128), F32)])
     begun, total = sum_wide(message, wide, beside=beside)
     if direct:
-        last_far = swap_wide(after(last_near, begun), 1, wide)
+        last_far = swap_wide(after(last_near, total), 1, wide)
     pre_ones = from_all(pre_one, total)
     sums_one = from_all(total)
     if direct:
         middle_slice = run(gather_middle, (middle_near, middle_far), [arr((mid, TAPS * 128), BF)])[0]
-        middle_slice = after(middle_slice, last_far)
 
     hidden_one, pre_two, coef_one, message, params = run(
         middle_forward, (*pre_ones, *sums_one, mask, to_canvas, to_rows, middle_slice),
@@ -697,6 +696,8 @@
     )
     if direct:
         last_slice = run(gather_last, (last_near, last_far), [arr((mid, low), BF)])[0]
+    if direct:
+        message = after(message, last_far)
     parts_two = exchange(message)
     pre_twos = from_all(pre_two, parts_two)
     held = after(middle_slice, pre_twos[3], parts_two)

time: 193 us -> 192 us (level)
  transfers between devices with their start and end apart: 63 -> 63, of which waited for: 27 -> 27; matrix products, arithmetic and copies ran while one was open for 3% -> 3% of each run, Pallas kernels for 13% -> 16%
where the time goes in v7:
time: 192 us
  starting transfers between devices  64.5 us (34%)
  waiting for transfers between devices  47 us (24%)
  blocking collectives  40.5 us (21%)
  Pallas kernels  32.2 us (17%)
  other arithmetic  3.52 us (2%)
  local copies, waits for them, and re-layouts  3.01 us (2%)
    ppermute x26, starting transfers between devices, swap_wide(): return lax.ppermute(values, 'wide', [(i, i ^ step) for i in range(wide)])  36.2 us
    pallas_call x25, Pallas kernels, run(): pl.pallas_call(kernel, out_shape=outs, name=kernel.__name__, in_specs=[pl...  32.2 us
    ppermute x26, waiting for transfers between devices, swap_wide(): return lax.ppermute(values, 'wide', [(i, i ^ step) for i in range(wide)])  28.3 us
    ppermute x11, starting transfers between devices, swap_chip(): return lax.ppermute(values, 'narrow', [(i, i ^ 2) for i in range(NARROW)])  13.1 us
    all_to_all x1, blocking collectives, exchange(): return lax.all_to_all(message, ('wide', 'narrow'), 0, 0, tiled=True)  11.3 us
    ppermute x4, starting transfers between devices, on_device(): first_pieces = [lax.ppermute(w_first, MESH, pairs) for pairs in steps]  11 us
    all_to_all x1, blocking collectives, on_device(): parts_three = lax.all_to_all(message, 'wide', 0, 0, tiled=True)  10.4 us
    all_to_all x1, blocking collectives, on_device(): parts_four = lax.all_to_all(message, 'wide', 0, 0, tiled=True)  9.79 us
  transfers between devices with their start and end apart: 63, of which 27 were waited for; matrix products, arithmetic and copies ran while one was open for 3% of the time, Pallas kernels for 16%

profile of v7, /device:TPU:0, one launch (start us, length us, event | category | flops | bytes accessed | tf_op | source)
XLA Modules:
  0.0 191.7 jit_solution(7588639947950058342)
XLA Ops:
  2.1 3.5 %collective-permute-start.1 = (bf16[256,128]{1,0:T(8,128)(2,1)}, bf16[256,128]{1,0:T(8,128)(2,1)S(1)}, u32[]{:S(2)}, u32[]{:S(2)}) collective-permute-start(bf16[256,128]{1,0:T(8,128)(2,1)} %param.14), channel_id=1, source_target_pairs={{0,2},{1,3},{2,10},{3,11},{4,18},{5,19},{6,26},{7,27},{8,4},{9,5},... | collective-permute-start | bytes 196616 | tf_op jit(solution)/shard_map/ppermute | solution.py:647
  5.7 3.4 %collective-permute-start.2 = (bf16[256,128]{1,0:T(8,128)(2,1)}, bf16[256,128]{1,0:T(8,128)(2,1)S(1)}, u32[]{:S(2)}, u32[]{:S(2)}) collective-permute-start(bf16[256,128]{1,0:T(8,128)(2,1)} %param.14), channel_id=1, source_target_pairs={{0,4},{1,5},{2,12},{3,13},{4,20},{5,21},{6,28},{7,29},{8,6},{9,7},... | collective-permute-start | bytes 196616 | tf_op jit(solution)/shard_map/ppermute | solution.py:647
  9.0 2.6 %collective-permute-start.3 = (bf16[256,128]{1,0:T(8,128)(2,1)}, bf16[256,128]{1,0:T(8,128)(2,1)S(1)}, u32[]{:S(2)}, u32[]{:S(2)}) collective-permute-start(bf16[256,128]{1,0:T(8,128)(2,1)} %param.14), channel_id=1, source_target_pairs={{0,6},{1,7},{2,14},{3,15},{4,22},{5,23},{6,30},{7,31},{8,0},{9,1},... | collective-permute-start | bytes 196616 | tf_op jit(solution)/shard_map/ppermute | solution.py:647
  17.2 3.1 %collective-permute-start.9 = (bf16[576,128]{1,0:T(8,128)(2,1)}, bf16[576,128]{1,0:T(8,128)(2,1)S(1)}, u32[]{:S(2)}, u32[]{:S(2)}) collective-permute-start(bf16[576,128]{1,0:T(8,128)(2,1)} %bitcast.17), channel_id=1, source_target_pairs={{0,4},{1,5},{2,6},{3,7},{4,0},{5,1},{6,2},{7,3},{8,12},{9,13},{10,... | collective-permute-start | bytes 442376 | tf_op jit(solution)/shard_map/ppermute | solution.py:568
  32.2 2.5 %collective-permute-start.12 = (bf16[64,512]{1,0:T(8,128)(2,1)S(1)}, bf16[64,512]{1,0:T(8,128)(2,1)S(1)}, u32[]{:S(2)}, u32[]{:S(2)}) collective-permute-start(bf16[64,512]{1,0:T(8,128)(2,1)S(1)} %copy-done.6), channel_id=1, source_target_pairs={{0,2},{1,3},{2,0},{3,1},{4,6},{5,7},{6,4},{7,5},{8,10},{9,11},{10,... | collective-permute-start | bytes 196616 | tf_op jit(solution)/shard_map/ppermute | solution.py:568
  45.8 2.7 %collective-permute-start.16 = (f32[16,128]{1,0:T(8,128)S(1)}, f32[16,128]{1,0:T(8,128)S(1)}, u32[]{:S(2)}, u32[]{:S(2)}) collective-permute-start(f32[16,128]{1,0:T(8,128)S(1)} %add_tiles.4.refs_0_), channel_id=1, source_target_pairs={{0,2},{1,3},{2,0},{3,1},{4,6},{5,7},{6,4},{7,5},{8,10},{9,11},{10,... | collective-permute-start | bytes 24584 | tf_op jit(solution)/shard_map/ppermute | solution.py:568
  50.9 2.1 %collective-permute-done.17.refs_2_ = f32[16,128]{1,0:T(8,128)S(1)} collective-permute-done((f32[16,128]{1,0:T(8,128)S(1)}, f32[16,128]{1,0:T(8,128)S(1)}, u32[]{:S(2)}, u32[]{:S(2)}) %collective-permute-start.17) | collective-permute-done | bytes 8224 | tf_op jit(solution)/shard_map/ppermute | solution.py:568
  59.7 5.6 %middle_forward.1 = (bf16[4,448,512]{2,1,0:T(8,128)(2,1)S(1)}, bf16[4,392,128]{2,1,0:T(8,128)(2,1)S(1)}, f32[4,8,512]{2,1,0:T(8,128)S(1)}, f32[32,8,128]{2,1,0:T(8,128)S(1)}, f32[4,8,128]{2,1,0:T(8,128)S(1)}) custom-call(bf16[392,512]{1,0:T(8,128)(2,1)S(1)} %get-tuple-element.109.pre0.first_pre.p0, bf16[392,512]{1,0:T(8,128)(2,1)S(1)} %collective-permute-done.19.pre1.p1, ...), custom_call_target="tpu_custom_call" | custom-call | flops 2113929216 | bytes 5976192 | tf_op jit(solution)/shard_map/middle_forward/pallas_call | solution.py:39
  67.6 11.3 %all_to_all.20.parts.norm = f32[32,8,128]{2,1,0:T(8,128)S(1)} all-to-all(f32[32,8,128]{2,1,0:T(8,128)S(1)} %get-tuple-element.114), channel_id=1, replica_groups=mesh['narrow'=4,'wide'=8] {'wide','narrow'}, dimensions={0} | all-to-all | bytes 262144 | tf_op jit(solution)/shard_map/all_to_all | solution.py:556
  83.4 2.2 %last_forward.1 = (bf16[4,392,512]{2,1,0:T(8,128)(2,1)S(1)}, bf16[392,512]{1,0:T(8,128)(2,1)S(1)}, f32[8,512]{1,0:T(8,128)S(1)}, f32[4,392,512]{2,1,0:T(8,128)S(1)}, f32[8,8,512]{2,1,0:T(8,128)S(1)}) custom-call(bf16[4,392,128]{2,1,0:T(8,128)(2,1)S(1)} %get-tuple-element.115.src0.pre, bf16[4,392,128]{2,1,0:T(8,128)(2,1)S(1)} %collective-permute-done.26.src1, ...), custom_call_target="tpu_custom_call" | custom-call | flops 822083584 | bytes 7649408 | tf_op jit(solution)/shard_map/last_forward/pallas_call | solution.py:39
  85.6 10.4 %all_to_all.21.parts = f32[8,8,512]{2,1,0:T(8,128)S(1)} all-to-all(f32[8,8,512]{2,1,0:T(8,128)S(1)} %get-tuple-element.119), channel_id=1, replica_groups=mesh['narrow'=4,'wide'=8] {'wide'}, dimensions={0} | all-to-all | bytes 262144 | tf_op jit(solution)/shard_map/all_to_all | solution.py:711
  96.0 3.4 %block_output.1 = (bf16[4,392,512]{2,1,0:T(8,128)(2,1)}, f32[4,392,512]{2,1,0:T(8,128)S(1)}, f32[4,8,512]{2,1,0:T(8,128)S(1)}, f32[8,8,512]{2,1,0:T(8,128)S(1)}) custom-call(f32[4,392,512]{2,1,0:T(8,128)S(1)} %get-tuple-element.118.pre, bf16[4,392,512]{2,1,0:T(8,128)(2,1)S(1)} %copy-done.1, bf16[4,392,512]{2,1,0:T(8,128)(2,1)S(1)} %copy-done.2, ...), custom_call_target="tpu_custom_call" | custom-call | bytes 11593856 | tf_op jit(solution)/shard_map/block_output/pallas_call | solution.py:39
  99.4 9.8 %all_to_all.22.parts = f32[8,8,512]{2,1,0:T(8,128)S(1)} all-to-all(f32[8,8,512]{2,1,0:T(8,128)S(1)} %get-tuple-element.122), channel_id=1, replica_groups=mesh['narrow'=4,'wide'=8] {'wide'}, dimensions={0} | all-to-all | bytes 262144 | tf_op jit(solution)/shard_map/all_to_all | solution.py:717
  115.6 7.9 %collective-permute-done.31.away_last = bf16[256,512]{1,0:T(8,128)(2,1)S(1)} collective-permute-done((bf16[256,512]{1,0:T(8,128)(2,1)S(1)}, bf16[256,512]{1,0:T(8,128)(2,1)S(1)}, u32[]{:S(2)}, u32[]{:S(2)}) %collective-permute-start.31) | collective-permute-done | bytes 262176 | tf_op jit(solution)/shard_map/ppermute | solution.py:568
  126.1 9.1 %all_to_all.23.parts = f32[8,8,128]{2,1,0:T(8,128)S(1)} all-to-all(f32[8,8,128]{2,1,0:T(8,128)S(1)} %get-tuple-element.139), channel_id=1, replica_groups=mesh['narrow'=4,'wide'=8] {'wide'}, dimensions={0} | all-to-all | bytes 65536 | tf_op jit(solution)/shard_map/all_to_all | solution.py:746
  136.8 4.1 %middle_backward.1 = (bf16[392,512]{1,0:T(8,128)(2,1)S(1)}, f32[8,128]{1,0:T(8,128)S(1)}) custom-call(f32[392,512]{1,0:T(8,128)S(1)} %get-tuple-element.137.grad, bf16[392,512]{1,0:T(8,128)(2,1)S(1)} %get-tuple-element.135.pre, f32[8,8,128]{2,1,0:T(8,128)S(1)} %all_to_all.23.parts, f32[4,8,128]{2,1,0:T(8,128)S(1)} %get-tuple-element.117.params, ...), custom_call_target="tpu_custom_call" | custom-call | flops 2113929216 | bytes 7569536 | tf_op jit(solution)/shard_map/middle_backward/pallas_call | solution.py:39
  143.6 4.0 %middle_weight.1 = (f32[1,128]{1,0:T(1,128)}, f32[1,128]{1,0:T(1,128)}, f32[256,1152]{1,0:T(8,128)S(1)}, bf16[256,1152]{1,0:T(8,128)(2,1)S(1)}) custom-call(bf16[4,448,512]{2,1,0:T(8,128)(2,1)S(1)} %get-tuple-element.144.hidden, bf16[392,128]{1,0:T(8,128)(2,1)S(1)} %get-tuple-element.145.q0, bf16[392,128]{1,0:T(8,128)(2,1)S(1)} %collective-permute-done.38.q1, ...), custom_call_target="tpu_custom_call" | custom-call | flops 2113929216 | bytes 5130368 | tf_op jit(solution)/shard_map/middle_weight/pallas_call | solution.py:39
  150.3 3.3 %collective-permute-start.45 = (f32[8,128]{1,0:T(8,128)S(1)}, f32[8,128]{1,0:T(8,128)S(1)}, u32[]{:S(2)}, u32[]{:S(2)}) collective-permute-start(f32[8,128]{1,0:T(8,128)S(1)} %add_tiles.6.refs_0_), channel_id=1, source_target_pairs={{0,6},{1,7},{2,4},{3,5},{4,2},{5,3},{6,0},{7,1},{8,14},{9,15},{10,... | collective-permute-start | bytes 12296 | tf_op jit(solution)/shard_map/ppermute | solution.py:568
  157.4 2.4 %collective-permute-done.50.sum2 = f32[8,128]{1,0:T(8,128)S(1)} collective-permute-done((f32[8,128]{1,0:T(8,128)S(1)}, f32[8,128]{1,0:T(8,128)S(1)}, u32[]{:S(2)}, u32[]{:S(2)}) %collective-permute-start.50) | collective-permute-done | bytes 4128 | tf_op jit(solution)/shard_map/ppermute | solution.py:564
  164.9 2.7 %collective-permute-start.57 = (bf16[64,1664]{1,0:T(8,128)(2,1)S(1)}, bf16[64,1664]{1,0:T(8,128)(2,1)S(1)}, u32[]{:S(2)}, u32[]{:S(2)}) collective-permute-start(bf16[64,1664]{1,0:T(8,128)(2,1)S(1)} %get-tuple-element.168), channel_id=1, source_target_pairs={{0,4},{1,5},{2,6},{3,7},{4,0},{5,1},{6,2},{7,3},{8,12},{9,13},{10,... | collective-permute-start | bytes 638984 | tf_op jit(solution)/shard_map/ppermute | solution.py:568
  167.6 7.8 %collective-permute-done.54.p1 = bf16[64,1664]{1,0:T(8,128)(2,1)S(1)} collective-permute-done((bf16[64,1664]{1,0:T(8,128)(2,1)S(1)}, bf16[64,1664]{1,0:T(8,128)(2,1)S(1)}, u32[]{:S(2)}, u32[]{:S(2)}) %collective-permute-start.54) | collective-permute-done | bytes 213024 | tf_op jit(solution)/shard_map/ppermute | solution.py:568
  178.1 2.4 %collective-permute-done.56.far = bf16[2,256,128]{2,1,0:T(8,128)(2,1)S(1)} collective-permute-done((bf16[2,256,128]{2,1,0:T(8,128)(2,1)S(1)}, bf16[2,256,128]{2,1,0:T(8,128)(2,1)S(1)}, u32[]{:S(2)}, u32[]{:S(2)}) %collective-permute-start.56) | collective-permute-done | bytes 131104 | tf_op jit(solution)/shard_map/ppermute | solution.py:564
  184.0 2.4 %collective-permute-start.61 = (bf16[256,128]{1,0:T(8,128)(2,1)S(1)}, bf16[256,128]{1,0:T(8,128)(2,1)S(1)}, u32[]{:S(2)}, u32[]{:S(2)}) collective-permute-start(bf16[256,128]{1,0:T(8,128)(2,1)S(1)} %get-tuple-element.173), channel_id=1, source_target_pairs={{0,6},{1,7},{2,4},{3,5},{4,2},{5,3},{6,0},{7,1},{8,14},{9,15},{10,... | collective-permute-start | bytes 196616 | tf_op jit(solution)/shard_map/ppermute | solution.py:568
  186.4 2.7 %input_gradient.1 = f32[4,392,512]{2,1,0:T(8,128)} custom-call(bf16[4,392,512]{2,1,0:T(8,128)(2,1)S(1)} %get-tuple-element.155.grad_pre, bf16[512,512]{1,0:T(8,128)(2,1)S(1)} %get-tuple-element.156.weight, f32[4,392,512]{2,1,0:T(8,128)S(1)} %get-tuple-element.121.grad), custom_call_target="tpu_custom_call" | custom-call | flops 822083584 | bytes 8552448 | tf_op jit(solution)/shard_map/input_gradient/pallas_call | solution.py:39
  (176 shorter events, 79.4 us)
Async XLA Ops:
  0.6 11.0 %collective-permute-start = (bf16[256,128]{1,0:T(8,128)(2,1)}, bf16[256,128]{1,0:T(8,128)(2,1)S(1)}, u32[]{:S(2)}, u32[]{:S(2)}) collective-permute-start(bf16[256,128]{1,0:T(8,128)(2,1)} %param.14), channel_id=1, source_target_pairs={{0,0},{1,1},{2,8},{3,9},{4,16},{5,17},{6,24},{7,25},{8,2},{9,3},{1... | collective-permute-start | bytes 196616 | tf_op jit(solution)/shard_map/ppermute | solution.py:647
  2.1 9.5 %collective-permute-start.1 = (bf16[256,128]{1,0:T(8,128)(2,1)}, bf16[256,128]{1,0:T(8,128)(2,1)S(1)}, u32[]{:S(2)}, u32[]{:S(2)}) collective-permute-start(bf16[256,128]{1,0:T(8,128)(2,1)} %param.14), channel_id=1, source_target_pairs={{0,2},{1,3},{2,10},{3,11},{4,18},{5,19},{6,26},{7,27},{8,4},{9,5},... | collective-permute-start | bytes 196616 | tf_op jit(solution)/shard_map/ppermute | solution.py:647
  14.0 8.9 %collective-permute-start.4 = (bf16[256,512]{1,0:T(8,128)(2,1)S(1)}, bf16[256,512]{1,0:T(8,128)(2,1)S(1)}, u32[]{:S(2)}, u32[]{:S(2)}) collective-permute-start(bf16[256,512]{1,0:T(8,128)(2,1)S(1)} %place_columns.1.refs_0_), channel_id=1, source_target_pairs={{0,1},{1,0},{2,3},{3,2},{4,5},{5,4},{6,7},{7,6},{8,9},{9,8},{10,11... | collective-permute-start | bytes 786440 | tf_op jit(solution)/shard_map/ppermute | solution.py:568
  15.6 13.1 %collective-permute-start.7 = (bf16[576,128]{1,0:T(8,128)(2,1)}, bf16[576,128]{1,0:T(8,128)(2,1)S(1)}, u32[]{:S(2)}, u32[]{:S(2)}) collective-permute-start(bf16[576,128]{1,0:T(8,128)(2,1)} %bitcast.16), channel_id=1, source_target_pairs={{0,2},{1,3},{2,0},{3,1},{4,6},{5,7},{6,4},{7,5},{8,10},{9,11},{10,... | collective-permute-start | bytes 442376 | tf_op jit(solution)/shard_map/ppermute | solution.py:568
  17.2 14.4 %collective-permute-start.9 = (bf16[576,128]{1,0:T(8,128)(2,1)}, bf16[576,128]{1,0:T(8,128)(2,1)S(1)}, u32[]{:S(2)}, u32[]{:S(2)}) collective-permute-start(bf16[576,128]{1,0:T(8,128)(2,1)} %bitcast.17), channel_id=1, source_target_pairs={{0,4},{1,5},{2,6},{3,7},{4,0},{5,1},{6,2},{7,3},{8,12},{9,13},{10,... | collective-permute-start | bytes 442376 | tf_op jit(solution)/shard_map/ppermute | solution.py:568
  20.3 11.3 %collective-permute-start.10 = (bf16[576,128]{1,0:T(8,128)(2,1)}, bf16[576,128]{1,0:T(8,128)(2,1)S(1)}, u32[]{:S(2)}, u32[]{:S(2)}) collective-permute-start(bf16[576,128]{1,0:T(8,128)(2,1)} %bitcast.18), channel_id=1, source_target_pairs={{0,6},{1,7},{2,4},{3,5},{4,2},{5,3},{6,0},{7,1},{8,14},{9,15},{10,... | collective-permute-start | bytes 442376 | tf_op jit(solution)/shard_map/ppermute | solution.py:568
  26.5 11.8 %collective-permute-start.5 = (bf16[392,512]{1,0:T(8,128)(2,1)}, bf16[392,512]{1,0:T(8,128)(2,1)S(1)}, u32[]{:S(2)}, u32[]{:S(2)}) collective-permute-start(bf16[392,512]{1,0:T(8,128)(2,1)} %get-tuple-element.99), channel_id=1, source_target_pairs={{0,8},{8,0},{16,24},{24,16},{1,9},{9,1},{17,25},{25,17},{2,10},{10... | collective-permute-start | bytes 1204232 | tf_op jit(solution)/shard_map/ppermute | solution.py:560
  28.6 11.8 %collective-permute-start.8 = (bf16[392,512]{1,0:T(8,128)(2,1)}, bf16[392,512]{1,0:T(8,128)(2,1)S(1)}, u32[]{:S(2)}, u32[]{:S(2)}) collective-permute-start(bf16[392,512]{1,0:T(8,128)(2,1)} %add_convert_fusion.1), channel_id=1, source_target_pairs={{0,16},{8,24},{16,0},{24,8},{1,17},{9,25},{17,1},{25,9},{2,18},{10... | collective-permute-start | bytes 1204232 | tf_op jit(solution)/shard_map/ppermute | solution.py:564
  31.6 13.9 %collective-permute-start.11 = (bf16[2304,128]{1,0:T(8,128)(2,1)S(1)}, bf16[2304,128]{1,0:T(8,128)(2,1)S(1)}, u32[]{:S(2)}, u32[]{:S(2)}) collective-permute-start(bf16[2304,128]{1,0:T(8,128)(2,1)S(1)} %constant_dynamic-update-slice_fusion.near), channel_id=1, source_target_pairs={{0,1},{1,0},{2,3},{3,2},{4,5},{5,4},{6,7},{7,6},{8,9},{9,8},{10,11... | collective-permute-start | bytes 1769480 | tf_op jit(solution)/shard_map/ppermute | solution.py:568
  32.2 9.8 %collective-permute-start.12 = (bf16[64,512]{1,0:T(8,128)(2,1)S(1)}, bf16[64,512]{1,0:T(8,128)(2,1)S(1)}, u32[]{:S(2)}, u32[]{:S(2)}) collective-permute-start(bf16[64,512]{1,0:T(8,128)(2,1)S(1)} %copy-done.6), channel_id=1, source_target_pairs={{0,2},{1,3},{2,0},{3,1},{4,6},{5,7},{6,4},{7,5},{8,10},{9,11},{10,... | collective-permute-start | bytes 196616 | tf_op jit(solution)/shard_map/ppermute | solution.py:568
  40.7 15.1 %collective-permute-start.20 = (bf16[392,512]{1,0:T(8,128)(2,1)S(1)}, bf16[392,512]{1,0:T(8,128)(2,1)S(1)}, u32[]{:S(2)}, u32[]{:S(2)}) collective-permute-start(bf16[392,512]{1,0:T(8,128)(2,1)S(1)} %get-tuple-element.109.pre0.first_pre.p0), channel_id=1, source_target_pairs={{0,16},{8,24},{16,0},{24,8},{1,17},{9,25},{17,1},{25,9},{2,18},{10... | collective-permute-start | bytes 1204232 | tf_op jit(solution)/shard_map/ppermute | solution.py:564
  65.3 13.6 %collective-permute-start.27 = (bf16[4,392,128]{2,1,0:T(8,128)(2,1)S(1)}, bf16[4,392,128]{2,1,0:T(8,128)(2,1)S(1)}, u32[]{:S(2)}, u32[]{:S(2)}) collective-permute-start(bf16[4,392,128]{2,1,0:T(8,128)(2,1)S(1)} %get-tuple-element.115.src0.pre), channel_id=1, source_target_pairs={{0,16},{8,24},{16,0},{24,8},{1,17},{9,25},{17,1},{25,9},{2,18},{10... | collective-permute-start | bytes 1204232 | tf_op jit(solution)/shard_map/ppermute | solution.py:564
  80.6 31.1 %collective-permute-start.30 = (bf16[512,1152]{1,0:T(8,128)(2,1)S(1)}, bf16[512,1152]{1,0:T(8,128)(2,1)S(1)}, u32[]{:S(2)}, u32[]{:S(2)}) collective-permute-start(bf16[512,1152]{1,0:T(8,128)(2,1)S(1)} %gather_middle.1.weight.w0), channel_id=1, source_target_pairs={{0,16},{8,24},{16,0},{24,8},{1,17},{9,25},{17,1},{25,9},{2,18},{10... | collective-permute-start | bytes 3538952 | tf_op jit(solution)/shard_map/ppermute | solution.py:564
  111.2 14.9 %collective-permute-start.34 = (bf16[512,1152]{1,0:T(8,128)(2,1)S(1)}, bf16[512,1152]{1,0:T(8,128)(2,1)S(1)}, u32[]{:S(2)}, u32[]{:S(2)}) collective-permute-start(bf16[512,1152]{1,0:T(8,128)(2,1)S(1)} %gather_middle.1.weight.w0), channel_id=1, source_target_pairs={{0,8},{8,0},{16,24},{24,16},{1,9},{9,1},{17,25},{25,17},{2,10},{10... | collective-permute-start | bytes 3538952 | tf_op jit(solution)/shard_map/ppermute | solution.py:560
  111.7 14.4 %collective-permute-start.35 = (bf16[512,1152]{1,0:T(8,128)(2,1)S(1)}, bf16[512,1152]{1,0:T(8,128)(2,1)S(1)}, u32[]{:S(2)}, u32[]{:S(2)}) collective-permute-start(bf16[512,1152]{1,0:T(8,128)(2,1)S(1)} %collective-permute-done.30.w2), channel_id=1, source_target_pairs={{0,8},{8,0},{16,24},{24,16},{1,9},{9,1},{17,25},{25,17},{2,10},{10... | collective-permute-start | bytes 3538952 | tf_op jit(solution)/shard_map/ppermute | solution.py:560
  111.7 11.7 %collective-permute-start.32 = (bf16[392,512]{1,0:T(8,128)(2,1)S(1)}, bf16[392,512]{1,0:T(8,128)(2,1)S(1)}, u32[]{:S(2)}, u32[]{:S(2)}) collective-permute-start(bf16[392,512]{1,0:T(8,128)(2,1)S(1)} %get-tuple-element.134), channel_id=1, source_target_pairs={{0,8},{8,0},{16,24},{24,16},{1,9},{9,1},{17,25},{25,17},{2,10},{10... | collective-permute-start | bytes 1204232 | tf_op jit(solution)/shard_map/ppermute | solution.py:560
  113.1 11.4 %collective-permute-start.33 = (bf16[392,512]{1,0:T(8,128)(2,1)S(1)}, bf16[392,512]{1,0:T(8,128)(2,1)S(1)}, u32[]{:S(2)}, u32[]{:S(2)}) collective-permute-start(bf16[392,512]{1,0:T(8,128)(2,1)S(1)} %add_convert_fusion), channel_id=1, source_target_pairs={{0,16},{8,24},{16,0},{24,8},{1,17},{9,25},{17,1},{25,9},{2,18},{10... | collective-permute-start | bytes 1204232 | tf_op jit(solution)/shard_map/ppermute | solution.py:564
  125.2 11.2 %collective-permute-start.37 = (bf16[2,392,128]{2,1,0:T(8,128)(2,1)S(1)}, bf16[2,392,128]{2,1,0:T(8,128)(2,1)S(1)}, u32[]{:S(2)}, u32[]{:S(2)}) collective-permute-start(bf16[2,392,128]{2,1,0:T(8,128)(2,1)S(1)} %get-tuple-element.147), channel_id=1, source_target_pairs={{0,16},{8,24},{16,0},{24,8},{1,17},{9,25},{17,1},{25,9},{2,18},{10... | collective-permute-start | bytes 602120 | tf_op jit(solution)/shard_map/ppermute | solution.py:564
  141.0 14.7 %collective-permute-start.47 = (bf16[392,512]{1,0:T(8,128)(2,1)S(1)}, bf16[392,512]{1,0:T(8,128)(2,1)S(1)}, u32[]{:S(2)}, u32[]{:S(2)}) collective-permute-start(bf16[392,512]{1,0:T(8,128)(2,1)S(1)} %get-tuple-element.153.g0), channel_id=1, source_target_pairs={{0,16},{8,24},{16,0},{24,8},{1,17},{9,25},{17,1},{25,9},{2,18},{10... | collective-permute-start | bytes 1204232 | tf_op jit(solution)/shard_map/ppermute | solution.py:564
  147.6 15.5 %collective-permute-start.52 = (bf16[256,1152]{1,0:T(8,128)(2,1)S(1)}, bf16[256,1152]{1,0:T(8,128)(2,1)S(1)}, u32[]{:S(2)}, u32[]{:S(2)}) collective-permute-start(bf16[256,1152]{1,0:T(8,128)(2,1)S(1)} %get-tuple-element.159), channel_id=1, source_target_pairs={{0,1},{1,0},{2,3},{3,2},{4,5},{5,4},{6,7},{7,6},{8,9},{9,8},{10,11... | collective-permute-start | bytes 1769480 | tf_op jit(solution)/shard_map/ppermute | solution.py:568
  163.0 12.3 %collective-permute-start.53 = (bf16[256,512]{1,0:T(8,128)(2,1)S(1)}, bf16[256,512]{1,0:T(8,128)(2,1)S(1)}, u32[]{:S(2)}, u32[]{:S(2)}) collective-permute-start(bf16[256,512]{1,0:T(8,128)(2,1)S(1)} %get-tuple-element.160), channel_id=1, source_target_pairs={{0,1},{1,0},{2,3},{3,2},{4,5},{5,4},{6,7},{7,6},{8,9},{9,8},{10,11... | collective-permute-start | bytes 786440 | tf_op jit(solution)/shard_map/ppermute | solution.py:568
  164.5 10.9 %collective-permute-start.54 = (bf16[64,1664]{1,0:T(8,128)(2,1)S(1)}, bf16[64,1664]{1,0:T(8,128)(2,1)S(1)}, u32[]{:S(2)}, u32[]{:S(2)}) collective-permute-start(bf16[64,1664]{1,0:T(8,128)(2,1)S(1)} %get-tuple-element.163), channel_id=1, source_target_pairs={{0,2},{1,3},{2,0},{3,1},{4,6},{5,7},{6,4},{7,5},{8,10},{9,11},{10,... | collective-permute-start | bytes 638984 | tf_op jit(solution)/shard_map/ppermute | solution.py:568
  164.9 13.1 %collective-permute-start.57 = (bf16[64,1664]{1,0:T(8,128)(2,1)S(1)}, bf16[64,1664]{1,0:T(8,128)(2,1)S(1)}, u32[]{:S(2)}, u32[]{:S(2)}) collective-permute-start(bf16[64,1664]{1,0:T(8,128)(2,1)S(1)} %get-tuple-element.168), channel_id=1, source_target_pairs={{0,4},{1,5},{2,6},{3,7},{4,0},{5,1},{6,2},{7,3},{8,12},{9,13},{10,... | collective-permute-start | bytes 638984 | tf_op jit(solution)/shard_map/ppermute | solution.py:568
  176.7 12.5 %collective-permute-start.62 = (bf16[64,1664]{1,0:T(8,128)(2,1)S(1)}, bf16[64,1664]{1,0:T(8,128)(2,1)S(1)}, u32[]{:S(2)}, u32[]{:S(2)}) collective-permute-start(bf16[64,1664]{1,0:T(8,128)(2,1)S(1)} %get-tuple-element.176), channel_id=1, source_target_pairs={{0,6},{1,7},{2,4},{3,5},{4,2},{5,3},{6,0},{7,1},{8,14},{9,15},{10,... | collective-permute-start | bytes 638984 | tf_op jit(solution)/shard_map/ppermute | solution.py:568
  (51 other events, 298.5 us)

commit v8 on v7

--- a/solution.py
+++ b/solution.py
@@ -575,7 +575,7 @@
 def from_all(values, *others):
     far = swap_chip(values)
     if others:
-        return values, swap_core(after(values, *others)), far, swap_core(after(far, *others))
+        return values, swap_core(values), far, swap_core(after(far, *others))
     return values, swap_core(values), far, swap_core(far)
 
 

time: 192 us -> 192 us (level)
  transfers between devices with their start and end apart: 63 -> 63, of which waited for: 27 -> 28; matrix products, arithmetic and copies ran while one was open for 3% -> 3% of each run, Pallas kernels for 16% -> 16%
where the time goes in v8:
time: 192 us; the launch traced here: 191 us
  starting transfers between devices  64.1 us (33%)
  waiting for transfers between devices  47 us (24%)
  blocking collectives  40.5 us (21%)
  Pallas kernels  32.2 us (17%)
  other arithmetic  3.52 us (2%)
  local copies, waits for them, and re-layouts  3.01 us (2%)
    ppermute x26, starting transfers between devices, swap_wide(): return lax.ppermute(values, 'wide', [(i, i ^ step) for i in range(wide)])  35.9 us
    pallas_call x25, Pallas kernels, run(): pl.pallas_call(kernel, out_shape=outs, name=kernel.__name__, in_specs=[pl...  32.2 us
    ppermute x26, waiting for transfers between devices, swap_wide(): return lax.ppermute(values, 'wide', [(i, i ^ step) for i in range(wide)])  28.3 us
    ppermute x11, starting transfers between devices, swap_chip(): return lax.ppermute(values, 'narrow', [(i, i ^ 2) for i in range(NARROW)])  13.2 us
    all_to_all x1, blocking collectives, exchange(): return lax.all_to_all(message, ('wide', 'narrow'), 0, 0, tiled=True)  11.3 us
    ppermute x4, starting transfers between devices, on_device(): first_pieces = [lax.ppermute(w_first, MESH, pairs) for pairs in steps]  11 us
    all_to_all x1, blocking collectives, on_device(): parts_three = lax.all_to_all(message, 'wide', 0, 0, tiled=True)  10.4 us
    all_to_all x1, blocking collectives, on_device(): parts_four = lax.all_to_all(message, 'wide', 0, 0, tiled=True)  9.79 us
  transfers between devices with their start and end apart: 63, of which 28 were waited for; matrix products, arithmetic and copies ran while one was open for 3% of the time, Pallas kernels for 16%

profile of v8, /device:TPU:0, one launch (start us, length us, event | category | flops | bytes accessed | tf_op | source)
XLA Modules:
  0.0 191.3 jit_solution(9885616435382696234)
XLA Ops:
  2.1 3.5 %collective-permute-start.1 = (bf16[256,128]{1,0:T(8,128)(2,1)}, bf16[256,128]{1,0:T(8,128)(2,1)S(1)}, u32[]{:S(2)}, u32[]{:S(2)}) collective-permute-start(bf16[256,128]{1,0:T(8,128)(2,1)} %param.14), channel_id=1, source_target_pairs={{0,2},{1,3},{2,10},{3,11},{4,18},{5,19},{6,26},{7,27},{8,4},{9,5},... | collective-permute-start | bytes 196616 | tf_op jit(solution)/shard_map/ppermute | solution.py:647
  5.7 3.4 %collective-permute-start.2 = (bf16[256,128]{1,0:T(8,128)(2,1)}, bf16[256,128]{1,0:T(8,128)(2,1)S(1)}, u32[]{:S(2)}, u32[]{:S(2)}) collective-permute-start(bf16[256,128]{1,0:T(8,128)(2,1)} %param.14), channel_id=1, source_target_pairs={{0,4},{1,5},{2,12},{3,13},{4,20},{5,21},{6,28},{7,29},{8,6},{9,7},... | collective-permute-start | bytes 196616 | tf_op jit(solution)/shard_map/ppermute | solution.py:647
  9.0 2.6 %collective-permute-start.3 = (bf16[256,128]{1,0:T(8,128)(2,1)}, bf16[256,128]{1,0:T(8,128)(2,1)S(1)}, u32[]{:S(2)}, u32[]{:S(2)}) collective-permute-start(bf16[256,128]{1,0:T(8,128)(2,1)} %param.14), channel_id=1, source_target_pairs={{0,6},{1,7},{2,14},{3,15},{4,22},{5,23},{6,30},{7,31},{8,0},{9,1},... | collective-permute-start | bytes 196616 | tf_op jit(solution)/shard_map/ppermute | solution.py:647
  17.2 3.1 %collective-permute-start.11 = (bf16[576,128]{1,0:T(8,128)(2,1)}, bf16[576,128]{1,0:T(8,128)(2,1)S(1)}, u32[]{:S(2)}, u32[]{:S(2)}) collective-permute-start(bf16[576,128]{1,0:T(8,128)(2,1)} %bitcast.17), channel_id=1, source_target_pairs={{0,4},{1,5},{2,6},{3,7},{4,0},{5,1},{6,2},{7,3},{8,12},{9,13},{10,... | collective-permute-start | bytes 442376 | tf_op jit(solution)/shard_map/ppermute | solution.py:568
  32.2 2.5 %collective-permute-start.14 = (bf16[64,512]{1,0:T(8,128)(2,1)S(1)}, bf16[64,512]{1,0:T(8,128)(2,1)S(1)}, u32[]{:S(2)}, u32[]{:S(2)}) collective-permute-start(bf16[64,512]{1,0:T(8,128)(2,1)S(1)} %copy-done.6), channel_id=1, source_target_pairs={{0,2},{1,3},{2,0},{3,1},{4,6},{5,7},{6,4},{7,5},{8,10},{9,11},{10,... | collective-permute-start | bytes 196616 | tf_op jit(solution)/shard_map/ppermute | solution.py:568
  45.8 2.7 %collective-permute-start.18 = (f32[16,128]{1,0:T(8,128)S(1)}, f32[16,128]{1,0:T(8,128)S(1)}, u32[]{:S(2)}, u32[]{:S(2)}) collective-permute-start(f32[16,128]{1,0:T(8,128)S(1)} %add_tiles.4.refs_0_), channel_id=1, source_target_pairs={{0,2},{1,3},{2,0},{3,1},{4,6},{5,7},{6,4},{7,5},{8,10},{9,11},{10,... | collective-permute-start | bytes 24584 | tf_op jit(solution)/shard_map/ppermute | solution.py:568
  59.7 5.6 %middle_forward.1 = (bf16[4,448,512]{2,1,0:T(8,128)(2,1)S(1)}, bf16[4,392,128]{2,1,0:T(8,128)(2,1)S(1)}, f32[4,8,512]{2,1,0:T(8,128)S(1)}, f32[32,8,128]{2,1,0:T(8,128)S(1)}, f32[4,8,128]{2,1,0:T(8,128)S(1)}) custom-call(bf16[392,512]{1,0:T(8,128)(2,1)S(1)} %get-tuple-element.101.pre0.first_pre.p0, bf16[392,512]{1,0:T(8,128)(2,1)S(1)} %collective-permute-done.9.pre1.p1, ...), custom_call_target="tpu_custom_call" | custom-call | flops 2113929216 | bytes 5976192 | tf_op jit(solution)/shard_map/middle_forward/pallas_call | solution.py:39
  67.6 11.3 %all_to_all.20.parts.norm = f32[32,8,128]{2,1,0:T(8,128)S(1)} all-to-all(f32[32,8,128]{2,1,0:T(8,128)S(1)} %get-tuple-element.110), channel_id=1, replica_groups=mesh['narrow'=4,'wide'=8] {'wide','narrow'}, dimensions={0} | all-to-all | bytes 262144 | tf_op jit(solution)/shard_map/all_to_all | solution.py:556
  83.4 2.2 %last_forward.1 = (bf16[4,392,512]{2,1,0:T(8,128)(2,1)S(1)}, bf16[392,512]{1,0:T(8,128)(2,1)S(1)}, f32[8,512]{1,0:T(8,128)S(1)}, f32[4,392,512]{2,1,0:T(8,128)S(1)}, f32[8,8,512]{2,1,0:T(8,128)S(1)}) custom-call(bf16[4,392,128]{2,1,0:T(8,128)(2,1)S(1)} %get-tuple-element.107.src0.pre, bf16[4,392,128]{2,1,0:T(8,128)(2,1)S(1)} %collective-permute-done.25.src1, ...), custom_call_target="tpu_custom_call" | custom-call | flops 822083584 | bytes 7649408 | tf_op jit(solution)/shard_map/last_forward/pallas_call | solution.py:39
  85.6 10.4 %all_to_all.21.parts = f32[8,8,512]{2,1,0:T(8,128)S(1)} all-to-all(f32[8,8,512]{2,1,0:T(8,128)S(1)} %get-tuple-element.114), channel_id=1, replica_groups=mesh['narrow'=4,'wide'=8] {'wide'}, dimensions={0} | all-to-all | bytes 262144 | tf_op jit(solution)/shard_map/all_to_all | solution.py:711
  96.0 3.4 %block_output.1 = (bf16[4,392,512]{2,1,0:T(8,128)(2,1)}, f32[4,392,512]{2,1,0:T(8,128)S(1)}, f32[4,8,512]{2,1,0:T(8,128)S(1)}, f32[8,8,512]{2,1,0:T(8,128)S(1)}) custom-call(f32[4,392,512]{2,1,0:T(8,128)S(1)} %get-tuple-element.113.pre, bf16[4,392,512]{2,1,0:T(8,128)(2,1)S(1)} %copy-done.1, bf16[4,392,512]{2,1,0:T(8,128)(2,1)S(1)} %copy-done.2, ...), custom_call_target="tpu_custom_call" | custom-call | bytes 11593856 | tf_op jit(solution)/shard_map/block_output/pallas_call | solution.py:39
  99.4 9.8 %all_to_all.22.parts = f32[8,8,512]{2,1,0:T(8,128)S(1)} all-to-all(f32[8,8,512]{2,1,0:T(8,128)S(1)} %get-tuple-element.117), channel_id=1, replica_groups=mesh['narrow'=4,'wide'=8] {'wide'}, dimensions={0} | all-to-all | bytes 262144 | tf_op jit(solution)/shard_map/all_to_all | solution.py:717
  115.6 7.9 %collective-permute-done.31.away_last = bf16[256,512]{1,0:T(8,128)(2,1)S(1)} collective-permute-done((bf16[256,512]{1,0:T(8,128)(2,1)S(1)}, bf16[256,512]{1,0:T(8,128)(2,1)S(1)}, u32[]{:S(2)}, u32[]{:S(2)}) %collective-permute-start.31) | collective-permute-done | bytes 262176 | tf_op jit(solution)/shard_map/ppermute | solution.py:568
  126.1 9.1 %all_to_all.23.parts = f32[8,8,128]{2,1,0:T(8,128)S(1)} all-to-all(f32[8,8,128]{2,1,0:T(8,128)S(1)} %get-tuple-element.134), channel_id=1, replica_groups=mesh['narrow'=4,'wide'=8] {'wide'}, dimensions={0} | all-to-all | bytes 65536 | tf_op jit(solution)/shard_map/all_to_all | solution.py:746
  136.8 4.1 %middle_backward.1 = (bf16[392,512]{1,0:T(8,128)(2,1)S(1)}, f32[8,128]{1,0:T(8,128)S(1)}) custom-call(f32[392,512]{1,0:T(8,128)S(1)} %get-tuple-element.132.grad, bf16[392,512]{1,0:T(8,128)(2,1)S(1)} %get-tuple-element.130.pre, f32[8,8,128]{2,1,0:T(8,128)S(1)} %all_to_all.23.parts, f32[4,8,128]{2,1,0:T(8,128)S(1)} %get-tuple-element.112.params, ...), custom_call_target="tpu_custom_call" | custom-call | flops 2113929216 | bytes 7569536 | tf_op jit(solution)/shard_map/middle_backward/pallas_call | solution.py:39
  143.6 4.0 %middle_weight.1 = (f32[1,128]{1,0:T(1,128)}, f32[1,128]{1,0:T(1,128)}, f32[256,1152]{1,0:T(8,128)S(1)}, bf16[256,1152]{1,0:T(8,128)(2,1)S(1)}) custom-call(bf16[4,448,512]{2,1,0:T(8,128)(2,1)S(1)} %get-tuple-element.139.hidden, bf16[392,128]{1,0:T(8,128)(2,1)S(1)} %get-tuple-element.140.q0, bf16[392,128]{1,0:T(8,128)(2,1)S(1)} %collective-permute-done.40.q1, ...), custom_call_target="tpu_custom_call" | custom-call | flops 2113929216 | bytes 5130368 | tf_op jit(solution)/shard_map/middle_weight/pallas_call | solution.py:39
  150.3 3.3 %collective-permute-start.47 = (f32[8,128]{1,0:T(8,128)S(1)}, f32[8,128]{1,0:T(8,128)S(1)}, u32[]{:S(2)}, u32[]{:S(2)}) collective-permute-start(f32[8,128]{1,0:T(8,128)S(1)} %add_tiles.6.refs_0_), channel_id=1, source_target_pairs={{0,6},{1,7},{2,4},{3,5},{4,2},{5,3},{6,0},{7,1},{8,14},{9,15},{10,... | collective-permute-start | bytes 12296 | tf_op jit(solution)/shard_map/ppermute | solution.py:568
  157.2 2.3 %collective-permute-done.50.sum2 = f32[8,128]{1,0:T(8,128)S(1)} collective-permute-done((f32[8,128]{1,0:T(8,128)S(1)}, f32[8,128]{1,0:T(8,128)S(1)}, u32[]{:S(2)}, u32[]{:S(2)}) %collective-permute-start.50) | collective-permute-done | bytes 4128 | tf_op jit(solution)/shard_map/ppermute | solution.py:564
  160.6 2.1 %first_weight.1 = (f32[1,128]{1,0:T(1,128)}, f32[1,128]{1,0:T(1,128)}, bf16[4,392,512]{2,1,0:T(8,128)(2,1)S(1)}, f32[256,512]{1,0:T(8,128)S(1)}, bf16[256,512]{1,0:T(8,128)(2,1)S(1)}) custom-call(bf16[392,512]{1,0:T(8,128)(2,1)S(1)} %get-tuple-element.137.g0, bf16[392,512]{1,0:T(8,128)(2,1)S(1)} %collective-permute-done.37.g1, ...), custom_call_target="tpu_custom_call" | custom-call | flops 822083584 | bytes 7314560 | tf_op jit(solution)/shard_map/first_weight/pallas_call | solution.py:39
  164.9 2.3 %collective-permute-start.57 = (bf16[64,1664]{1,0:T(8,128)(2,1)S(1)}, bf16[64,1664]{1,0:T(8,128)(2,1)S(1)}, u32[]{:S(2)}, u32[]{:S(2)}) collective-permute-start(bf16[64,1664]{1,0:T(8,128)(2,1)S(1)} %get-tuple-element.162), channel_id=1, source_target_pairs={{0,4},{1,5},{2,6},{3,7},{4,0},{5,1},{6,2},{7,3},{8,12},{9,13},{10,... | collective-permute-start | bytes 638984 | tf_op jit(solution)/shard_map/ppermute | solution.py:568
  167.2 7.8 %collective-permute-done.54.p1 = bf16[64,1664]{1,0:T(8,128)(2,1)S(1)} collective-permute-done((bf16[64,1664]{1,0:T(8,128)(2,1)S(1)}, bf16[64,1664]{1,0:T(8,128)(2,1)S(1)}, u32[]{:S(2)}, u32[]{:S(2)}) %collective-permute-start.54) | collective-permute-done | bytes 213024 | tf_op jit(solution)/shard_map/ppermute | solution.py:568
  177.6 2.5 %collective-permute-done.56.far = bf16[2,256,128]{2,1,0:T(8,128)(2,1)S(1)} collective-permute-done((bf16[2,256,128]{2,1,0:T(8,128)(2,1)S(1)}, bf16[2,256,128]{2,1,0:T(8,128)(2,1)S(1)}, u32[]{:S(2)}, u32[]{:S(2)}) %collective-permute-start.56) | collective-permute-done | bytes 131104 | tf_op jit(solution)/shard_map/ppermute | solution.py:564
  183.5 2.5 %collective-permute-start.61 = (bf16[256,128]{1,0:T(8,128)(2,1)S(1)}, bf16[256,128]{1,0:T(8,128)(2,1)S(1)}, u32[]{:S(2)}, u32[]{:S(2)}) collective-permute-start(bf16[256,128]{1,0:T(8,128)(2,1)S(1)} %get-tuple-element.167), channel_id=1, source_target_pairs={{0,6},{1,7},{2,4},{3,5},{4,2},{5,3},{6,0},{7,1},{8,14},{9,15},{10,... | collective-permute-start | bytes 196616 | tf_op jit(solution)/shard_map/ppermute | solution.py:568
  186.1 2.7 %input_gradient.1 = f32[4,392,512]{2,1,0:T(8,128)} custom-call(bf16[4,392,512]{2,1,0:T(8,128)(2,1)S(1)} %get-tuple-element.149.grad_pre, bf16[512,512]{1,0:T(8,128)(2,1)S(1)} %get-tuple-element.150.weight, f32[4,392,512]{2,1,0:T(8,128)S(1)} %get-tuple-element.116.grad), custom_call_target="tpu_custom_call" | custom-call | flops 822083584 | bytes 8552448 | tf_op jit(solution)/shard_map/input_gradient/pallas_call | solution.py:39
  (176 shorter events, 79.4 us)
Async XLA Ops:
  0.6 11.0 %collective-permute-start = (bf16[256,128]{1,0:T(8,128)(2,1)}, bf16[256,128]{1,0:T(8,128)(2,1)S(1)}, u32[]{:S(2)}, u32[]{:S(2)}) collective-permute-start(bf16[256,128]{1,0:T(8,128)(2,1)} %param.14), channel_id=1, source_target_pairs={{0,0},{1,1},{2,8},{3,9},{4,16},{5,17},{6,24},{7,25},{8,2},{9,3},{1... | collective-permute-start | bytes 196616 | tf_op jit(solution)/shard_map/ppermute | solution.py:647
  2.1 9.5 %collective-permute-start.1 = (bf16[256,128]{1,0:T(8,128)(2,1)}, bf16[256,128]{1,0:T(8,128)(2,1)S(1)}, u32[]{:S(2)}, u32[]{:S(2)}) collective-permute-start(bf16[256,128]{1,0:T(8,128)(2,1)} %param.14), channel_id=1, source_target_pairs={{0,2},{1,3},{2,10},{3,11},{4,18},{5,19},{6,26},{7,27},{8,4},{9,5},... | collective-permute-start | bytes 196616 | tf_op jit(solution)/shard_map/ppermute | solution.py:647
  14.0 8.9 %collective-permute-start.4 = (bf16[256,512]{1,0:T(8,128)(2,1)S(1)}, bf16[256,512]{1,0:T(8,128)(2,1)S(1)}, u32[]{:S(2)}, u32[]{:S(2)}) collective-permute-start(bf16[256,512]{1,0:T(8,128)(2,1)S(1)} %place_columns.1.refs_0_), channel_id=1, source_target_pairs={{0,1},{1,0},{2,3},{3,2},{4,5},{5,4},{6,7},{7,6},{8,9},{9,8},{10,11... | collective-permute-start | bytes 786440 | tf_op jit(solution)/shard_map/ppermute | solution.py:568
  15.6 13.1 %collective-permute-start.7 = (bf16[576,128]{1,0:T(8,128)(2,1)}, bf16[576,128]{1,0:T(8,128)(2,1)S(1)}, u32[]{:S(2)}, u32[]{:S(2)}) collective-permute-start(bf16[576,128]{1,0:T(8,128)(2,1)} %bitcast.16), channel_id=1, source_target_pairs={{0,2},{1,3},{2,0},{3,1},{4,6},{5,7},{6,4},{7,5},{8,10},{9,11},{10,... | collective-permute-start | bytes 442376 | tf_op jit(solution)/shard_map/ppermute | solution.py:568
  17.2 14.4 %collective-permute-start.11 = (bf16[576,128]{1,0:T(8,128)(2,1)}, bf16[576,128]{1,0:T(8,128)(2,1)S(1)}, u32[]{:S(2)}, u32[]{:S(2)}) collective-permute-start(bf16[576,128]{1,0:T(8,128)(2,1)} %bitcast.17), channel_id=1, source_target_pairs={{0,4},{1,5},{2,6},{3,7},{4,0},{5,1},{6,2},{7,3},{8,12},{9,13},{10,... | collective-permute-start | bytes 442376 | tf_op jit(solution)/shard_map/ppermute | solution.py:568
  20.3 11.3 %collective-permute-start.12 = (bf16[576,128]{1,0:T(8,128)(2,1)}, bf16[576,128]{1,0:T(8,128)(2,1)S(1)}, u32[]{:S(2)}, u32[]{:S(2)}) collective-permute-start(bf16[576,128]{1,0:T(8,128)(2,1)} %bitcast.18), channel_id=1, source_target_pairs={{0,6},{1,7},{2,4},{3,5},{4,2},{5,3},{6,0},{7,1},{8,14},{9,15},{10,... | collective-permute-start | bytes 442376 | tf_op jit(solution)/shard_map/ppermute | solution.py:568
  26.5 11.8 %collective-permute-start.5 = (bf16[392,512]{1,0:T(8,128)(2,1)}, bf16[392,512]{1,0:T(8,128)(2,1)S(1)}, u32[]{:S(2)}, u32[]{:S(2)}) collective-permute-start(bf16[392,512]{1,0:T(8,128)(2,1)} %get-tuple-element.96), channel_id=1, source_target_pairs={{0,8},{8,0},{16,24},{24,16},{1,9},{9,1},{17,25},{25,17},{2,10},{10... | collective-permute-start | bytes 1204232 | tf_op jit(solution)/shard_map/ppermute | solution.py:560
  28.6 11.8 %collective-permute-start.8 = (bf16[392,512]{1,0:T(8,128)(2,1)}, bf16[392,512]{1,0:T(8,128)(2,1)S(1)}, u32[]{:S(2)}, u32[]{:S(2)}) collective-permute-start(bf16[392,512]{1,0:T(8,128)(2,1)} %add_convert_fusion.1), channel_id=1, source_target_pairs={{0,16},{8,24},{16,0},{24,8},{1,17},{9,25},{17,1},{25,9},{2,18},{10... | collective-permute-start | bytes 1204232 | tf_op jit(solution)/shard_map/ppermute | solution.py:564
  31.6 13.9 %collective-permute-start.13 = (bf16[2304,128]{1,0:T(8,128)(2,1)S(1)}, bf16[2304,128]{1,0:T(8,128)(2,1)S(1)}, u32[]{:S(2)}, u32[]{:S(2)}) collective-permute-start(bf16[2304,128]{1,0:T(8,128)(2,1)S(1)} %constant_dynamic-update-slice_fusion.near), channel_id=1, source_target_pairs={{0,1},{1,0},{2,3},{3,2},{4,5},{5,4},{6,7},{7,6},{8,9},{9,8},{10,11... | collective-permute-start | bytes 1769480 | tf_op jit(solution)/shard_map/ppermute | solution.py:568
  32.2 9.8 %collective-permute-start.14 = (bf16[64,512]{1,0:T(8,128)(2,1)S(1)}, bf16[64,512]{1,0:T(8,128)(2,1)S(1)}, u32[]{:S(2)}, u32[]{:S(2)}) collective-permute-start(bf16[64,512]{1,0:T(8,128)(2,1)S(1)} %copy-done.6), channel_id=1, source_target_pairs={{0,2},{1,3},{2,0},{3,1},{4,6},{5,7},{6,4},{7,5},{8,10},{9,11},{10,... | collective-permute-start | bytes 196616 | tf_op jit(solution)/shard_map/ppermute | solution.py:568
  40.7 15.1 %collective-permute-start.10 = (bf16[392,512]{1,0:T(8,128)(2,1)S(1)}, bf16[392,512]{1,0:T(8,128)(2,1)S(1)}, u32[]{:S(2)}, u32[]{:S(2)}) collective-permute-start(bf16[392,512]{1,0:T(8,128)(2,1)S(1)} %get-tuple-element.101.pre0.first_pre.p0), channel_id=1, source_target_pairs={{0,16},{8,24},{16,0},{24,8},{1,17},{9,25},{17,1},{25,9},{2,18},{10... | collective-permute-start | bytes 1204232 | tf_op jit(solution)/shard_map/ppermute | solution.py:564
  65.3 13.6 %collective-permute-start.26 = (bf16[4,392,128]{2,1,0:T(8,128)(2,1)S(1)}, bf16[4,392,128]{2,1,0:T(8,128)(2,1)S(1)}, u32[]{:S(2)}, u32[]{:S(2)}) collective-permute-start(bf16[4,392,128]{2,1,0:T(8,128)(2,1)S(1)} %get-tuple-element.107.src0.pre), channel_id=1, source_target_pairs={{0,16},{8,24},{16,0},{24,8},{1,17},{9,25},{17,1},{25,9},{2,18},{10... | collective-permute-start | bytes 1204232 | tf_op jit(solution)/shard_map/ppermute | solution.py:564
  80.6 31.1 %collective-permute-start.30 = (bf16[512,1152]{1,0:T(8,128)(2,1)S(1)}, bf16[512,1152]{1,0:T(8,128)(2,1)S(1)}, u32[]{:S(2)}, u32[]{:S(2)}) collective-permute-start(bf16[512,1152]{1,0:T(8,128)(2,1)S(1)} %gather_middle.1.weight.w0), channel_id=1, source_target_pairs={{0,16},{8,24},{16,0},{24,8},{1,17},{9,25},{17,1},{25,9},{2,18},{10... | collective-permute-start | bytes 3538952 | tf_op jit(solution)/shard_map/ppermute | solution.py:564
  111.2 14.9 %collective-permute-start.34 = (bf16[512,1152]{1,0:T(8,128)(2,1)S(1)}, bf16[512,1152]{1,0:T(8,128)(2,1)S(1)}, u32[]{:S(2)}, u32[]{:S(2)}) collective-permute-start(bf16[512,1152]{1,0:T(8,128)(2,1)S(1)} %gather_middle.1.weight.w0), channel_id=1, source_target_pairs={{0,8},{8,0},{16,24},{24,16},{1,9},{9,1},{17,25},{25,17},{2,10},{10... | collective-permute-start | bytes 3538952 | tf_op jit(solution)/shard_map/ppermute | solution.py:560
  111.7 14.4 %collective-permute-start.35 = (bf16[512,1152]{1,0:T(8,128)(2,1)S(1)}, bf16[512,1152]{1,0:T(8,128)(2,1)S(1)}, u32[]{:S(2)}, u32[]{:S(2)}) collective-permute-start(bf16[512,1152]{1,0:T(8,128)(2,1)S(1)} %collective-permute-done.30.w2), channel_id=1, source_target_pairs={{0,8},{8,0},{16,24},{24,16},{1,9},{9,1},{17,25},{25,17},{2,10},{10... | collective-permute-start | bytes 3538952 | tf_op jit(solution)/shard_map/ppermute | solution.py:560
  111.7 11.7 %collective-permute-start.32 = (bf16[392,512]{1,0:T(8,128)(2,1)S(1)}, bf16[392,512]{1,0:T(8,128)(2,1)S(1)}, u32[]{:S(2)}, u32[]{:S(2)}) collective-permute-start(bf16[392,512]{1,0:T(8,128)(2,1)S(1)} %get-tuple-element.129), channel_id=1, source_target_pairs={{0,8},{8,0},{16,24},{24,16},{1,9},{9,1},{17,25},{25,17},{2,10},{10... | collective-permute-start | bytes 1204232 | tf_op jit(solution)/shard_map/ppermute | solution.py:560
  113.1 11.4 %collective-permute-start.33 = (bf16[392,512]{1,0:T(8,128)(2,1)S(1)}, bf16[392,512]{1,0:T(8,128)(2,1)S(1)}, u32[]{:S(2)}, u32[]{:S(2)}) collective-permute-start(bf16[392,512]{1,0:T(8,128)(2,1)S(1)} %add_convert_fusion), channel_id=1, source_target_pairs={{0,16},{8,24},{16,0},{24,8},{1,17},{9,25},{17,1},{25,9},{2,18},{10... | collective-permute-start | bytes 1204232 | tf_op jit(solution)/shard_map/ppermute | solution.py:564
  125.2 11.2 %collective-permute-start.39 = (bf16[2,392,128]{2,1,0:T(8,128)(2,1)S(1)}, bf16[2,392,128]{2,1,0:T(8,128)(2,1)S(1)}, u32[]{:S(2)}, u32[]{:S(2)}) collective-permute-start(bf16[2,392,128]{2,1,0:T(8,128)(2,1)S(1)} %get-tuple-element.142), channel_id=1, source_target_pairs={{0,16},{8,24},{16,0},{24,8},{1,17},{9,25},{17,1},{25,9},{2,18},{10... | collective-permute-start | bytes 602120 | tf_op jit(solution)/shard_map/ppermute | solution.py:564
  141.0 14.7 %collective-permute-start.38 = (bf16[392,512]{1,0:T(8,128)(2,1)S(1)}, bf16[392,512]{1,0:T(8,128)(2,1)S(1)}, u32[]{:S(2)}, u32[]{:S(2)}) collective-permute-start(bf16[392,512]{1,0:T(8,128)(2,1)S(1)} %get-tuple-element.137.g0), channel_id=1, source_target_pairs={{0,16},{8,24},{16,0},{24,8},{1,17},{9,25},{17,1},{25,9},{2,18},{10... | collective-permute-start | bytes 1204232 | tf_op jit(solution)/shard_map/ppermute | solution.py:564
  147.6 15.3 %collective-permute-start.52 = (bf16[256,1152]{1,0:T(8,128)(2,1)S(1)}, bf16[256,1152]{1,0:T(8,128)(2,1)S(1)}, u32[]{:S(2)}, u32[]{:S(2)}) collective-permute-start(bf16[256,1152]{1,0:T(8,128)(2,1)S(1)} %get-tuple-element.153), channel_id=1, source_target_pairs={{0,1},{1,0},{2,3},{3,2},{4,5},{5,4},{6,7},{7,6},{8,9},{9,8},{10,11... | collective-permute-start | bytes 1769480 | tf_op jit(solution)/shard_map/ppermute | solution.py:568
  162.8 12.2 %collective-permute-start.53 = (bf16[256,512]{1,0:T(8,128)(2,1)S(1)}, bf16[256,512]{1,0:T(8,128)(2,1)S(1)}, u32[]{:S(2)}, u32[]{:S(2)}) collective-permute-start(bf16[256,512]{1,0:T(8,128)(2,1)S(1)} %get-tuple-element.154), channel_id=1, source_target_pairs={{0,1},{1,0},{2,3},{3,2},{4,5},{5,4},{6,7},{7,6},{8,9},{9,8},{10,11... | collective-permute-start | bytes 786440 | tf_op jit(solution)/shard_map/ppermute | solution.py:568
  164.5 10.5 %collective-permute-start.54 = (bf16[64,1664]{1,0:T(8,128)(2,1)S(1)}, bf16[64,1664]{1,0:T(8,128)(2,1)S(1)}, u32[]{:S(2)}, u32[]{:S(2)}) collective-permute-start(bf16[64,1664]{1,0:T(8,128)(2,1)S(1)} %get-tuple-element.157), channel_id=1, source_target_pairs={{0,2},{1,3},{2,0},{3,1},{4,6},{5,7},{6,4},{7,5},{8,10},{9,11},{10,... | collective-permute-start | bytes 638984 | tf_op jit(solution)/shard_map/ppermute | solution.py:568
  164.9 12.7 %collective-permute-start.57 = (bf16[64,1664]{1,0:T(8,128)(2,1)S(1)}, bf16[64,1664]{1,0:T(8,128)(2,1)S(1)}, u32[]{:S(2)}, u32[]{:S(2)}) collective-permute-start(bf16[64,1664]{1,0:T(8,128)(2,1)S(1)} %get-tuple-element.162), channel_id=1, source_target_pairs={{0,4},{1,5},{2,6},{3,7},{4,0},{5,1},{6,2},{7,3},{8,12},{9,13},{10,... | collective-permute-start | bytes 638984 | tf_op jit(solution)/shard_map/ppermute | solution.py:568
  176.3 12.5 %collective-permute-start.62 = (bf16[64,1664]{1,0:T(8,128)(2,1)S(1)}, bf16[64,1664]{1,0:T(8,128)(2,1)S(1)}, u32[]{:S(2)}, u32[]{:S(2)}) collective-permute-start(bf16[64,1664]{1,0:T(8,128)(2,1)S(1)} %get-tuple-element.170), channel_id=1, source_target_pairs={{0,6},{1,7},{2,4},{3,5},{4,2},{5,3},{6,0},{7,1},{8,14},{9,15},{10,... | collective-permute-start | bytes 638984 | tf_op jit(solution)/shard_map/ppermute | solution.py:568
  (51 other events, 305.5 us)
